TPU v7x, 32 devices: a whole 2x2x4 slice. The times are simulated.
32 devices in a mesh: dp: 16 (over z, y, x), head: 2 (over core).
Axes of the slice: x: 2, y: 2, z: 4, core: 2. Of those that a mesh axis runs over, the one named last changes fastest.
Arguments:
- tokens: bfloat16 [256, 32, 32, 128], P('dp'), may hold values from -6 to 6
- cotangent: bfloat16 [256, 32, 32, 128], P('dp'), may hold values from -6 to 6
- resolution: int32 [256], P('dp'), may hold values from 8 to 16, as said below
- live_images: int32 [256], P('dp'), may hold values from 1 to 16, as said below
- entry_weight: float32 [3, 128, 128], P(None, 'dp', 'head'), may hold values from -0.5 to 0.5
- entry_momentum: float32 [3, 128, 128], P(None, 'dp', 'head'), may hold values from -320 to 320
- entry_average: float32 [3, 128, 128], P(None, 'dp', 'head'), may hold values from -1.25 to 1.25
- mixing_weight: float32 [128, 128], P('head', 'dp'), may hold values from -1 to 1
- mixing_momentum: float32 [128, 128], P('head', 'dp'), may hold values from -1536 to 1536
- mixing_average: float32 [128, 128], P('head', 'dp'), may hold values from -2.5 to 2.5
- expand_weight: float32 [128, 1024], P('dp', 'head'), may hold values from -0.5 to 0.5
- expand_momentum: float32 [128, 1024], P('dp', 'head'), may hold values from -768 to 768
- expand_average: float32 [128, 1024], P('dp', 'head'), may hold values from -1.25 to 1.25
- shrink_weight: float32 [1024, 128], P('head', 'dp'), may hold values from -0.25 to 0.25
- shrink_momentum: float32 [1024, 128], P('head', 'dp'), may hold values from -1536 to 1536
- shrink_average: float32 [1024, 128], P('head', 'dp'), may hold values from -0.625 to 0.625
- reduce_weight: float32 [2560, 128], P('dp', 'head'), may hold values from -0.1875 to 0.1875
- reduce_momentum: float32 [2560, 128], P('dp', 'head'), may hold values from -160 to 160
- reduce_average: float32 [2560, 128], P('dp', 'head'), may hold values from -0.5 to 0.5
- norm_params: float32 [2, 4, 128], replicated, may hold values from -1.2 to 1.5
- norm_momentum: float32 [2, 4, 128], replicated, may hold values from -1536 to 1536
- norm_average: float32 [2, 4, 128], replicated, may hold values from -6 to 6
- value_filter: float32 [2, 9, 64], P(None, None, 'head'), may hold values from -2 to 2
- value_momentum: float32 [2, 9, 64], P(None, None, 'head'), may hold values from -768 to 768
- value_average: float32 [2, 9, 64], P(None, None, 'head'), may hold values from -5 to 5
- hidden_filter: float32 [9, 1024], P(None, 'head'), may hold values from -2 to 2
- hidden_momentum: float32 [9, 1024], P(None, 'head'), may hold values from -640 to 640
- hidden_average: float32 [9, 1024], P(None, 'head'), may hold values from -5 to 5
Outputs:
- output: bfloat16 [256, 32, 32, 128], P('dp')
- input_grad: float32 [256, 32, 32, 128], P('dp')
- entry_velocity: float32 [3, 128, 128], P(None, 'dp', 'head')
- entry_updated: float32 [3, 128, 128], P(None, 'dp', 'head')
- entry_smoothed: float32 [3, 128, 128], P(None, 'dp', 'head')
- mixing_velocity: float32 [128, 128], P('head', 'dp')
- mixing_updated: float32 [128, 128], P('head', 'dp')
- mixing_smoothed: float32 [128, 128], P('head', 'dp')
- expand_velocity: float32 [128, 1024], P('dp', 'head')
- expand_updated: float32 [128, 1024], P('dp', 'head')
- expand_smoothed: float32 [128, 1024], P('dp', 'head')
- shrink_velocity: float32 [1024, 128], P('head', 'dp')
- shrink_updated: float32 [1024, 128], P('head', 'dp')
- shrink_smoothed: float32 [1024, 128], P('head', 'dp')
- reduce_velocity: float32 [2560, 128], P('dp', 'head')
- reduce_updated: float32 [2560, 128], P('dp', 'head')
- reduce_smoothed: float32 [2560, 128], P('dp', 'head')
- norm_velocity: float32 [2, 4, 128], replicated
- norm_updated: float32 [2, 4, 128], replicated
- norm_smoothed: float32 [2, 4, 128], replicated
- value_velocity: float32 [2, 9, 64], P(None, None, 'head')
- value_updated: float32 [2, 9, 64], P(None, None, 'head')
- value_smoothed: float32 [2, 9, 64], P(None, None, 'head')
- hidden_velocity: float32 [9, 1024], P(None, 'head')
- hidden_updated: float32 [9, 1024], P(None, 'head')
- hidden_smoothed: float32 [9, 1024], P(None, 'head')
Inputs may be any that keep to these rules, and one draw needn't show every extreme that they name: `resolution`: 32 is a multiple of it; every image of a grid is a square of resolution x resolution patches, numbered in raster order. `live_images`: the images that hold data are the first ones in raster order; at most (32 // resolution) ** 2.
All inputs are finite; a program needn't handle non-finite values.
Results may differ from a plain program's by a relative error of at most 0.019.
Values may be sent and summed in bfloat16 or wider, within the bound.
A program may use at most 704 MiB of HBM per device.

v0:
```python
from functools import partial

import jax
import jax.numpy as jnp
from jax import lax
from jax.sharding import PartitionSpec as P

SR_WIDE = 4
SR_NARROW = 2


NEGATIVE = -1000000000.0
EPSILON = 1e-06


def layer_norm(values, norm_gain, norm_shift):
    average = jnp.mean(values, -1, keepdims=True)
    centred = values - average
    spread = jnp.mean(centred * centred, -1, keepdims=True)
    return centred * lax.rsqrt(spread + EPSILON) * norm_gain + norm_shift


def cell_act(values, norm_gain, norm_shift):
    return jax.nn.gelu(layer_norm(values, norm_gain, norm_shift), approximate=False)


def image_ids(resolution, grid_side, stride):
    cells_side = grid_side // stride
    positions = jnp.arange(cells_side, dtype=jnp.int32) * stride
    across = (grid_side // resolution)[:, None, None]
    row_image = positions[None, :, None] // resolution[:, None, None]
    column_image = positions[None, None, :] // resolution[:, None, None]
    return row_image * across + column_image


def depthwise(values, image_map, weights):
    cells_side = values.shape[1]
    padded = jnp.pad(values, ((0, 0), (1, 1), (1, 1), (0, 0)))
    padded_map = jnp.pad(image_map, ((0, 0), (1, 1), (1, 1)), constant_values=-1)
    summed = jnp.zeros_like(values)
    for offset in range(9):
        row_shift = offset // 3
        column_shift = offset % 3
        same_image = (
            padded_map[
                :, row_shift : row_shift + cells_side, column_shift : column_shift + cells_side
            ]
            == image_map
        ).astype(values.dtype)
        summed = (
            summed
            + padded[
                :, row_shift : row_shift + cells_side, column_shift : column_shift + cells_side, :
            ]
            * same_image[..., None]
            * weights[offset]
        )
    return summed


def conv_add(values, weights, image_map):
    return values + depthwise(values, image_map, weights)


def patch_rows(active, stride):
    count_grids = active.shape[0]
    cells_side = active.shape[1] // stride
    features = active.shape[3]
    blocks = active.reshape(count_grids, cells_side, stride, cells_side, stride, features)
    return blocks.transpose(0, 1, 3, 2, 4, 5).reshape(
        count_grids, cells_side, cells_side, stride * stride * features
    )


def patch_back(gradient, stride, grid_side):
    count_grids = gradient.shape[0]
    cells_side = gradient.shape[1]
    features = gradient.shape[3] // (stride * stride)
    blocks = gradient.reshape(count_grids, cells_side, cells_side, stride, stride, features)
    return blocks.transpose(0, 1, 3, 2, 4, 5).reshape(count_grids, grid_side, grid_side, features)


def dense(left_side, right_side):
    return jnp.einsum("...d,de->...e", left_side, right_side, preferred_element_type=jnp.float32)


def dense_back(gradient, weight):
    return jnp.einsum("...e,de->...d", gradient, weight, preferred_element_type=jnp.float32)


def weight_grad(inputs, gradient):
    flat_inputs = inputs.reshape(-1, inputs.shape[-1])
    flat_grad = gradient.reshape(-1, gradient.shape[-1])
    return lax.dot_general(
        flat_inputs, flat_grad, (((0,), (0,)), ((), ())), preferred_element_type=jnp.float32
    )


def advance(weight, moment, average, gradient, step_rate, weight_decay):
    gradient = gradient + weight_decay * weight
    moment = 0.9 * moment + gradient
    weight = weight - step_rate * (gradient + 0.9 * moment)
    return (moment, weight, 0.8 * average + 0.2 * weight)


def per_device(
    tokens,
    cotangent,
    resolution,
    live_images,
    entry_weight,
    entry_momentum,
    entry_average,
    mixing_weight,
    mixing_momentum,
    mixing_average,
    expand_weight,
    expand_momentum,
    expand_average,
    shrink_weight,
    shrink_momentum,
    shrink_average,
    reduce_weight,
    reduce_momentum,
    reduce_average,
    norm_params,
    norm_momentum,
    norm_average,
    value_filter,
    value_momentum,
    value_average,
    hidden_filter,
    hidden_momentum,
    hidden_average,
):
    initial_grids = tokens.shape[0]
    grid_side = tokens.shape[1]
    features = tokens.shape[3]
    head_width = features // 4
    scaling = head_width ** (-0.5)
    positions = grid_side * grid_side
    entry_low, mixing_low, expand_low, shrink_low, reduce_low = (
        lax.all_gather(entry_weight.astype(jnp.bfloat16), "dp", axis=1, tiled=True),
        lax.all_gather(mixing_weight.astype(jnp.bfloat16), "dp", axis=1, tiled=True),
        lax.all_gather(expand_weight.astype(jnp.bfloat16), "dp", axis=0, tiled=True),
        lax.all_gather(shrink_weight.astype(jnp.bfloat16), "dp", axis=1, tiled=True),
        lax.all_gather(reduce_weight.astype(jnp.bfloat16), "dp", axis=0, tiled=True),
    )
    reduce_full = lax.all_gather(reduce_low, "head", axis=1, tiled=True)
    heads_here = entry_low.shape[2] // (2 * head_width)
    image_map = image_ids(resolution, grid_side, 1)
    live_mask = (image_map < live_images[:, None, None]).astype(jnp.float32)
    live_count = jnp.sum(live_mask)
    inputs = tokens.astype(jnp.float32)
    first_norm, first_back = jax.vjp(layer_norm, inputs, norm_params[0, 0], norm_params[1, 0])
    normed = first_norm.astype(jnp.bfloat16)
    queries = (
        dense(normed, entry_low[0])
        .astype(jnp.bfloat16)
        .reshape(initial_grids, positions, heads_here, 2, head_width)
    )
    strides = (SR_WIDE, SR_NARROW)
    starts = (0, SR_WIDE * SR_WIDE * features)
    row_counts = (SR_WIDE * SR_WIDE * features, SR_NARROW * SR_NARROW * features)
    patches = [patch_rows(normed, stride) for stride in strides]
    reduced = [
        dense(
            patches[group_index],
            reduce_full[starts[group_index] : starts[group_index] + row_counts[group_index]],
        )
        for group_index in range(2)
    ]
    saved_group = []
    results = []
    for group_index in range(2):
        cells_side = grid_side // strides[group_index]
        keys_count = cells_side * cells_side
        cell_map = image_ids(resolution, grid_side, strides[group_index])
        cell_out, cell_back = jax.vjp(
            cell_act,
            reduced[group_index],
            norm_params[0, 1 + group_index],
            norm_params[1, 1 + group_index],
        )
        cell_low = cell_out.astype(jnp.bfloat16)
        key_value = dense(cell_low, entry_low[1 + group_index]).reshape(
            initial_grids, cells_side, cells_side, heads_here, 2, head_width
        )
        keys_low = (
            key_value[..., 0, :]
            .astype(jnp.bfloat16)
            .reshape(initial_grids, keys_count, heads_here, head_width)
        )
        values_raw = key_value[..., 1, :].reshape(
            initial_grids, cells_side, cells_side, heads_here * head_width
        )
        enhanced, enhance_back = jax.vjp(
            partial(conv_add, image_map=cell_map), values_raw, value_filter[group_index]
        )
        values_low = enhanced.astype(jnp.bfloat16).reshape(
            initial_grids, keys_count, heads_here, head_width
        )
        query_group = queries[:, :, :, group_index, :]
        scores = jnp.einsum(
            "gqje,gkje->gjkq", query_group, keys_low, preferred_element_type=jnp.float32
        )
        same_image = cell_map.reshape(initial_grids, 1, keys_count, 1) == image_map.reshape(
            initial_grids, 1, 1, positions
        )
        scores = jnp.where(same_image, scaling * scores, NEGATIVE)
        exponent = jnp.exp(scores - jnp.max(scores, 2, keepdims=True))
        weights_soft = exponent / jnp.sum(exponent, 2, keepdims=True)
        weights_low = weights_soft.astype(jnp.bfloat16)
        results.append(
            jnp.einsum(
                "gjkq,gkje->gqje", weights_low, values_low, preferred_element_type=jnp.float32
            )
        )
        saved_group.append(
            (
                cell_low,
                cell_back,
                keys_low,
                values_low,
                enhance_back,
                weights_soft,
                weights_low,
                query_group,
            )
        )
    mixed = (
        jnp.stack(results, 3)
        .astype(jnp.bfloat16)
        .reshape(initial_grids, grid_side, grid_side, heads_here * 2 * head_width)
    )
    attended = dense(mixed, mixing_low)
    attended = lax.psum(attended.astype(jnp.bfloat16), "head").astype(jnp.float32)
    middle = inputs + attended
    second_norm, second_back = jax.vjp(layer_norm, middle, norm_params[0, 3], norm_params[1, 3])
    second = second_norm.astype(jnp.bfloat16)
    hidden = dense(second, expand_low)
    mixed_hidden, hidden_back = jax.vjp(
        partial(conv_add, image_map=image_map), hidden, hidden_filter
    )
    activated, gelu_back = jax.vjp(partial(jax.nn.gelu, approximate=False), mixed_hidden)
    activated_low = activated.astype(jnp.bfloat16)
    feedforward = dense(activated_low, shrink_low)
    feedforward = lax.psum(feedforward.astype(jnp.bfloat16), "head").astype(jnp.float32)
    output_here = (middle + feedforward).astype(jnp.bfloat16)
    upstream = cotangent.astype(jnp.float32) * live_mask[..., None]
    upstream_low = upstream.astype(jnp.bfloat16)
    shrink_grad = weight_grad(activated_low, upstream_low)
    (activated_grad,) = gelu_back(dense_back(upstream_low, shrink_low))
    hidden_grad, hidden_filter_grad = hidden_back(activated_grad)
    hidden_low = hidden_grad.astype(jnp.bfloat16)
    expand_grad = weight_grad(second, hidden_low)
    second_grad = dense_back(hidden_low, expand_low)
    second_grad = lax.psum(second_grad.astype(jnp.bfloat16), "head").astype(jnp.float32)
    middle_part, second_gain, second_shift = second_back(second_grad)
    middle_grad = upstream + middle_part
    middle_low = middle_grad.astype(jnp.bfloat16)
    mixing_grad = weight_grad(mixed, middle_low)
    mixed_grad = (
        dense_back(middle_low, mixing_low)
        .astype(jnp.bfloat16)
        .reshape(initial_grids, positions, heads_here, 2, head_width)
    )
    query_grads = []
    entry_grads = []
    cell_grads = []
    value_grads = []
    for group_index in range(2):
        (
            cell_low,
            cell_back,
            keys_low,
            values_low,
            enhance_back,
            weights_soft,
            weights_low,
            query_group,
        ) = saved_group[group_index]
        cells_side = grid_side // strides[group_index]
        output_grad = mixed_grad[:, :, :, group_index, :]
        prob_grad = jnp.einsum(
            "gqje,gkje->gjkq", output_grad, values_low, preferred_element_type=jnp.float32
        )
        score_grad = weights_soft * (
            prob_grad - jnp.sum(weights_soft * prob_grad, 2, keepdims=True)
        )
        score_low = (scaling * score_grad).astype(jnp.bfloat16)
        query_grads.append(
            jnp.einsum("gjkq,gkje->gqje", score_low, keys_low, preferred_element_type=jnp.float32)
        )
        key_grad = jnp.einsum(
            "gjkq,gqje->gkje", score_low, query_group, preferred_element_type=jnp.float32
        )
        enhanced_grad = jnp.einsum(
            "gjkq,gqje->gkje", weights_low, output_grad, preferred_element_type=jnp.float32
        )
        enhanced_grad = lax.optimization_barrier(enhanced_grad.astype(jnp.bfloat16)).astype(
            jnp.float32
        )
        raw_grad, filter_grad = enhance_back(
            enhanced_grad.reshape(initial_grids, cells_side, cells_side, heads_here * head_width)
        )
        key_part = key_grad.astype(jnp.bfloat16).reshape(
            initial_grids, cells_side, cells_side, heads_here, head_width
        )
        value_part = raw_grad.astype(jnp.bfloat16).reshape(
            initial_grids, cells_side, cells_side, heads_here, head_width
        )
        pair_low = jnp.stack([key_part, value_part], 4).reshape(
            initial_grids, cells_side, cells_side, heads_here * 2 * head_width
        )
        entry_grads.append(weight_grad(cell_low, pair_low))
        cell_grads.append(dense_back(pair_low, entry_low[1 + group_index]))
        value_grads.append(filter_grad)
    query_low = (
        jnp.stack(query_grads, 3)
        .astype(jnp.bfloat16)
        .reshape(initial_grids, grid_side, grid_side, heads_here * 2 * head_width)
    )
    entry_grads = [weight_grad(normed, query_low)] + entry_grads
    normed_part = dense_back(query_low, entry_low[0])
    cell_first, cell_second, normed_grad = (
        lax.psum(cell_grads[0].astype(jnp.bfloat16), "head").astype(jnp.float32),
        lax.psum(cell_grads[1].astype(jnp.bfloat16), "head").astype(jnp.float32),
        lax.psum(normed_part.astype(jnp.bfloat16), "head").astype(jnp.float32),
    )
    summed_cells = (cell_first, cell_second)
    cell_gains = []
    cell_shifts = []
    reduce_parts = []
    for group_index in range(2):
        reduced_grad, cell_gain, cell_shift = saved_group[group_index][1](summed_cells[group_index])
        reduced_low = reduced_grad.astype(jnp.bfloat16)
        own_columns = lax.dynamic_slice_in_dim(
            reduced_low, lax.axis_index("head") * 2 * head_width, 2 * head_width, 3
        )
        reduce_parts.append(weight_grad(patches[group_index], own_columns))
        rows_slice = reduce_full[
            starts[group_index] : starts[group_index] + row_counts[group_index]
        ]
        normed_grad = normed_grad + patch_back(
            dense_back(reduced_low, rows_slice), strides[group_index], grid_side
        )
        cell_gains.append(cell_gain)
        cell_shifts.append(cell_shift)
    reduce_grad = jnp.concatenate(reduce_parts, 0)
    input_part, first_gain, first_shift = first_back(normed_grad)
    input_raw = middle_grad + input_part
    norm_grad = jnp.stack(
        [
            jnp.stack([first_gain, cell_gains[0], cell_gains[1], second_gain]),
            jnp.stack([first_shift, cell_shifts[0], cell_shifts[1], second_shift]),
        ]
    )
    value_grad = jnp.stack(value_grads)
    entry_grad = jnp.stack(entry_grads)
    entry_grad, mixing_grad, expand_grad, shrink_grad, reduce_grad = (
        lax.psum_scatter(entry_grad, "dp", scatter_dimension=1, tiled=True),
        lax.psum_scatter(mixing_grad, "dp", scatter_dimension=1, tiled=True),
        lax.psum_scatter(expand_grad, "dp", scatter_dimension=0, tiled=True),
        lax.psum_scatter(shrink_grad, "dp", scatter_dimension=1, tiled=True),
        lax.psum_scatter(reduce_grad, "dp", scatter_dimension=0, tiled=True),
    )
    norm_grad, value_grad, hidden_filter_grad, live_total = lax.psum(
        (norm_grad, value_grad, hidden_filter_grad, live_count), "dp"
    )
    tokens_all = lax.axis_size("dp") * initial_grids * positions
    factor = tokens_all / live_total
    rate_unit = tokens_all ** (-0.5)
    input_grad = factor * input_raw
    entry_velocity, entry_updated, entry_smoothed = advance(
        entry_weight, entry_momentum, entry_average, factor * entry_grad, 0.3 * rate_unit, 0.05
    )
    mixing_velocity, mixing_updated, mixing_smoothed = advance(
        mixing_weight, mixing_momentum, mixing_average, factor * mixing_grad, 0.12 * rate_unit, 0.05
    )
    expand_velocity, expand_updated, expand_smoothed = advance(
        expand_weight, expand_momentum, expand_average, factor * expand_grad, 0.12 * rate_unit, 0.05
    )
    shrink_velocity, shrink_updated, shrink_smoothed = advance(
        shrink_weight, shrink_momentum, shrink_average, factor * shrink_grad, 0.03 * rate_unit, 0.05
    )
    reduce_velocity, reduce_updated, reduce_smoothed = advance(
        reduce_weight, reduce_momentum, reduce_average, factor * reduce_grad, 0.1 * rate_unit, 0.05
    )
    norm_velocity, norm_updated, norm_smoothed = advance(
        norm_params, norm_momentum, norm_average, factor * norm_grad, 0.2 * rate_unit, 0.0
    )
    value_velocity, value_updated, value_smoothed = advance(
        value_filter, value_momentum, value_average, factor * value_grad, 0.4 * rate_unit, 0.05
    )
    hidden_velocity, hidden_updated, hidden_smoothed = advance(
        hidden_filter,
        hidden_momentum,
        hidden_average,
        factor * hidden_filter_grad,
        0.5 * rate_unit,
        0.05,
    )
    return (
        output_here,
        input_grad,
        entry_velocity,
        entry_updated,
        entry_smoothed,
        mixing_velocity,
        mixing_updated,
        mixing_smoothed,
        expand_velocity,
        expand_updated,
        expand_smoothed,
        shrink_velocity,
        shrink_updated,
        shrink_smoothed,
        reduce_velocity,
        reduce_updated,
        reduce_smoothed,
        norm_velocity,
        norm_updated,
        norm_smoothed,
        value_velocity,
        value_updated,
        value_smoothed,
        hidden_velocity,
        hidden_updated,
        hidden_smoothed,
    )


def solution(mesh):
    in_specs = (
        P("dp", None, None, None),
        P("dp", None, None, None),
        P("dp"),
        P("dp"),
        P(None, "dp", "head"),
        P(None, "dp", "head"),
        P(None, "dp", "head"),
        P("head", "dp"),
        P("head", "dp"),
        P("head", "dp"),
        P("dp", "head"),
        P("dp", "head"),
        P("dp", "head"),
        P("head", "dp"),
        P("head", "dp"),
        P("head", "dp"),
        P("dp", "head"),
        P("dp", "head"),
        P("dp", "head"),
        P(),
        P(),
        P(),
        P(None, None, "head"),
        P(None, None, "head"),
        P(None, None, "head"),
        P(None, "head"),
        P(None, "head"),
        P(None, "head"),
    )
    out_specs = (
        P("dp", None, None, None),
        P("dp", None, None, None),
        P(None, "dp", "head"),
        P(None, "dp", "head"),
        P(None, "dp", "head"),
        P("head", "dp"),
        P("head", "dp"),
        P("head", "dp"),
        P("dp", "head"),
        P("dp", "head"),
        P("dp", "head"),
        P("head", "dp"),
        P("head", "dp"),
        P("head", "dp"),
        P("dp", "head"),
        P("dp", "head"),
        P("dp", "head"),
        P(),
        P(),
        P(),
        P(None, None, "head"),
        P(None, None, "head"),
        P(None, None, "head"),
        P(None, "head"),
        P(None, "head"),
        P(None, "head"),
    )
    return jax.shard_map(
        per_device, mesh=mesh, in_specs=in_specs, out_specs=out_specs, check_vma=False
    )
```

profile of v0, /device:TPU:0, one launch (start us, length us, event | category | flops | bytes accessed | tf_op | source)
XLA Modules:
  0.0 1771.9 jit_solution(214941649878217232)
XLA Ops:
  15.0 42.9 %all_gather.20 = bf16[3,128,64]{2,1,0:T(8,128)(2,1)S(1)} all-gather(bf16[3,8,64]{2,1,0:T(8,128)(2,1)S(1)} %convert_element_type.336), channel_id=1, replica_groups=mesh['dp'=16,'head'=2] {'dp'}, dimensions={1}, use_global_device_ids=true | all-gather | bytes 52224 | tf_op jit(solution)/shard_map/all_gather | solution.py:143
  70.0 38.3 %all-gather = bf16[16,160,64]{1,2,0:T(8,128)(2,1)S(1)} all-gather(bf16[1,160,64]{1,2,0:T(8,128)(2,1)S(1)} %convert_bitcast_fusion), channel_id=1, replica_groups=mesh['dp'=16,'head'=2] {'dp'}, dimensions={0}, use_global_device_ids=true | all-gather | bytes 348160 | tf_op jit(solution)/shard_map/all_gather | solution.py:147
  153.9 39.9 %all_gather.21 = bf16[64,128]{0,1:T(8,128)(2,1)} all-gather(bf16[64,8]{0,1:T(8,128)(2,1)S(1)} %convert_element_type.363), channel_id=1, replica_groups=mesh['dp'=16,'head'=2] {'dp'}, dimensions={1}, use_global_device_ids=true | all-gather | bytes 17408 | tf_op jit(solution)/shard_map/all_gather | solution.py:144
  216.4 14.9 reshape.1450
  231.2 17.7 %fusion.287 = (bf16[16,1024,1,1,32]{4,3,1,0,2:T(2,128)(2,1)}, bf16[16,1024,1,1,32]{4,3,1,0,2:T(2,128)(2,1)}) fusion(bf16[16,1024,1,2,32]{4,3,1,0,2:T(2,128)(2,1)} %reshape.1450), kind=kLoop, calls=%fused_computation.590 | loop fusion | bytes 4194304 | tf_op jit(solution)/shard_map/slice | solution.py:203
  249.0 19.0 %copy.379 = bf16[16,1024,1,1,32]{1,4,0,3,2:T(8,128)(2,1)} copy(bf16[16,1024,1,1,32]{4,3,1,0,2:T(2,128)(2,1)} %get-tuple-element.253) | data formatting | bytes 2097152
  267.9 19.1 %copy.382 = bf16[16,1024,1,1,32]{1,4,0,3,2:T(8,128)(2,1)} copy(bf16[16,1024,1,1,32]{4,3,1,0,2:T(2,128)(2,1)} %get-tuple-element.254) | data formatting | bytes 2097152
  293.0 11.2 fusion.292
  311.6 9.4 fusion.101
  326.7 14.6 copy.367
  341.3 14.2 reshape.1451
  361.1 38.5 %all_gather.23 = bf16[512,128]{0,1:T(8,128)(2,1)} all-gather(bf16[512,8]{0,1:T(8,128)(2,1)S(1)} %convert_element_type.377), channel_id=1, replica_groups=mesh['dp'=16,'head'=2] {'dp'}, dimensions={1}, use_global_device_ids=true | all-gather | bytes 139264 | tf_op jit(solution)/shard_map/all_gather | solution.py:146
  399.5 38.2 %all_gather.22 = bf16[128,512]{1,0:T(8,128)(2,1)S(1)} all-gather(bf16[8,512]{1,0:T(8,128)(2,1)S(1)} %convert_element_type.367), channel_id=1, replica_groups=mesh['dp'=16,'head'=2] {'dp'}, dimensions={0}, use_global_device_ids=true | all-gather | bytes 139264 | tf_op jit(solution)/shard_map/all_gather | solution.py:145
  451.4 12.8 fusion.215
  464.3 147.8 %convert_reduce_fusion.1 = (u32[16,32,512]{2,1,0:T(8,128)S(1)}, u32[16,32,512]{2,1,0:T(8,128)S(1)}, f32[16,32,32,512]{3,2,1,0:T(8,128)}) fusion(f32[16,32,32,512]{3,2,1,0:T(8,128)} %fusion.215, f32[512]{0:T(512)S(1)} %bitcast.511, f32[16,32,32]{2,1,0:T(8,128)} %get-tuple-element.284, f32[512]{0:T(512)S(1)} %bitcast.497, ...), kind=kLoop, calls=%fused_computation.27 | loop fusion | flops 309854208 | bytes 69748736
  612.1 77.0 %multiply_convert_fusion = (bf16[16,32,32,512]{3,2,1,0:T(8,128)(2,1)}, f32[16,32,32,512]{3,2,1,0:T(8,128)}) fusion(f32[16,32,32,512]{3,2,1,0:T(8,128)} %get-tuple-element.235, u32[16,32,512]{2,1,0:T(8,128)S(1)} %get-tuple-element.166, u32[16,32,512]{2,1,0:T(8,128)S(1)} %get-tuple-element.165), kind=kLoop, calls=%fused_computation.54 | loop fusion | flops 570425344 | bytes 85983232 | tf_op jit(solution)/shard_map/convert_element_type | solution.py:246
  689.2 136.3 %multiply_reduce_fusion.8 = (f32[512]{0:T(512)}, f32[512]{0:T(512)}, f32[512]{0:T(512)}, f32[512]{0:T(512)}, f32[512]{0:T(512)}, /*index=5*/f32[512]{0:T(512)}, ...) fusion(f32[16,32,32,512]{3,2,1,0:T(8,128)} %fusion.215, ...), kind=kOutput, calls=%fused_computation.44 | convolution fusion | flops 2497703424 | bytes 172707840 | tf_op jit(solution)/shard_map/...e,de->...d/dot_general | solution.py:88
  825.6 95.9 %multiply_multiply_fusion.7 = (f32[16,32,32,512]{3,2,1,0:T(8,128)}, f32[16,32,32,512]{3,2,1,0:T(8,128)}, f32[16,32,32,512]{3,2,1,0:T(8,128)}, f32[16,32,32,512]{...) fusion(f32[16,32,32,512]{3,2,1,0:T(8,128)} %get-tuple-element.3, ...), kind=kLoop, calls=%fused_computation.52 | loop fusion | flops 125829120 | bytes 302465024 | tf_op jit(solution)/shard_map/transpose(jvp())/mul | solution.py:52
  921.4 50.4 %pad_add_fusion = f32[16,34,34,512]{3,2,1,0:T(8,128)} fusion(f32[16,32,32,512]{3,2,1,0:T(8,128)} %get-tuple-element.247, f32[16,32,32,512]{3,2,1,0:T(8,128)} %get-tuple-element.248, f32[16,32,32,512]{3,2,1,0:T(8,128)} %get-tuple-element.241), kind=kLoop, calls=%fused_computation.13 | loop fusion | flops 18939904 | bytes 138543104 | tf_op jit(solution)/shard_map/transpose(jvp())/add_any | solution.py:52
  971.9 91.5 %fusion.14 = bf16[16,32,32,512]{3,2,1,0:T(8,128)(2,1)} fusion(f32[16,32,32,512]{3,2,1,0:T(8,128)} %get-tuple-element.358, f32[16,32,32,512]{3,2,1,0:T(8,128)} %get-tuple-element.240, f32[16,32,32,512]{3,2,1,0:T(8,128)} %get-tuple-element.242, f32[16,32,32,512]{3,2,1,0:T(8,128)} %get-tuple-element.243, f32[16,32,32,512]{3,2,1,0:T(8,128)} %get-tuple-element.244, ...), kind=kLoop, calls=%fused_computation.30 | loop fusion | flops 67108864 | bytes 285212672 | tf_op jit(solution)/shard_map/convert_element_type | solution.py:255
  1063.4 12.4 convolution_convert_fusion.2
  1075.8 14.4 convolution_convert_fusion.3
  1090.2 10.0 all-reduce.71.cloned.1.call-done
  1100.2 9.6 fusion.35
  1109.9 10.9 fusion.38
  1121.6 12.2 fusion.52
  1139.0 14.7 reshape.1452
  1153.7 17.8 %fusion.286 = (bf16[16,1024,1,1,32]{4,3,1,0,2:T(2,128)(2,1)}, bf16[16,1024,1,1,32]{4,3,1,0,2:T(2,128)(2,1)}) fusion(bf16[16,1024,1,2,32]{4,3,1,0,2:T(2,128)(2,1)} %reshape.1452), kind=kLoop, calls=%fused_computation.589 | loop fusion | bytes 4194304 | tf_op jit(solution)/shard_map/slice | solution.py:284
  1171.5 17.2 copy.383
  1202.2 8.6 fusion.113
  1223.9 17.2 copy.384
  1241.2 9.4 fusion.125
  1252.0 12.8 multiply_reduce_fusion.19
  1280.6 22.3 %fusion.122 = bf16[16,256,1,32]{1,3,0,2:T(8,128)(2,1)S(1)} fusion(f32[16,256,1024]{2,1,0:T(8,128)} %fusion.140, bf16[16,1024,1,1,32]{1,4,0,3,2:T(8,128)(2,1)} %copy.382, f32[16,256,1024]{2,1,0:T(8,128)} %get-tuple-element.353, f32[16,1024]{1,0:T(8,128)S(1)} %copy-done.236), kind=kOutput, calls=%fused_computation.242 | convolution fusion | flops 297943296 | bytes 34930688 | tf_op jit(solution)/shard_map/gjkq,gqje->gkje/dot_general | solution.py:295
  1303.0 23.0 %fusion.110 = bf16[16,1024,1,1,32]{1,4,0,3,2:T(8,128)(2,1)} fusion(bf16[16,256,32]{2,1,0:T(8,128)(2,1)S(1)} %bitcast.493, f32[16,256,1024]{2,1,0:T(8,128)} %fusion.140, f32[16,256,1024]{2,1,0:T(8,128)} %get-tuple-element.353, f32[16,1024]{1,0:T(8,128)S(1)} %copy-done.236), kind=kOutput, calls=%fused_computation.235 | convolution fusion | flops 298336512 | bytes 34930688 | tf_op jit(solution)/shard_map/gjkq,gkje->gqje/dot_general | solution.py:293
  1347.4 14.2 copy.371
  1372.0 14.2 reshape.1453
  1413.1 12.4 convolution_bitcast_fusion.3
  1425.6 10.9 fusion.128
  1447.8 32.3 %all-reduce.73.cloned.1.call-done = f32[3,128,64]{2,0,1:T(4,128)} async-done(((f32[3,128,64]{2,0,1:T(4,128)}), f32[3,128,64]{2,0,1:T(4,128)}) %all-reduce.73.cloned.1.call-update) | async-done | bytes 98320
  1480.9 43.2 %all-reduce.75.cloned.1.call-done = (bf16[16,32,32,128]{3,2,1,0:T(8,128)(2,1)}, bf16[16,16,16,128]{3,2,1,0:T(8,128)(2,1)}, bf16[16,8,8,128]{3,2,1,0:T(8,128)(2,1)}, bf16[16,32,32,128]{3,2,1,0:T(8,128)(2,1)}) async-done(((bf16[16,32,32,128]{3,2,1,0:T(8,128)(2,1)}, bf16[16,16,16,128]{3,2,1,0:T(8,128)(2,1)}, bf16[16,8,8,128]{3,2,1,0:T(8,128)(2,1)}, bf16[16,32,32,128]{3,2,1,0:T(8,128)(2,1)}), ...) | async-done | bytes 9699344 | tf_op jit(solution)/shard_map/psum | solution.py:248
  1550.7 10.6 reshape.1426
  1569.7 10.0 copy.322
  1579.7 10.9 fusion.37
  1592.7 11.1 fusion.34
  1604.0 78.1 %all-reduce.62 = (f32[]{:T(128)}, f32[64,128]{0,1:T(8,128)S(1)}, f32[2,4,128]{2,1,0:T(4,128)S(1)}, f32[2,9,32]{2,1,0:T(8,128)S(1)}, f32[9,512]{1,0:T(8,128)S(1)}) all-reduce(f32[]{:T(128)} %fusion.233, f32[64,128]{0,1:T(8,128)S(1)} %copy-done.118, f32[2,4,128]{2,1,0:T(4,128)S(1)} %pad_maximum_fusion.6, ...), channel_id=1, replica_groups=mesh['dp'=16,'head'=2] {'dp'}, use_global_device_ids=true, to_apply=%region_15.16 | all-reduce | flops 14401 | bytes 115208 | tf_op jit(solution)/shard_map/psum | solution.py:368
  1688.2 27.1 %add_multiply_fusion = (f32[16,32,32,128]{3,2,1,0:T(8,128)}, bf16[16,32,32,128]{3,2,1,0:T(8,128)(2,1)}) fusion(bf16[16,32,32,128]{3,2,1,0:T(8,128)(2,1)} %param.29, f32[16,32,32]{2,1,0:T(8,128)S(1)} %negate_multiply_fusion.3, f32[16,32,32]{2,1,0:T(8,128)S(1)} %copy-done.55, f32[16,32,32]{2,1,0:T(8,128)S(1)} %copy-done.53, f32[]{:T(128)S(6)} %div.239, ...), kind=kLoop, calls=%fused_computation.98 | loop fusion | flops 54525952 | bytes 42533892 | tf_op jit(solution)/shard_map/mul | solution.py:374
  1720.6 42.3 %reduce-scatter.10.cloned.1.call-done = f32[160,64]{1,0:T(8,128)} async-done(((f32[2560,64]{1,0:T(8,128)}), f32[160,64]{1,0:T(8,128)}) %reduce-scatter.10.cloned.1.call-update) | async-done | bytes 40976
  (652 shorter events, 293.6 us)
Async XLA Ops:
  7.2 432.8 %all-reduce.69.cloned.1.call-start = ((), (), s32[]{:S(2)}) async-start(), calls=%async_computation.3 | async-start | bytes 8388608 | tf_op jit(solution)/shard_map/psum | solution.py:237
  11.9 292.4 %copy-start.69 = (f32[16,16,16]{2,1,0:T(8,128)}, f32[16,16,16]{2,1,0:T(8,128)S(1)}, u32[]{:S(2)}) copy-start(f32[16,16,16]{2,1,0:T(8,128)S(1)} %get-tuple-element.287) | copy-start | bytes 49156
  11.9 292.4 %copy-start.71 = (f32[16,16,16]{2,1,0:T(8,128)}, f32[16,16,16]{2,1,0:T(8,128)S(1)}, u32[]{:S(2)}) copy-start(f32[16,16,16]{2,1,0:T(8,128)S(1)} %get-tuple-element.288) | copy-start | bytes 49156
  11.9 292.4 %copy-start.73 = (f32[16,16,16]{2,1,0:T(8,128)}, f32[16,16,16]{2,1,0:T(8,128)S(1)}, u32[]{:S(2)}) copy-start(f32[16,16,16]{2,1,0:T(8,128)S(1)} %get-tuple-element.289) | copy-start | bytes 49156
  11.9 292.4 %copy-start.75 = (f32[16,16,16]{2,1,0:T(8,128)}, f32[16,16,16]{2,1,0:T(8,128)S(1)}, u32[]{:S(2)}) copy-start(f32[16,16,16]{2,1,0:T(8,128)S(1)} %get-tuple-element.290) | copy-start | bytes 49156
  13.5 105.9 %copy-start.174 = (f32[128]{0:T(128)}, f32[128]{0:T(128)S(1)}, u32[]{:S(2)}) copy-start(f32[128]{0:T(128)S(1)} %get-tuple-element.340) | copy-start | bytes 1540
  57.9 91.9 %copy-start.106 = (bf16[3,128,64]{2,1,0:T(8,128)(2,1)}, bf16[3,128,64]{2,1,0:T(8,128)(2,1)S(1)}, u32[]{:S(2)}) copy-start(bf16[3,128,64]{2,1,0:T(8,128)(2,1)S(1)} %all_gather.20) | copy-start | bytes 147460
  111.8 95.2 %copy-start.33 = (bf16[2560,128]{0,1:T(8,128)(2,1)}, bf16[2560,128]{0,1:T(8,128)(2,1)S(1)}, u32[]{:S(2)}) copy-start(bf16[2560,128]{0,1:T(8,128)(2,1)S(1)} %all_gather.19) | copy-start | bytes 1966084
  149.8 154.4 %copy-start.15 = (f32[16,16,16,32]{3,2,1,0:T(8,128)}, f32[16,16,16,32]{3,2,1,0:T(8,128)S(1)}, u32[]{:S(2)}) copy-start(f32[16,16,16,32]{3,2,1,0:T(8,128)S(1)} %get-tuple-element.256) | copy-start | bytes 1572868
  153.9 284.5 %copy-start.120 = (s32[16,32]{1,0:T(8,128)}, s32[16,32]{1,0:T(8,128)S(1)}, u32[]{:S(2)}) copy-start(s32[16,32]{1,0:T(8,128)S(1)} %get-tuple-element.346) | copy-start | bytes 6148
  153.9 284.5 %copy-start.122 = (s32[16,32]{1,0:T(8,128)}, s32[16,32]{1,0:T(8,128)S(1)}, u32[]{:S(2)}) copy-start(s32[16,32]{1,0:T(8,128)S(1)} %get-tuple-element.347) | copy-start | bytes 6148
  216.4 104.6 %copy-start.37 = (f32[16,8,8,32]{3,2,1,0:T(8,128)}, f32[16,8,8,32]{3,2,1,0:T(8,128)S(1)}, u32[]{:S(2)}) copy-start(f32[16,8,8,32]{3,2,1,0:T(8,128)S(1)} %get-tuple-element.267) | copy-start | bytes 393220
  355.5 82.2 %copy-start.126 = (f32[9,512]{1,0:T(8,128)S(1)}, f32[9,512]{1,0:T(8,128)}, u32[]{:S(2)}) copy-start(f32[9,512]{1,0:T(8,128)} %param.53) | copy-start | bytes 55300
  355.5 82.9 %copy-start.225 = (s32[16]{0:T(128)S(1)}, s32[16]{0:T(128)}, u32[]{:S(2)}) copy-start(s32[16]{0:T(128)} %param.31) | copy-start | bytes 196
  361.0 739.2 %all-reduce.71.cloned.1.call-start = ((), (), s32[]{:S(2)}) async-start(), calls=%async_computation.4 | async-start | bytes 8388608 | tf_op jit(solution)/shard_map/psum | solution.py:258
  440.0 249.1 %copy-start.50 = (f32[16,32,32]{2,1,0:T(8,128)}, f32[16,32,32]{2,1,0:T(8,128)S(1)}, u32[]{:S(2)}) copy-start(f32[16,32,32]{2,1,0:T(8,128)S(1)} %get-tuple-element.313) | copy-start | bytes 196612
  612.1 77.0 %copy-start.113 = (bf16[512,128]{0,1:T(8,128)(2,1)S(1)}, bf16[512,128]{0,1:T(8,128)(2,1)}, u32[]{:S(2)}) copy-start(bf16[512,128]{0,1:T(8,128)(2,1)} %all_gather.23) | copy-start | bytes 393220
  689.1 136.4 %copy-start.66 = (f32[16,32,32]{2,1,0:T(8,128)S(1)}, f32[16,32,32]{2,1,0:T(8,128)}, u32[]{:S(2)}) copy-start(f32[16,32,32]{2,1,0:T(8,128)} %get-tuple-element.282) | copy-start | bytes 196612
  689.1 136.4 %copy-start.67 = (f32[16,32,32]{2,1,0:T(8,128)S(1)}, f32[16,32,32]{2,1,0:T(8,128)}, u32[]{:S(2)}) copy-start(f32[16,32,32]{2,1,0:T(8,128)} %get-tuple-element.283) | copy-start | bytes 196612
  689.1 136.4 %copy-start.68 = (f32[16,32,32]{2,1,0:T(8,128)S(1)}, f32[16,32,32]{2,1,0:T(8,128)}, u32[]{:S(2)}) copy-start(f32[16,32,32]{2,1,0:T(8,128)} %get-tuple-element.284) | copy-start | bytes 196612
  689.1 136.4 %copy-start.150 = (f32[1,512]{1,0:T(1,128)S(1)}, f32[1,512]{1,0:T(1,128)}, u32[]{:S(2)}) copy-start(f32[1,512]{1,0:T(1,128)} %get-tuple-element.305) | copy-start | bytes 6148
  689.1 136.4 %copy-start.152 = (f32[1,512]{1,0:T(1,128)S(1)}, f32[1,512]{1,0:T(1,128)}, u32[]{:S(2)}) copy-start(f32[1,512]{1,0:T(1,128)} %get-tuple-element.306) | copy-start | bytes 6148
  689.1 136.4 %copy-start.154 = (f32[1,512]{1,0:T(1,128)S(1)}, f32[1,512]{1,0:T(1,128)}, u32[]{:S(2)}) copy-start(f32[1,512]{1,0:T(1,128)} %get-tuple-element.307) | copy-start | bytes 6148
  689.2 136.4 %copy-start.156 = (f32[1,512]{1,0:T(1,128)S(1)}, f32[1,512]{1,0:T(1,128)}, u32[]{:S(2)}) copy-start(f32[1,512]{1,0:T(1,128)} %get-tuple-element.308) | copy-start | bytes 6148
  689.2 136.4 %copy-start.158 = (f32[1,512]{1,0:T(1,128)S(1)}, f32[1,512]{1,0:T(1,128)}, u32[]{:S(2)}) copy-start(f32[1,512]{1,0:T(1,128)} %get-tuple-element.309) | copy-start | bytes 6148
  689.2 136.4 %copy-start.160 = (f32[1,512]{1,0:T(1,128)S(1)}, f32[1,512]{1,0:T(1,128)}, u32[]{:S(2)}) copy-start(f32[1,512]{1,0:T(1,128)} %get-tuple-element.310) | copy-start | bytes 6148
  689.2 136.4 %copy-start.162 = (f32[1,512]{1,0:T(1,128)S(1)}, f32[1,512]{1,0:T(1,128)}, u32[]{:S(2)}) copy-start(f32[1,512]{1,0:T(1,128)} %get-tuple-element.311) | copy-start | bytes 6148
  689.2 136.4 %copy-start.164 = (f32[1,512]{1,0:T(1,128)S(1)}, f32[1,512]{1,0:T(1,128)}, u32[]{:S(2)}) copy-start(f32[1,512]{1,0:T(1,128)} %get-tuple-element.312) | copy-start | bytes 6148
  971.9 91.5 %copy-start.84 = (bf16[128,512]{1,0:T(8,128)(2,1)S(1)}, bf16[128,512]{1,0:T(8,128)(2,1)}, u32[]{:S(2)}) copy-start(bf16[128,512]{1,0:T(8,128)(2,1)} %copy-done.83) | copy-start | bytes 393220
  1075.7 404.4 %all-reduce.73.cloned.1.call-start = ((), (), s32[]{:S(2)}) async-start(), calls=%async_computation.8 | async-start | bytes 524288
  1371.9 152.2 %all-reduce.75.cloned.1.call-start = ((), (), s32[]{:S(2)}) async-start(), calls=%async_computation.9 | async-start | bytes 19398656 | tf_op jit(solution)/shard_map/psum | solution.py:248
  1392.7 324.5 %reduce-scatter.6.cloned.1.call-start = ((), (), s32[]{:S(2)}) async-start(), calls=%async_computation.5 | async-start | bytes 278528 | tf_op jit(solution)/shard_map/reduce_scatter | solution.py:364
  1425.5 98.6 %copy-start.58 = (f32[16,8,8]{2,1,0:T(8,128)S(1)}, f32[16,8,8]{2,1,0:T(8,128)}, u32[]{:S(2)}) copy-start(f32[16,8,8]{2,1,0:T(8,128)} %copy-done.57) | copy-start | bytes 12292
  1425.5 98.6 %copy-start.82 = (f32[16,8,8]{2,1,0:T(8,128)S(1)}, f32[16,8,8]{2,1,0:T(8,128)}, u32[]{:S(2)}) copy-start(f32[16,8,8]{2,1,0:T(8,128)} %copy-done.81) | copy-start | bytes 12292
  1425.6 293.0 %reduce-scatter.8.cloned.1.call-start = ((), (), s32[]{:S(2)}) async-start(), calls=%async_computation.6 | async-start | bytes 278528 | tf_op jit(solution)/shard_map/reduce_scatter | solution.py:365
  1436.5 87.6 %copy-start.19 = (f32[16,8,8,128]{3,2,1,0:T(8,128)S(1)}, f32[16,8,8,128]{3,2,1,0:T(8,128)}, u32[]{:S(2)}) copy-start(f32[16,8,8,128]{3,2,1,0:T(8,128)} %copy-done.18) | copy-start | bytes 1572868
  1436.5 93.3 %copy-start.10 = (f32[16,16,16,128]{3,2,1,0:T(8,128)S(1)}, f32[16,16,16,128]{3,2,1,0:T(8,128)}, u32[]{:S(2)}) copy-start(f32[16,16,16,128]{3,2,1,0:T(8,128)} %copy-done.9) | copy-start | bytes 6291460
  1436.5 93.3 %copy-start.36 = (f32[16,16,16]{2,1,0:T(8,128)S(1)}, f32[16,16,16]{2,1,0:T(8,128)}, u32[]{:S(2)}) copy-start(f32[16,16,16]{2,1,0:T(8,128)} %copy-done.35) | copy-start | bytes 49156
  1436.5 93.3 %copy-start.49 = (f32[16,16,16]{2,1,0:T(8,128)S(1)}, f32[16,16,16]{2,1,0:T(8,128)}, u32[]{:S(2)}) copy-start(f32[16,16,16]{2,1,0:T(8,128)} %copy-done.48) | copy-start | bytes 49156
  1436.5 326.3 %reduce-scatter.10.cloned.1.call-start = ((), (), s32[]{:S(2)}) async-start(), calls=%async_computation.7 | async-start | bytes 1392640
  1592.7 91.6 %copy-start.142 = (f32[2,9,32]{2,0,1:T(2,128)S(1)}, f32[2,9,32]{2,0,1:T(2,128)}, u32[]{:S(2)}) copy-start(f32[2,9,32]{2,0,1:T(2,128)} %param.50) | copy-start | bytes 6916
  1592.7 95.2 %copy-start.40 = (f32[16,32,32]{2,1,0:T(8,128)S(1)}, f32[16,32,32]{2,1,0:T(8,128)}, u32[]{:S(2)}) copy-start(f32[16,32,32]{2,1,0:T(8,128)} %copy-done.39) | copy-start | bytes 196612
  1592.7 95.2 %copy-start.53 = (f32[16,32,32]{2,1,0:T(8,128)S(1)}, f32[16,32,32]{2,1,0:T(8,128)}, u32[]{:S(2)}) copy-start(f32[16,32,32]{2,1,0:T(8,128)} %copy-done.50) | copy-start | bytes 196612
  1592.7 95.2 %copy-start.55 = (f32[16,32,32]{2,1,0:T(8,128)S(1)}, f32[16,32,32]{2,1,0:T(8,128)}, u32[]{:S(2)}) copy-start(f32[16,32,32]{2,1,0:T(8,128)} %copy-done.54) | copy-start | bytes 196612
  1592.7 95.2 %copy-start.146 = (f32[128]{0:T(128)S(1)}, f32[128]{0:T(128)}, u32[]{:S(2)}) copy-start(f32[128]{0:T(128)} %get-tuple-element.334) | copy-start | bytes 1540
  1688.1 75.7 %copy-start.119 = (f32[160,64]{0,1:T(8,128)S(1)}, f32[160,64]{0,1:T(8,128)}, u32[]{:S(2)}) copy-start(f32[160,64]{0,1:T(8,128)} %param.44) | copy-start | bytes 122884
  1688.1 75.7 %copy-start.134 = (f32[160,64]{0,1:T(8,128)S(1)}, f32[160,64]{0,1:T(8,128)}, u32[]{:S(2)}) copy-start(f32[160,64]{0,1:T(8,128)} %param.46) | copy-start | bytes 122884
  1688.2 75.7 %copy-start.135 = (f32[160,64]{0,1:T(8,128)S(1)}, f32[160,64]{0,1:T(8,128)}, u32[]{:S(2)}) copy-start(f32[160,64]{0,1:T(8,128)} %param.45) | copy-start | bytes 122884
  (196 other events, 2728.6 us)
Sparse Core Ops, SparseCore 0:
  361.1 24.2 all-reduce.68
  1075.9 24.2 all-reduce.70
  1372.1 108.0 all-reduce.72
  1483.7 40.3 all-reduce.74
  1526.2 77.4 reduce-scatter.5
  1605.8 72.5 reduce-scatter.7
  1688.0 74.8 reduce-scatter.9
where the time goes:
time: 1780 us; the launch traced here: 1770 us
  other arithmetic  677 us (38%)
  matrix products  356 us (20%)
  local copies, waits for them, and re-layouts  313 us (18%)
  blocking collectives  278 us (16%)
  waiting for transfers between devices  128 us (7%)
  between operations  19.2 us (1%)
    dot_general x8, matrix products, dense_back(): jnp.einsum('...e,de->...d', gradient, weight, preferred_element_type=jnp....  170 us
    unnamed x2, other arithmetic  149 us
    mul x3, other arithmetic, depthwise(): padded[:, row_shift:row_shift + cells_side, column_shift:column_shift + c...  106 us
    unnamed x490, local copies, waits for them, and re-layouts  98.5 us
    convert_element_type x1, other arithmetic, per_device(): hidden_low = hidden_grad.astype(jnp.bfloat16)  91.5 us
    psum x1, blocking collectives, per_device(): lax.psum((norm_grad, value_grad, hidden_filter_grad, live_count), 'dp')  78.1 us
    convert_element_type x1, other arithmetic, per_device(): activated_low = activated.astype(jnp.bfloat16)  77 us
    unnamed x9, waiting for transfers between devices  74.7 us
  transfers between devices with their start and end apart: 7, of which 4 were waited for; matrix products, arithmetic and copies ran while one was open for 12% of the time, Pallas kernels for 0%

commit v1 on v0

v1 whole, which is shorter than its diff:
```python
import math

import jax
import jax.numpy as jnp
import numpy as np
from jax import lax
from jax.experimental import pallas as pl
from jax.experimental.pallas import tpu as pltpu
from jax.sharding import PartitionSpec as P

BF = jnp.bfloat16
F32 = jnp.float32
EPSILON = 1e-06
HALF = 16
MASKED = -1e9
NN = (((1,), (0,)), ((), ()))
NT = (((1,), (1,)), ((), ()))
TN = (((0,), (0,)), ((), ()))


def mm(a, b, dims=NN):
    return lax.dot_general(a, b, dims, preferred_element_type=F32)


def block_of(a4, b4):
    return (a4 % 2) * 8 + (b4 % 2) * 4 + (a4 // 2) * 2 + b4 // 2


def place_of(block):
    return ((block >> 1) & 1) * 2 + (block >> 3), (block & 1) * 2 + ((block >> 2) & 1)


def order_matrix():
    perm = np.zeros((256, 256), np.float32)
    for block in range(16):
        a4, b4 = place_of(block)
        for ci in range(4):
            for ck in range(4):
                perm[block * 16 + ci * 4 + ck, (4 * ci + a4) * HALF + 4 * ck + b4] = 1
    return perm


def cell_shifts():
    places = []
    for ci in range(4):
        for ck in range(4):
            places.append((0, ci, ck, ci // 2, ck // 2))
    for ah in range(2):
        for bh in range(2):
            for ci in range(4):
                for ck in range(4):
                    places.append((1, 2 * ci + ah, 2 * ck + bh, ci // 2, ck // 2))
    index = {p[:3]: n for n, p in enumerate(places)}
    shifts = np.zeros((2, 9, 80, 80), np.float32)
    for n, (g, i, k, si, sk) in enumerate(places):
        for tap in range(9):
            other = index.get((g, i + tap // 3 - 1, k + tap % 3 - 1))
            if other is not None:
                shifts[0, tap, n, other] = 1
                if places[other][3:] == (si, sk):
                    shifts[1, tap, n, other] = 1
    return shifts.reshape(2, 720, 80)


def score_bias():
    rows = np.array([(n % 16) for _ in range(2) for n in list(range(16)) + list(range(64))])
    cols = np.arange(256) % 16

    def image(n):
        return (n // 8) * 2 + (n % 4) // 2

    return np.where(image(rows)[:, None] == image(cols)[None, :], 0.0, MASKED).astype(np.float32)


def shift_masks():
    masks = np.zeros((2, 4, 16, 128), np.float32)
    for fine in range(2):
        for ci in range(4):
            for ck in range(4):
                row = ci * 4 + ck
                for n, (d, e) in enumerate(((1, 0), (-1, 0), (0, 1), (0, -1))):
                    ni, nk = ci + d, ck + e
                    ok = 0 <= ni < 4 and 0 <= nk < 4
                    if fine:
                        ok = ok and ni // 2 == ci // 2 and nk // 2 == ck // 2
                    masks[fine, n, row] = ok
    return masks


def normalise(x):
    centred = x - jnp.mean(x, -1, keepdims=True)
    scale = lax.rsqrt(jnp.mean(centred * centred, -1, keepdims=True) + EPSILON)
    return centred * scale, scale


def normalise_back(grad, unit, scale):
    return scale * (
        grad
        - jnp.mean(grad, -1, keepdims=True)
        - unit * jnp.mean(grad * unit, -1, keepdims=True)
    )


def gelu_pair(h):
    density = jnp.exp(-0.5 * (h * h))
    t = 1.0 / (1.0 + (0.3275911 * math.sqrt(0.5)) * jnp.abs(h))
    poly = 1.061405429 * 0.5
    for c in (-1.453152027, 1.421413741, -0.284496736, 0.254829592):
        poly = poly * t + c * 0.5
    tail = poly * t * density
    below = jnp.where(h >= 0, 1.0 - tail, tail)
    return h * below, below + h * density * (1.0 / math.sqrt(2 * math.pi))


def block_kernel(
    info,
    tokens,
    cotangent,
    entry,
    mixing_t,
    expand,
    shrink_t,
    reduce_w,
    norms,
    value_filter,
    hidden_filter,
    perm,
    perm_t,
    shifts,
    bias,
    edge,
    out,
    input_grad,
    d_entry,
    d_mixing_t,
    d_expand,
    d_shrink_t,
    d_reduce,
    d_norm,
    d_value,
    d_hidden,
    conv_w,
    key_value_w,
    im2col,
    im2col_t,
    g_low,
    m_sum,
    folds,
    d_key_value,
    probs,
    normed_s,
    queries_s,
    *,
    steps,
):
    step = pl.program_id(0)
    ff = expand.shape[1]
    lane = lax.broadcasted_iota(jnp.int32, (128, 128), 1)
    first_lanes = lane % 64 < 32

    @pl.when(step == 0)
    def prepare():
        for tap in range(9):
            gain = hidden_filter[tap : tap + 1, :]
            if tap == 4:
                gain = gain + 1.0
            conv_w[tap * 128 : (tap + 1) * 128, :] = (expand[...].astype(F32) * gain).astype(BF)
        for g in range(2):
            w = entry[1 + g].astype(F32)
            if g == 0:
                keys, vals = w, pltpu.roll(w, 96, 1)
                keep = first_lanes
            else:
                keys, vals = pltpu.roll(w, 32, 1), w
                keep = jnp.logical_not(first_lanes)
            key_value_w[g, :, :128] = jnp.where(keep, keys, 0.0).astype(BF)
            key_value_w[g, :, 128:] = jnp.where(keep, vals, 0.0).astype(BF)
        for ref in (d_entry, d_mixing_t, d_shrink_t, d_reduce, d_norm, d_value, m_sum, d_key_value):
            ref[...] = jnp.zeros_like(ref)

    fine = info[0, step]
    alive = info[1, step]
    fine_f = fine.astype(F32)

    def ordered(ref):
        parts = [
            ref[0, a * 16 : a * 16 + 16, b * 16 : b * 16 + 16, :].reshape(256, 128)
            for a in range(2)
            for b in range(2)
        ]
        rows = mm(perm[...], jnp.concatenate(parts, 1))
        return jnp.stack(
            [rows[:, q * 128 : q * 128 + 128].reshape(16, 16, 128) for q in range(4)], 1
        ).reshape(1024, 128)

    def restore(value, ref):
        blocks = value.reshape(16, 4, 16, 128)
        rows = mm(
            perm_t[...],
            jnp.concatenate([blocks[:, q].reshape(256, 128) for q in range(4)], 1),
        ).astype(BF)
        for q in range(4):
            a, b = q // 2, q % 2
            ref[0, a * 16 : a * 16 + 16, b * 16 : b * 16 + 16, :] = rows[
                :, q * 128 : q * 128 + 128
            ].reshape(16, 16, 128)

    def of_quadrant(value, q, blocks):
        return value.reshape(blocks, 4, 16, 128)[:, q].reshape(blocks * 16, 128)

    def of_quadrants(parts, blocks):
        return jnp.stack([p.reshape(blocks, 16, 128) for p in parts], 1).reshape(
            blocks * 64, 128
        )

    def gain(n):
        return norms[0, n : n + 1, :]

    def shift_by(n):
        return norms[1, n : n + 1, :]

    def add_norm(n, grad, unit):
        d_norm[n : n + 1, :] += jnp.sum(grad * unit, 0, keepdims=True)
        d_norm[4 + n : 5 + n, :] += jnp.sum(grad, 0, keepdims=True)

    x = ordered(tokens)
    unit1, scale1 = normalise(x)
    normed = (unit1 * gain(0) + shift_by(0)).astype(BF)
    normed_s[...] = normed
    queries_s[...] = mm(normed, entry[0]).astype(BF)
    patches = (
        jnp.concatenate(
            [
                normed_s[block_of(t // 4, t % 4) * 64 : block_of(t // 4, t % 4) * 64 + 64, :]
                for t in range(16)
            ],
            1,
        ),
        jnp.concatenate([normed_s[t * 256 : t * 256 + 256, :] for t in range(4)], 1),
    )
    rows_of = (slice(0, 2048), slice(2048, 2560))
    cell_saved = []
    keys, values = [], []
    for g in range(2):
        reduced = mm(patches[g], reduce_w[rows_of[g], :])
        unit, scale = normalise(reduced)
        act, slope = gelu_pair(unit * gain(1 + g) + shift_by(1 + g))
        cell_low = act.astype(BF)
        pair = mm(cell_low, key_value_w[g])
        keys.append(pair[:, :128].astype(BF))
        values.append(pair[:, 128:])
        cell_saved.append((unit, scale, slope, cell_low))
    keys_all = [
        jnp.concatenate([keys[0][q * 16 : q * 16 + 16], of_quadrant(keys[1], q, 4)], 0)
        for q in range(4)
    ]
    values_all = jnp.concatenate(
        [
            jnp.concatenate([values[0][q * 16 : q * 16 + 16], of_quadrant(values[1], q, 4)], 0)
            for q in range(4)
        ],
        1,
    )
    moves = shifts[pl.ds(fine, 1)][0]
    high = values_all.astype(BF)
    rest = (values_all - high.astype(F32)).astype(BF)
    moved = mm(moves, high) + mm(moves, rest)
    taps4 = jnp.concatenate([value_filter[...]] * 4, 1)
    enhanced = values_all
    for tap in range(9):
        enhanced = enhanced + moved[tap * 80 : tap * 80 + 80] * taps4[tap : tap + 1]
    enhanced = enhanced.astype(BF)
    lane80 = lax.broadcasted_iota(jnp.int32, (80, 128), 1)
    zero80 = jnp.zeros((80, 128), BF)

    def both_heads(rows):
        return jnp.concatenate(
            [jnp.where(lane80 < 64, rows, zero80), jnp.where(lane80 < 64, zero80, rows)], 0
        )

    segments = ((0, 16), (16, 80), (80, 96), (96, 160))
    queries = queries_s[...]
    query_q = [of_quadrant(queries, q, 16) for q in range(4)]
    keys_q = [both_heads(keys_all[q]) for q in range(4)]
    enhanced_q = [both_heads(enhanced[:, q * 128 : q * 128 + 128]) for q in range(4)]
    mixed_parts = []
    scaling = 32**-0.5
    for q in range(4):
        scores = mm(keys_q[q], query_q[q], NT) * scaling + fine_f * bias[...]
        weights = []
        for lo, hi in segments:
            part = scores[lo:hi]
            part = jnp.exp(part - jnp.max(part, 0, keepdims=True))
            weights.append(part / jnp.sum(part, 0, keepdims=True))
        weights = jnp.concatenate(weights, 0)
        probs[q] = weights
        mixed_parts.append(mm(weights.astype(BF), enhanced_q[q], TN))
    mixed = of_quadrants(mixed_parts, 16).astype(BF)
    middle = x + mm(mixed, mixing_t[...], NT)
    unit2, scale2 = normalise(middle)
    second = unit2 * gain(3) + shift_by(3)
    second_low = second.astype(BF)
    second_f = second_low.astype(F32)

    def move(value, rows, columns):
        size = value.shape[0]
        if rows:
            n = 0 if rows > 0 else 1
            value = pltpu.roll(value, (-4 * rows) % size, 0)
            value = (
                value.reshape(size // 16, 16, 128) * edge[pl.ds(fine, 1), n : n + 1][0]
            ).reshape(size, 128)
        if columns:
            n = 2 if columns > 0 else 3
            value = pltpu.roll(value, (-columns) % size, 0)
            value = (
                value.reshape(size // 16, 16, 128) * edge[pl.ds(fine, 1), n : n + 1][0]
            ).reshape(size, 128)
        return value

    def wrap(a4, d):
        return (a4 + d) % 4, (a4 + d) // 4

    moved_blocks = {}
    for block in range(16):
        a4, b4 = place_of(block)
        for tap in range(9):
            na, wa = wrap(a4, tap // 3 - 1)
            nb, wb = wrap(b4, tap % 3 - 1)
            source = block_of(na, nb)
            key = (source, wa, wb)
            if key not in moved_blocks:
                rows = slice(source * 64, source * 64 + 64)
                if wa or wb:
                    moved_blocks[key] = move(second_f[rows], wa, wb).astype(BF)
                else:
                    moved_blocks[key] = second_low[rows]
            im2col[block * 64 : block * 64 + 64, tap * 128 : tap * 128 + 128] = moved_blocks[key]
    for tap in range(9):
        im2col_t[tap * 128 : tap * 128 + 128, :] = im2col[:, tap * 128 : tap * 128 + 128].T

    row16 = lax.broadcasted_iota(jnp.int32, (16, 128), 0)
    within = (row16 // 8) * 4 + (row16 % 4) // 2
    live = jnp.stack(
        [
            jnp.where(
                jnp.where(fine == 1, within + (q // 2) * 8 + (q % 2) * 2, q) < alive, 1.0, 0.0
            )
            for q in range(4)
        ],
        0,
    )
    upstream = (ordered(cotangent).reshape(16, 4, 16, 128) * live[None]).reshape(1024, 128)
    up_low = upstream.astype(BF)
    up_t = up_low.T

    feed = jnp.zeros((1024, 128), F32)
    wide = 256
    for c in range(0, ff, wide):
        cols = slice(c, c + wide)
        hidden = mm(im2col[...], conv_w[:, cols])
        act, slope = gelu_pair(hidden)
        act = act.astype(BF)
        grad = mm(up_low, shrink_t[:, cols]) * slope
        grad = grad.astype(BF)
        g_low[:, cols] = grad
        feed = feed + mm(act, shrink_t[:, cols], NT)
        d_shrink_t[:, cols] += mm(up_t, act)
        m_sum[:, cols] += mm(im2col_t[...], grad)
    restore((middle + feed).astype(BF), out)

    for t in range(0, 9, 2):
        rows = slice(t * 128, min(t + 2, 9) * 128)
        folds[:, rows] = mm(g_low[...], conv_w[rows, :], NT)
    sums = {}
    for block in range(16):
        a4, b4 = place_of(block)
        for tap in range(9):
            na, wa = wrap(a4, tap // 3 - 1)
            nb, wb = wrap(b4, tap % 3 - 1)
            key = (block_of(na, nb), wa, wb)
            sums.setdefault(key, []).append((block, tap))
    second_parts = []
    for block in range(16):
        total = None
        for (source, wa, wb), terms in sums.items():
            if source != block:
                continue
            part = None
            for other, tap in terms:
                term = folds[other * 64 : other * 64 + 64, tap * 128 : tap * 128 + 128]
                part = term if part is None else part + term
            if wa or wb:
                part = move(part, -wa, -wb)
            total = part if total is None else total + part
        second_parts.append(total)
    second_grad = jnp.concatenate(second_parts, 0)
    add_norm(3, second_grad, unit2)
    middle_grad = upstream + normalise_back(second_grad * gain(3), unit2, scale2)
    middle_low = middle_grad.astype(BF)
    d_mixing_t[...] += mm(middle_low, mixed, TN)
    mixed_grad = mm(middle_low, mixing_t[...]).astype(BF)

    query_parts, key_parts, enhanced_parts = [], [], []
    for q in range(4):
        out_grad = of_quadrant(mixed_grad, q, 16)
        weights = probs[q]
        prob_grad = mm(enhanced_q[q], out_grad, NT)
        product = weights * prob_grad
        score_grad = []
        for lo, hi in segments:
            score_grad.append(
                product[lo:hi] - weights[lo:hi] * jnp.sum(product[lo:hi], 0, keepdims=True)
            )
        score_low = (scaling * jnp.concatenate(score_grad, 0)).astype(BF)
        query_parts.append(mm(score_low, keys_q[q], TN))
        key_full = mm(score_low, query_q[q])
        enhanced_full = mm(weights.astype(BF), out_grad)
        key_parts.append(jnp.where(lane80 < 64, key_full[:80], key_full[80:]).astype(BF))
        enhanced_parts.append(
            jnp.where(lane80 < 64, enhanced_full[:80], enhanced_full[80:]).astype(BF)
        )
    query_low = of_quadrants(query_parts, 16).astype(BF)
    enhanced_grad = jnp.concatenate(enhanced_parts, 1)
    moved = mm(moves, enhanced_grad)
    value_grad = enhanced_grad.astype(F32)
    for tap in range(9):
        part = moved[(8 - tap) * 80 : (8 - tap) * 80 + 80]
        value_grad = value_grad + part * taps4[tap : tap + 1]
        row = jnp.sum(part * values_all, 0, keepdims=True)
        d_value[tap : tap + 1, :] += (
            row[:, :128] + row[:, 128:256] + row[:, 256:384] + row[:, 384:]
        )
    value_grad = value_grad.astype(BF)
    value_parts = [value_grad[:, q * 128 : q * 128 + 128] for q in range(4)]
    normed = normed_s[...]
    normed_grad = mm(query_low, entry[0], NT)
    d_entry[0] += mm(normed, query_low, TN)
    for g in range(2):
        if g == 0:
            sides = [jnp.concatenate([p[:16] for p in parts], 0) for parts in (key_parts, value_parts)]
        else:
            sides = [of_quadrants([p[16:] for p in parts], 4) for parts in (key_parts, value_parts)]
        pair = jnp.concatenate(sides, 1)
        unit, scale, slope, cell_low = cell_saved[g]
        d_key_value[g] += mm(cell_low, pair, TN)
        cell_grad = mm(pair, key_value_w[g], NT) * slope
        add_norm(1 + g, cell_grad, unit)
        reduced_low = normalise_back(cell_grad * gain(1 + g), unit, scale).astype(BF)
        d_reduce[rows_of[g], :] += mm(patches[g], reduced_low, TN)
        back = mm(reduced_low, reduce_w[rows_of[g], :], NT)
        if g == 0:
            order = [place_of(block) for block in range(16)]
            order = [a4 * 4 + b4 for a4, b4 in order]
        else:
            order = range(4)
        normed_grad = normed_grad + jnp.concatenate(
            [back[:, t * 128 : t * 128 + 128] for t in order], 0
        )
    add_norm(0, normed_grad, unit1)
    raw = middle_grad + normalise_back(normed_grad * gain(0), unit1, scale1)
    restore(raw.astype(BF), input_grad)

    @pl.when(step == steps - 1)
    def finish():
        weight = expand[...].astype(F32)
        total = None
        for tap in range(9):
            part = m_sum[tap * 128 : tap * 128 + 128, :]
            factor = hidden_filter[tap : tap + 1, :]
            if tap == 4:
                factor = factor + 1.0
            d_hidden[tap : tap + 1, :] = jnp.sum(part * weight, 0, keepdims=True)
            total = part * factor if total is None else total + part * factor
        d_expand[...] = total
        d_entry[1] = jnp.where(
            first_lanes, d_key_value[0, :, :128], pltpu.roll(d_key_value[0, :, 128:], 32, 1)
        )
        d_entry[2] = jnp.where(
            first_lanes, pltpu.roll(d_key_value[1, :, :128], 96, 1), d_key_value[1, :, 128:]
        )


def run_block(
    info,
    offset,
    tokens,
    cotangent,
    entry,
    mixing_t,
    expand,
    shrink_t,
    reduce_w,
    norms,
    value_filter,
    hidden_filter,
):
    steps = info.shape[1]
    ff = expand.shape[1]
    consts = [
        jnp.asarray(order_matrix(), BF),
        jnp.asarray(order_matrix().T, BF),
        jnp.asarray(cell_shifts(), BF),
        jnp.asarray(score_bias(), F32),
        jnp.asarray(shift_masks(), F32),
    ]
    whole = [entry, mixing_t, expand, shrink_t, reduce_w, norms, value_filter, hidden_filter] + consts

    def all_of(a):
        return pl.BlockSpec(a.shape, lambda i, *_: (0,) * a.ndim)

    grid_in = pl.BlockSpec((1, 32, 32, 128), lambda i, info, off: (off[0] + i, 0, 0, 0))
    grid_out = pl.BlockSpec((1, 32, 32, 128), lambda i, *_: (i, 0, 0, 0))
    sums = [(3, 128, 128), (128, 128), (128, ff), (128, ff), (2560, 128), (8, 128), (9, 128), (9, ff)]
    out_shape = [
        jax.ShapeDtypeStruct((steps, 32, 32, 128), BF),
        jax.ShapeDtypeStruct((steps, 32, 32, 128), BF),
    ] + [jax.ShapeDtypeStruct(s, F32) for s in sums]

    def kernel(info, off, *refs):
        block_kernel(info, *refs, steps=steps)

    return pl.pallas_call(
        kernel,
        out_shape=out_shape,
        grid_spec=pltpu.PrefetchScalarGridSpec(
            num_scalar_prefetch=2,
            grid=(steps,),
            in_specs=[grid_in, grid_in] + [all_of(a) for a in whole],
            out_specs=[grid_out, grid_out]
            + [pl.BlockSpec(s, lambda i, *_, n=len(s): (0,) * n) for s in sums],
            scratch_shapes=[
                pltpu.VMEM((1152, ff), BF),
                pltpu.VMEM((2, 128, 256), BF),
                pltpu.VMEM((1024, 1152), BF),
                pltpu.VMEM((1152, 1024), BF),
                pltpu.VMEM((1024, ff), BF),
                pltpu.VMEM((1152, ff), F32),
                pltpu.VMEM((1024, 1152), F32),
                pltpu.VMEM((2, 128, 256), F32),
                pltpu.VMEM((4, 160, 256), F32),
                pltpu.VMEM((1024, 128), BF),
                pltpu.VMEM((1024, 128), BF),
            ],
        ),
        compiler_params=pltpu.CompilerParams(
            dimension_semantics=("arbitrary",), vmem_limit_bytes=60 * 1024 * 1024
        ),
        name="block",
    )(info, offset, tokens, cotangent, *whole)


def advance(weight, moment, average, gradient, step_rate, weight_decay):
    gradient = gradient + weight_decay * weight
    moment = 0.9 * moment + gradient
    weight = weight - step_rate * (gradient + 0.9 * moment)
    return (moment, weight, 0.8 * average + 0.2 * weight)


def per_device(
    tokens,
    cotangent,
    resolution,
    live_images,
    entry_weight,
    entry_momentum,
    entry_average,
    mixing_weight,
    mixing_momentum,
    mixing_average,
    expand_weight,
    expand_momentum,
    expand_average,
    shrink_weight,
    shrink_momentum,
    shrink_average,
    reduce_weight,
    reduce_momentum,
    reduce_average,
    norm_params,
    norm_momentum,
    norm_average,
    value_filter,
    value_momentum,
    value_average,
    hidden_filter,
    hidden_momentum,
    hidden_average,
):
    devices = lax.axis_size("dp")
    head = lax.axis_index("head")
    swap = [(0, 1), (1, 0)]
    grids = tokens.shape[0]
    half = grids // 2
    ff = 2 * expand_weight.shape[1]

    def pair(own, axis):
        other = lax.ppermute(own, "head", swap)
        return jnp.where(
            head == 0, jnp.concatenate([own, other], axis), jnp.concatenate([other, own], axis)
        )

    shards = (entry_weight, mixing_weight.T, expand_weight, shrink_weight.T, reduce_weight)
    shapes = [s.shape for s in shards]
    sizes = [s.size for s in shards]
    starts = [sum(sizes[:n]) for n in range(6)]
    packed = jnp.concatenate([s.astype(BF).reshape(-1) for s in shards]).reshape(-1, 128)
    gathered = lax.all_gather(packed, ("dp", "head")).reshape(devices, 2, -1)
    parts = [
        gathered[:, :, starts[n] : starts[n + 1]].reshape((devices, 2) + shapes[n]) for n in range(5)
    ]
    entry = parts[0].transpose(2, 0, 3, 1, 4).reshape(3, 128, 128)
    mixing_t, expand, shrink_t, reduce_w = [
        p.transpose(0, 2, 1, 3).reshape(devices * p.shape[2], -1) for p in parts[1:]
    ]
    values_here = value_filter.transpose(1, 0, 2).reshape(9, 64)
    filters = pair(jnp.concatenate([values_here, hidden_filter], 1)[None], 0)
    values_full = filters[:, :, :64].transpose(1, 0, 2).reshape(9, 128)
    hidden_full = filters[:, :, 64:].transpose(1, 0, 2).reshape(9, ff)

    fine = (resolution == 8).astype(jnp.int32)
    info = lax.dynamic_slice_in_dim(jnp.stack([fine, live_images]), head * half, half, 1)
    offset = (head * half).reshape(1).astype(jnp.int32)
    (
        out_half,
        input_half,
        d_entry,
        d_mixing_t,
        d_expand,
        d_shrink_t,
        d_reduce,
        d_norm,
        d_value,
        d_hidden,
    ) = run_block(
        info,
        offset,
        tokens,
        cotangent,
        entry,
        mixing_t,
        expand,
        shrink_t,
        reduce_w,
        norm_params,
        values_full,
        hidden_full,
    )
    live_here = jnp.sum(info[1] * jnp.where(info[0] == 1, 64, 256)).astype(F32)

    small = jnp.concatenate(
        [d_norm.reshape(-1), d_value.reshape(-1), d_hidden.reshape(-1), live_here.reshape(1)]
    )
    small = lax.psum(small, ("dp", "head"))
    norm_grad = small[:1024].reshape(2, 4, 128)
    value_grad = small[1024 : 1024 + 1152].reshape(9, 2, 2, 32)
    value_grad = lax.dynamic_index_in_dim(value_grad, head, 1, False).transpose(1, 0, 2)
    hidden_grad = small[2176 : 2176 + 9 * ff].reshape(9, 2, ff // 2)
    hidden_grad = lax.dynamic_index_in_dim(hidden_grad, head, 1, False)
    live_total = small[-1]

    d_entry = d_entry.reshape(3, devices, -1, 2, 64).transpose(3, 1, 0, 2, 4)
    d_rest = [
        d.reshape(devices, -1, 2, d.shape[1] // 2).transpose(2, 0, 1, 3)
        for d in (d_mixing_t, d_expand, d_shrink_t, d_reduce)
    ]
    grads = jnp.concatenate([d.reshape(2, devices, -1) for d in [d_entry] + d_rest], 2)
    mine = lax.dynamic_index_in_dim(grads, head, 0, False)
    theirs = lax.dynamic_index_in_dim(grads, 1 - head, 0, False)
    mine = mine + lax.ppermute(theirs, "head", swap)
    mine = lax.psum_scatter(mine.reshape(devices, -1, 128), "dp", scatter_dimension=0)
    mine = mine.reshape(-1)
    entry_grad, mixing_grad, expand_grad, shrink_grad, reduce_grad = [
        mine[starts[n] : starts[n + 1]].reshape(shapes[n]) for n in range(5)
    ]
    mixing_grad, shrink_grad = mixing_grad.T, shrink_grad.T

    output = pair(out_half, 0)
    input_raw = pair(input_half, 0)
    tokens_all = devices * grids * tokens.shape[1] * tokens.shape[2]
    factor = tokens_all / live_total
    rate_unit = tokens_all ** (-0.5)
    input_grad = factor * input_raw.astype(F32)
    results = []
    for weight, moment, average, grad, rate, decay in (
        (entry_weight, entry_momentum, entry_average, entry_grad, 0.3, 0.05),
        (mixing_weight, mixing_momentum, mixing_average, mixing_grad, 0.12, 0.05),
        (expand_weight, expand_momentum, expand_average, expand_grad, 0.12, 0.05),
        (shrink_weight, shrink_momentum, shrink_average, shrink_grad, 0.03, 0.05),
        (reduce_weight, reduce_momentum, reduce_average, reduce_grad, 0.1, 0.05),
        (norm_params, norm_momentum, norm_average, norm_grad, 0.2, 0.0),
        (value_filter, value_momentum, value_average, value_grad, 0.4, 0.05),
        (hidden_filter, hidden_momentum, hidden_average, hidden_grad, 0.5, 0.05),
    ):
        results.extend(advance(weight, moment, average, factor * grad, rate * rate_unit, decay))
    return (output, input_grad, *results)


def solution(mesh):
    in_specs = (
        P("dp", None, None, None),
        P("dp", None, None, None),
        P("dp"),
        P("dp"),
        P(None, "dp", "head"),
        P(None, "dp", "head"),
        P(None, "dp", "head"),
        P("head", "dp"),
        P("head", "dp"),
        P("head", "dp"),
        P("dp", "head"),
        P("dp", "head"),
        P("dp", "head"),
        P("head", "dp"),
        P("head", "dp"),
        P("head", "dp"),
        P("dp", "head"),
        P("dp", "head"),
        P("dp", "head"),
        P(),
        P(),
        P(),
        P(None, None, "head"),
        P(None, None, "head"),
        P(None, None, "head"),
        P(None, "head"),
        P(None, "head"),
        P(None, "head"),
    )
    out_specs = (
        P("dp", None, None, None),
        P("dp", None, None, None),
        P(None, "dp", "head"),
        P(None, "dp", "head"),
        P(None, "dp", "head"),
        P("head", "dp"),
        P("head", "dp"),
        P("head", "dp"),
        P("dp", "head"),
        P("dp", "head"),
        P("dp", "head"),
        P("head", "dp"),
        P("head", "dp"),
        P("head", "dp"),
        P("dp", "head"),
        P("dp", "head"),
        P("dp", "head"),
        P(),
        P(),
        P(),
        P(None, None, "head"),
        P(None, None, "head"),
        P(None, None, "head"),
        P(None, "head"),
        P(None, "head"),
        P(None, "head"),
    )
    return jax.shard_map(
        per_device, mesh=mesh, in_specs=in_specs, out_specs=out_specs, check_vma=False
    )
```

time: 1780 us -> 366 us (0.21)
  other arithmetic: 677 us -> 26 us
  matrix products: 356 us -> 0 us
  local copies, waits for them, and re-layouts: 313 us -> 44.6 us
  blocking collectives: 278 us -> 39.9 us
  Pallas kernels: 0 us -> 161 us
  waiting for transfers between devices: 128 us -> 75.9 us
    dot_general x35 -> x0, matrix products: 345 us -> none  [the longest x8 170 us: dense_back(): jnp.einsum('...e,de->...d', gradient, weight, preferred_element_type=jnp....]
    convert_element_type x18 -> x3, other arithmetic: 214 us -> 2.24 us  [per_device(): s.astype(BF).reshape(-1)]
    all_gather x6 -> x0, blocking collectives: 200 us -> none  [the longest x1 42.9 us: per_device(): lax.all_gather(entry_weight.astype(jnp.bfloat16), 'dp', axis=1, tiled=True)]
    pallas_call x0 -> x1, Pallas kernels: none -> 161 us  [run_block(): pl.pallas_call(kernel, out_shape=out_shape, grid_spec=pltpu.PrefetchScala...]
    unnamed x2 -> x4, other arithmetic: 149 us -> 2.89 us
    mul x8 -> x7, other arithmetic: 135 us -> 8.43 us  [the longest x1 5.5 us: per_device(): input_grad = factor * input_raw.astype(F32)]
    reduce_sum x19 -> x1, other arithmetic: 95.6 us -> 0.63 us  [per_device(): live_here = jnp.sum(info[1] * jnp.where(info[0] == 1, 64, 256)).astype(F32)]
    unnamed x490 -> x91, local copies, waits for them, and re-layouts: 98.5 us -> 10.8 us
  transfers between devices with their start and end apart: 7 -> 6, of which waited for: 4 -> 3; matrix products, arithmetic and copies ran while one was open for 12% -> 6% of each run, Pallas kernels for 0% -> 0%
where the time goes in v1:
time: 366 us; the launch traced here: 365 us
  Pallas kernels  161 us (44%)
  waiting for transfers between devices  75.9 us (21%)
  local copies, waits for them, and re-layouts  44.6 us (12%)
  blocking collectives  39.9 us (11%)
  other arithmetic  26 us (7%)
  between operations  16.1 us (4%)
    pallas_call x1, Pallas kernels, run_block(): pl.pallas_call(kernel, out_shape=out_shape, grid_spec=pltpu.PrefetchScala...  161 us
    all_gather x1, waiting for transfers between devices, per_device(): gathered = lax.all_gather(packed, ('dp', 'head')).reshape(devices, 2, -1)  51.5 us
    psum x1, blocking collectives, per_device(): small = lax.psum(small, ('dp', 'head'))  39.9 us
    reduce_scatter x1, waiting for transfers between devices, per_device(): lax.psum_scatter(mine.reshape(devices, -1, 128), 'dp', scatter_dimension=0)  21.4 us
    unnamed x91, local copies, waits for them, and re-layouts  10.8 us
  transfers between devices with their start and end apart: 6, of which 3 were waited for; matrix products, arithmetic and copies ran while one was open for 6% of the time, Pallas kernels for 0%

profile of v1, /device:TPU:0, one launch (start us, length us, event | category | flops | bytes accessed | tf_op | source)
XLA Modules:
  0.0 364.8 jit_solution(6469303436873233281)
XLA Ops:
  7.3 0.7 convert_element_type.28
  8.1 0.7 convert_bitcast_fusion.2
  8.8 0.7 convert_bitcast_fusion.1
  9.6 0.7 convert_bitcast_fusion
  10.3 0.8 convert_element_type.34
  12.6 0.8 reshape.220
  13.4 0.8 maximum_bitcast_fusion
  14.7 0.7 fusion.2
  15.3 0.7 pad_add_fusion
  16.0 0.6 constant_dynamic-slice_fusion.info
  16.8 0.6 copy.138
  17.4 0.7 reshape.221.refs_8_
  18.1 51.5 %all-gather.2.cloned.1.call-done = bf16[32,160,128]{2,1,0:T(8,128)(2,1)} async-done(((bf16[1,160,128]{2,1,0:T(8,128)(2,1)}), bf16[32,160,128]{2,1,0:T(8,128)(2,1)}) %all-gather.2.cloned.1.call-update) | async-done | bytes 1310736 | tf_op jit(solution)/shard_map/all_gather | solution.py:608
  69.6 3.3 reshape.209
  73.8 0.9 reshape.216
  74.7 0.9 reshape.214
  75.7 1.3 reshape.218
  77.1 2.4 copy.131
  79.5 3.4 reshape.241.refs_6_
  83.3 0.8 reshape.211.refs_2_
  84.3 0.7 reshape.213.refs_3_
  85.0 161.0 %block.1 = (bf16[8,32,32,128]{3,2,1,0:T(8,128)(2,1)}, bf16[8,32,32,128]{3,2,1,0:T(8,128)(2,1)}, f32[3,128,128]{2,1,0:T(8,128)}, f32[128,128]{1,0:T(8,128)}, f32[...) custom-call(s32[2,8]{1,0:T(2,128)} %constant_dynamic-slice_fusion.in, ...), custom_call_target="tpu_custom_call" | custom-call | tf_op jit(solution)/shard_map/block/pallas_call | solution.py:523
  246.1 1.3 reshape.227
  247.5 0.7 constant_dynamic-update-slice_fusion.2
  248.2 1.0 reshape.229
  249.3 1.3 reshape.242
  251.5 2.5 reshape.235
  253.9 2.3 copy.123
  256.3 1.9 reshape.236
  258.8 2.1 copy_dynamic-update-slice_fusion.1
  260.9 1.1 copy_dynamic-update-slice_fusion
  262.0 1.1 constant_dynamic-update-slice_fusion
  263.2 2.6 dynamic-slice_bitcast_fusion
  266.3 2.9 collective-permute-done.3
  269.2 1.4 fusion
  270.9 1.3 copy.139
  274.6 39.9 %psum.7 = f32[11393]{0:T(1024)S(1)} all-reduce(f32[11393]{0:T(1024)S(1)} %pad_maximum_fusion), channel_id=1, replica_groups=mesh['dp'=16,'head'=2] {'dp','head'}, use_global_device_ids=true, to_apply=%region_1.2 | all-reduce | flops 11393 | bytes 91144 | tf_op jit(solution)/shard_map/psum | solution.py:654
  317.1 0.7 multiply_add_fusion.3
  317.8 5.3 %maximum_select_fusion = bf16[16,32,32,128]{3,2,1,0:T(8,128)(2,1)} fusion(bf16[8,32,32,128]{3,2,1,0:T(8,128)(2,1)} %collective-permute-done.1, bf16[8,32,32,128]{3,2,1,0:T(8,128)(2,1)} %get-tuple-element.36, pred[]{:T(512)S(6)} %eq.12), kind=kLoop, calls=%fused_computation.1 | loop fusion | flops 6291456 | bytes 8388609 | tf_op jit(solution)/shard_map/jit(_where)/select_n | solution.py:599
  323.2 5.5 %convert_multiply_fusion = f32[16,32,32,128]{3,2,1,0:T(8,128)} fusion(bf16[8,32,32,128]{3,2,1,0:T(8,128)(2,1)} %collective-permute-done.2, bf16[8,32,32,128]{3,2,1,0:T(8,128)(2,1)S(1)} %copy-done.3, f32[]{:T(128)} %bitcast.20, pred[]{:T(512)S(6)} %eq.12), kind=kLoop, calls=%fused_computation | loop fusion | flops 10485760 | bytes 12582917 | tf_op jit(solution)/shard_map/mul | solution.py:683
  328.7 21.4 %reduce-scatter.2.cloned.1.call-done = f32[1,160,128]{2,1,0:T(8,128)} async-done(((f32[16,160,128]{2,1,0:T(8,128)}), f32[1,160,128]{2,1,0:T(8,128)}) %reduce-scatter.2.cloned.1.call-update) | async-done | bytes 81936 | tf_op jit(solution)/shard_map/reduce_scatter | solution.py:671
  350.1 0.8 slice_multiply_fusion
  351.0 0.7 copy.128
  351.7 0.7 copy.129
  352.4 0.7 copy.130
  353.2 0.7 slice_multiply_fusion.1
  353.9 0.7 slice_multiply_fusion.5
  354.7 0.7 slice_multiply_fusion.3
  (146 shorter events, 12.6 us)
Async XLA Ops:
  7.2 62.4 %all-gather.2.cloned.1.call-start = ((), (), s32[]{:S(2)}) async-start(), calls=%async_computation.1 | async-start | bytes 1351680 | tf_op jit(solution)/shard_map/all_gather | solution.py:608
  11.9 0.6 copy-start.15
  12.5 337.6 %reduce-scatter.2.cloned.1.call-start = ((), (), s32[]{:S(2)}) async-start(), calls=%async_computation.2 | async-start | bytes 1392640 | tf_op jit(solution)/shard_map/reduce_scatter | solution.py:671
  14.2 2.4 collective-permute-start
  72.9 4.2 %copy-start = (bf16[16,2,20480]{2,1,0:T(2,128)(2,1)}, bf16[16,2,20480]{2,1,0:T(2,128)(2,1)S(1)}, u32[]{:S(2)}) copy-start(bf16[16,2,20480]{2,1,0:T(2,128)(2,1)S(1)} %reshape.209) | copy-start | bytes 3932164
  77.1 5.8 %slice-start = ((bf16[16,2,20480]{2,1,0:T(2,128)(2,1)}), bf16[16,2,1536]{2,1,0:T(2,128)(2,1)S(1)}, s32[]{:S(2)}) async-start(bf16[16,2,20480]{2,1,0:T(2,128)(2,1)} %copy-done), calls=%async_computation.3 | async-start | bytes 196608 | tf_op jit(solution)/shard_map/slice | solution.py:610
  77.1 7.0 %slice-start.1 = ((bf16[16,2,20480]{2,1,0:T(2,128)(2,1)}), bf16[16,2,512]{2,1,0:T(2,128)(2,1)S(1)}, s32[]{:S(2)}) async-start(bf16[16,2,20480]{2,1,0:T(2,128)(2,1)} %copy-done), calls=%async_computation.4 | async-start | bytes 65536 | tf_op jit(solution)/shard_map/slice | solution.py:610
  246.0 3.3 copy-start.6
  246.0 4.6 %copy-start.5 = (f32[128,1024]{1,0:T(8,128)S(1)}, f32[128,1024]{1,0:T(8,128)}, u32[]{:S(2)}) copy-start(f32[128,1024]{1,0:T(8,128)} %get-tuple-element.44) | copy-start | bytes 1572868
  246.0 5.0 %copy-start.4 = (f32[2560,128]{1,0:T(8,128)S(1)}, f32[2560,128]{1,0:T(8,128)}, u32[]{:S(2)}) copy-start(f32[2560,128]{1,0:T(8,128)} %get-tuple-element.45) | copy-start | bytes 3932164
  258.1 3.9 %copy-start.1 = (f32[2,16,10240]{2,1,0:T(8,128)S(1)}, f32[2,16,10240]{2,1,0:T(8,128)}, u32[]{:S(2)}) copy-start(f32[2,16,10240]{2,1,0:T(8,128)} %reshape.236) | copy-start | bytes 3932164
  263.2 6.0 %copy-start.2 = (f32[2,16,20480]{2,1,0:T(8,128)S(1)}, f32[2,16,20480]{2,1,0:T(8,128)}, u32[]{:S(2)}) copy-start(f32[2,16,20480]{2,1,0:T(8,128)} %constant_dynamic-update-slice_fusion) | copy-start | bytes 7864324
  265.8 3.4 collective-permute-start.3
  266.1 51.7 %collective-permute-start.1 = (bf16[8,32,32,128]{3,2,1,0:T(8,128)(2,1)}, bf16[8,32,32,128]{3,2,1,0:T(8,128)(2,1)}, u32[]{:S(2)}, u32[]{:S(2)}) collective-permute-start(bf16[8,32,32,128]{3,2,1,0:T(8,128)(2,1)} %get-tuple-element.36), channel_id=1, source_target_pairs={{0,1},{1,0},{2,3},{3,2},{4,5},{5,4},{6,7},{7,6},{8,9},{9,8},{10,11... | collective-permute-start | bytes 6291464 | tf_op jit(solution)/shard_map/ppermute | solution.py:598
  270.6 2.0 copy-start.3
  270.7 2.3 copy-start.7
  270.7 2.3 copy-start.35
  270.7 3.6 copy-start.11
  270.7 3.7 %copy-start.12 = (f32[160,64]{0,1:T(8,128)S(1)}, f32[160,64]{0,1:T(8,128)}, u32[]{:S(2)}) copy-start(f32[160,64]{0,1:T(8,128)} %param.51) | copy-start | bytes 122884
  270.7 3.8 %copy-start.13 = (f32[9,1024]{1,0:T(8,128)S(1)}, f32[9,1024]{1,0:T(8,128)}, u32[]{:S(2)}) copy-start(f32[9,1024]{1,0:T(8,128)} %get-tuple-element.39) | copy-start | bytes 110596
  270.7 3.8 %copy-start.29 = (f32[9,128]{1,0:T(8,128)S(1)}, f32[9,128]{1,0:T(8,128)}, u32[]{:S(2)}) copy-start(f32[9,128]{1,0:T(8,128)} %get-tuple-element.38) | copy-start | bytes 13828
  270.7 3.8 %copy-start.34 = (f32[8,128]{1,0:T(8,128)S(1)}, f32[8,128]{1,0:T(8,128)}, u32[]{:S(2)}) copy-start(f32[8,128]{1,0:T(8,128)} %get-tuple-element.37) | copy-start | bytes 12292
  270.7 45.1 %copy-start.19 = (f32[2,4,128]{2,1,0:T(4,128)S(1)}, f32[2,4,128]{2,1,0:T(4,128)}, u32[]{:S(2)}) copy-start(f32[2,4,128]{2,1,0:T(4,128)} %refs_7_.1) | copy-start | bytes 12292
  270.8 45.1 %copy-start.30 = (f32[2,4,128]{2,1,0:T(4,128)S(1)}, f32[2,4,128]{2,1,0:T(4,128)}, u32[]{:S(2)}) copy-start(f32[2,4,128]{2,1,0:T(4,128)} %param.54) | copy-start | bytes 12292
  270.8 45.1 %copy-start.31 = (f32[2,4,128]{2,1,0:T(4,128)S(1)}, f32[2,4,128]{2,1,0:T(4,128)}, u32[]{:S(2)}) copy-start(f32[2,4,128]{2,1,0:T(4,128)} %param.53) | copy-start | bytes 12292
  270.8 45.7 %copy-start.16 = (f32[2,9,32]{2,0,1:T(2,128)S(1)}, f32[2,9,32]{2,0,1:T(2,128)}, u32[]{:S(2)}) copy-start(f32[2,9,32]{2,0,1:T(2,128)} %param.55) | copy-start | bytes 6916
  270.8 45.7 %copy-start.27 = (f32[2,9,32]{2,0,1:T(2,128)S(1)}, f32[2,9,32]{2,0,1:T(2,128)}, u32[]{:S(2)}) copy-start(f32[2,9,32]{2,0,1:T(2,128)} %param.57) | copy-start | bytes 6916
  270.8 45.7 %copy-start.28 = (f32[2,9,32]{2,0,1:T(2,128)S(1)}, f32[2,9,32]{2,0,1:T(2,128)}, u32[]{:S(2)}) copy-start(f32[2,9,32]{2,0,1:T(2,128)} %param.56) | copy-start | bytes 6916
  270.8 46.3 %copy-start.8 = (f32[9,512]{1,0:T(8,128)S(1)}, f32[9,512]{1,0:T(8,128)}, u32[]{:S(2)}) copy-start(f32[9,512]{1,0:T(8,128)} %param.58) | copy-start | bytes 55300
  270.8 46.3 %copy-start.17 = (f32[9,512]{1,0:T(8,128)S(1)}, f32[9,512]{1,0:T(8,128)}, u32[]{:S(2)}) copy-start(f32[9,512]{1,0:T(8,128)} %param.60) | copy-start | bytes 55300
  270.8 46.3 %copy-start.18 = (f32[9,512]{1,0:T(8,128)S(1)}, f32[9,512]{1,0:T(8,128)}, u32[]{:S(2)}) copy-start(f32[9,512]{1,0:T(8,128)} %param.59) | copy-start | bytes 55300
  272.6 50.5 %collective-permute-start.2 = (bf16[8,32,32,128]{3,2,1,0:T(8,128)(2,1)S(1)}, bf16[8,32,32,128]{3,2,1,0:T(8,128)(2,1)}, u32[]{:S(2)}, u32[]{:S(2)}) collective-permute-start(bf16[8,32,32,128]{3,2,1,0:T(8,128)(2,1)S(1)} %copy-done.3), channel_id=1, source_target_pairs={{0,1},{1,0},{2,3},{3,2},{4,5},{5,4},{6,7},{7,6},{8,9},{9,8},{10,11... | collective-permute-start | bytes 6291464 | tf_op jit(solution)/shard_map/ppermute | solution.py:598
  323.1 32.4 %copy-start.9 = (f32[512,8]{0,1:T(8,128)S(1)}, f32[512,8]{0,1:T(8,128)}, u32[]{:S(2)}) copy-start(f32[512,8]{0,1:T(8,128)} %param.46) | copy-start | bytes 49156
  323.1 32.4 %copy-start.20 = (f32[512,8]{0,1:T(8,128)S(1)}, f32[512,8]{0,1:T(8,128)}, u32[]{:S(2)}) copy-start(f32[512,8]{0,1:T(8,128)} %param.48) | copy-start | bytes 49156
  323.1 32.4 %copy-start.21 = (f32[512,8]{0,1:T(8,128)S(1)}, f32[512,8]{0,1:T(8,128)}, u32[]{:S(2)}) copy-start(f32[512,8]{0,1:T(8,128)} %param.47) | copy-start | bytes 49156
  323.1 33.0 %copy-start.10 = (f32[8,512]{1,0:T(8,128)S(1)}, f32[8,512]{1,0:T(8,128)}, u32[]{:S(2)}) copy-start(f32[8,512]{1,0:T(8,128)} %param.43) | copy-start | bytes 49156
  323.1 33.0 %copy-start.22 = (f32[8,512]{1,0:T(8,128)S(1)}, f32[8,512]{1,0:T(8,128)}, u32[]{:S(2)}) copy-start(f32[8,512]{1,0:T(8,128)} %param.45) | copy-start | bytes 49156
  323.1 33.0 %copy-start.23 = (f32[8,512]{1,0:T(8,128)S(1)}, f32[8,512]{1,0:T(8,128)}, u32[]{:S(2)}) copy-start(f32[8,512]{1,0:T(8,128)} %param.44) | copy-start | bytes 49156
  323.1 33.6 %copy-start.24 = (f32[64,8]{0,1:T(8,128)S(1)}, f32[64,8]{0,1:T(8,128)}, u32[]{:S(2)}) copy-start(f32[64,8]{0,1:T(8,128)} %param.40) | copy-start | bytes 6148
  323.1 33.6 %copy-start.32 = (f32[64,8]{0,1:T(8,128)S(1)}, f32[64,8]{0,1:T(8,128)}, u32[]{:S(2)}) copy-start(f32[64,8]{0,1:T(8,128)} %param.42) | copy-start | bytes 6148
  323.1 33.6 %copy-start.33 = (f32[64,8]{0,1:T(8,128)S(1)}, f32[64,8]{0,1:T(8,128)}, u32[]{:S(2)}) copy-start(f32[64,8]{0,1:T(8,128)} %param.41) | copy-start | bytes 6148
  323.1 34.2 %copy-start.14 = (f32[3,8,64]{2,1,0:T(8,128)S(1)}, f32[3,8,64]{2,1,0:T(8,128)}, u32[]{:S(2)}) copy-start(f32[3,8,64]{2,1,0:T(8,128)} %param.37) | copy-start | bytes 18436
  323.2 34.2 %copy-start.25 = (f32[3,8,64]{2,1,0:T(8,128)S(1)}, f32[3,8,64]{2,1,0:T(8,128)}, u32[]{:S(2)}) copy-start(f32[3,8,64]{2,1,0:T(8,128)} %param.39) | copy-start | bytes 18436
  323.2 34.2 %copy-start.26 = (f32[3,8,64]{2,1,0:T(8,128)S(1)}, f32[3,8,64]{2,1,0:T(8,128)}, u32[]{:S(2)}) copy-start(f32[3,8,64]{2,1,0:T(8,128)} %param.38) | copy-start | bytes 18436
Sparse Core Ops, SparseCore 0:
  12.6 56.9 all-gather.1
  272.3 77.7 reduce-scatter.1

commit v2 on v1

--- a/solution.py
+++ b/solution.py
@@ -16,6 +16,9 @@
 NN = (((1,), (0,)), ((), ()))
 NT = (((1,), (1,)), ((), ()))
 TN = (((0,), (0,)), ((), ()))
+MESH = pl.DeviceIdType.MESH
+SMALL = 64
+LIMIT = 60 * 1024 * 1024
 
 
 def mm(a, b, dims=NN):
@@ -113,17 +116,14 @@
 
 
 def block_kernel(
-    info,
+    resolution,
+    live_images,
+    head,
     tokens,
     cotangent,
-    entry,
-    mixing_t,
-    expand,
-    shrink_t,
-    reduce_w,
+    packed,
+    filters,
     norms,
-    value_filter,
-    hidden_filter,
     perm,
     perm_t,
     shifts,
@@ -131,14 +131,25 @@
     edge,
     out,
     input_grad,
+    mine,
+    theirs,
+    small_mine,
+    small_theirs,
+    entry,
+    mixing_t,
+    expand,
+    shrink_t,
+    reduce_w,
+    value_filter,
+    hidden_filter,
+    wide_s,
+    square_s,
     d_entry,
     d_mixing_t,
-    d_expand,
     d_shrink_t,
     d_reduce,
     d_norm,
     d_value,
-    d_hidden,
     conv_w,
     key_value_w,
     im2col,
@@ -150,21 +161,58 @@
     probs,
     normed_s,
     queries_s,
+    reduce_low,
     *,
     steps,
 ):
     step = pl.program_id(0)
+    devices = packed.shape[0] // 2
+    width = 128 // devices
     ff = expand.shape[1]
     lane = lax.broadcasted_iota(jnp.int32, (128, 128), 1)
     first_lanes = lane % 64 < 32
 
+    def left(rows):
+        return lax.broadcasted_iota(jnp.int32, (rows, 128), 1) < 64
+
     @pl.when(step == 0)
     def prepare():
+        top, chunk = 12 * width, ff // 256
+        for d in range(devices):
+            one, two = [packed[2 * d + h].astype(F32) for h in range(2)]
+            mask = left(top)
+            reduce_w[20 * width * d : 20 * width * d + top, :] = jnp.where(
+                mask, one[:top], pltpu.roll(two[:top], 64, 1)
+            )
+            rest = jnp.where(mask, pltpu.roll(one[:top], 64, 1), two[:top])
+            reduce_w[20 * width * d + top : 20 * width * (d + 1), :] = rest[: 8 * width]
+            rows = slice(width * d, width * d + width)
+            for e in range(4):
+                square_s[e, rows, :] = rest[(8 + e) * width : (9 + e) * width]
+            for h, part in enumerate((one, two)):
+                for u in range(chunk):
+                    cols = slice((h * chunk + u) * 128, (h * chunk + u + 1) * 128)
+                    wide_s[0, rows, cols] = part[top + u * width : top + (u + 1) * width]
+                    wide_s[1, rows, cols] = part[
+                        top + (chunk + u) * width : top + (chunk + u + 1) * width
+                    ]
+        reduce_low[...] = reduce_w[...].astype(BF)
+        entry[...] = square_s[:3].astype(BF)
+        mixing_t[...] = square_s[3].astype(BF)
+        expand[...] = wide_s[0]
+        shrink_t[...] = wide_s[1].astype(BF)
+        for h in range(2):
+            hidden_filter[:, h * (ff // 2) : (h + 1) * (ff // 2)] = filters[h, :9, : ff // 2]
+        value_filter[...] = jnp.where(
+            left(9),
+            filters[0, :9, ff // 2 :],
+            pltpu.roll(filters[1, :9, ff // 2 :], 64, 1),
+        )
         for tap in range(9):
             gain = hidden_filter[tap : tap + 1, :]
             if tap == 4:
                 gain = gain + 1.0
-            conv_w[tap * 128 : (tap + 1) * 128, :] = (expand[...].astype(F32) * gain).astype(BF)
+            conv_w[tap * 128 : (tap + 1) * 128, :] = (expand[...] * gain).astype(BF)
         for g in range(2):
             w = entry[1 + g].astype(F32)
             if g == 0:
@@ -178,8 +226,9 @@
         for ref in (d_entry, d_mixing_t, d_shrink_t, d_reduce, d_norm, d_value, m_sum, d_key_value):
             ref[...] = jnp.zeros_like(ref)
 
-    fine = info[0, step]
-    alive = info[1, step]
+    grid = head[0] * steps + step
+    fine = (resolution[grid] == 8).astype(jnp.int32)
+    alive = live_images[grid]
     fine_f = fine.astype(F32)
 
     def ordered(ref):
@@ -242,7 +291,7 @@
     cell_saved = []
     keys, values = [], []
     for g in range(2):
-        reduced = mm(patches[g], reduce_w[rows_of[g], :])
+        reduced = mm(patches[g], reduce_low[rows_of[g], :])
         unit, scale = normalise(reduced)
         act, slope = gelu_pair(unit * gain(1 + g) + shift_by(1 + g))
         cell_low = act.astype(BF)
@@ -448,7 +497,7 @@
         add_norm(1 + g, cell_grad, unit)
         reduced_low = normalise_back(cell_grad * gain(1 + g), unit, scale).astype(BF)
         d_reduce[rows_of[g], :] += mm(patches[g], reduced_low, TN)
-        back = mm(reduced_low, reduce_w[rows_of[g], :], NT)
+        back = mm(reduced_low, reduce_low[rows_of[g], :], NT)
         if g == 0:
             order = [place_of(block) for block in range(16)]
             order = [a4 * 4 + b4 for a4, b4 in order]
@@ -463,40 +512,81 @@
 
     @pl.when(step == steps - 1)
     def finish():
-        weight = expand[...].astype(F32)
+        weight = expand[...]
         total = None
         for tap in range(9):
             part = m_sum[tap * 128 : tap * 128 + 128, :]
             factor = hidden_filter[tap : tap + 1, :]
             if tap == 4:
                 factor = factor + 1.0
-            d_hidden[tap : tap + 1, :] = jnp.sum(part * weight, 0, keepdims=True)
+            hidden_filter[tap : tap + 1, :] = jnp.sum(part * weight, 0, keepdims=True)
             total = part * factor if total is None else total + part * factor
-        d_expand[...] = total
+        wide_s[0] = total
+        wide_s[1] = d_shrink_t[...]
         d_entry[1] = jnp.where(
             first_lanes, d_key_value[0, :, :128], pltpu.roll(d_key_value[0, :, 128:], 32, 1)
         )
         d_entry[2] = jnp.where(
             first_lanes, pltpu.roll(d_key_value[1, :, :128], 96, 1), d_key_value[1, :, 128:]
         )
-
-
-def run_block(
-    info,
-    offset,
-    tokens,
-    cotangent,
-    entry,
-    mixing_t,
-    expand,
-    shrink_t,
-    reduce_w,
-    norms,
-    value_filter,
-    hidden_filter,
-):
-    steps = info.shape[1]
-    ff = expand.shape[1]
+        is_second = head[0] == 1
+        top, chunk = 12 * width, ff // 256
+        planes, lines = mine.shape[0], mine.shape[1]
+
+        def put(d, rows, first, second):
+            place = (d % planes, d // planes, rows)
+            mine[place] = jnp.where(is_second, second, first)
+            theirs[place] = jnp.where(is_second, first, second).astype(BF)
+
+        for d in range(devices):
+            rows = slice(width * d, width * d + width)
+            upper = d_reduce[20 * width * d : 20 * width * d + top, :]
+            lower = jnp.concatenate(
+                [d_reduce[20 * width * d + top : 20 * width * (d + 1), :]]
+                + [d_entry[e, rows, :] for e in range(3)]
+                + [d_mixing_t[rows, :]],
+                0,
+            )
+            firsts = [jnp.where(left(top), upper, pltpu.roll(lower, 64, 1))]
+            seconds = [jnp.where(left(top), pltpu.roll(upper, 64, 1), lower)]
+            for n in range(2):
+                for h, parts in enumerate((firsts, seconds)):
+                    for u in range(chunk):
+                        cols = slice((h * chunk + u) * 128, (h * chunk + u + 1) * 128)
+                        parts.append(wide_s[n, rows, cols])
+            pad = mine.shape[2] - 20 * width
+            if pad:
+                firsts.append(jnp.zeros((pad, 128), F32))
+                seconds.append(jnp.zeros((pad, 128), F32))
+            put(d, slice(None), jnp.concatenate(firsts, 0), jnp.concatenate(seconds, 0))
+        count = jnp.int32(0)
+        for n in range(steps):
+            side = resolution[head[0] * steps + n]
+            count = count + side * side * live_images[head[0] * steps + n]
+        halves = [
+            jnp.concatenate(
+                [
+                    hidden_filter[:, (h * chunk + u) * 128 : (h * chunk + u + 1) * 128]
+                    for u in range(chunk)
+                ],
+                0,
+            )
+            for h in range(2)
+        ]
+        for ref, flip in ((small_mine, False), (small_theirs, True)):
+            ref[...] = jnp.zeros_like(ref)
+            ref[:8, :] = d_norm[...]
+            ref[8:17, :] = d_value[...]
+            ref[17:18, :] = jnp.full((1, 128), count, jnp.int32).astype(F32)
+            second = jnp.logical_not(is_second) if flip else is_second
+            ref[18 : 18 + 9 * chunk, :] = jnp.where(second, halves[1], halves[0])
+
+
+def run_block(resolution, live_images, head, tokens, cotangent, packed, filters, norms):
+    steps = tokens.shape[0] // 2
+    devices, rows = packed.shape[0] // 2, packed.shape[1]
+    ff = 2 * (filters.shape[2] - 128)
+    lines = line_of(devices)
     consts = [
         jnp.asarray(order_matrix(), BF),
         jnp.asarray(order_matrix().T, BF),
@@ -504,32 +594,49 @@
         jnp.asarray(score_bias(), F32),
         jnp.asarray(shift_masks(), F32),
     ]
-    whole = [entry, mixing_t, expand, shrink_t, reduce_w, norms, value_filter, hidden_filter] + consts
+    whole = [packed, filters, norms] + consts
 
     def all_of(a):
-        return pl.BlockSpec(a.shape, lambda i, *_: (0,) * a.ndim)
-
-    grid_in = pl.BlockSpec((1, 32, 32, 128), lambda i, info, off: (off[0] + i, 0, 0, 0))
+        return pl.BlockSpec(a.shape, lambda i, *_, n=a.ndim: (0,) * n)
+
+    grid_in = pl.BlockSpec((1, 32, 32, 128), lambda i, res, live, head: (head[0] * steps + i, 0, 0, 0))
     grid_out = pl.BlockSpec((1, 32, 32, 128), lambda i, *_: (i, 0, 0, 0))
-    sums = [(3, 128, 128), (128, 128), (128, ff), (128, ff), (2560, 128), (8, 128), (9, 128), (9, ff)]
     out_shape = [
         jax.ShapeDtypeStruct((steps, 32, 32, 128), BF),
         jax.ShapeDtypeStruct((steps, 32, 32, 128), BF),
-    ] + [jax.ShapeDtypeStruct(s, F32) for s in sums]
-
-    def kernel(info, off, *refs):
-        block_kernel(info, *refs, steps=steps)
+        jax.ShapeDtypeStruct((devices // lines, lines, rows, 128), F32),
+        jax.ShapeDtypeStruct((devices // lines, lines, rows, 128), BF),
+        jax.ShapeDtypeStruct((SMALL, 128), F32),
+        jax.ShapeDtypeStruct((SMALL, 128), F32),
+    ]
+
+    def kernel(*refs):
+        block_kernel(*refs, steps=steps)
 
     return pl.pallas_call(
         kernel,
         out_shape=out_shape,
         grid_spec=pltpu.PrefetchScalarGridSpec(
-            num_scalar_prefetch=2,
+            num_scalar_prefetch=3,
             grid=(steps,),
             in_specs=[grid_in, grid_in] + [all_of(a) for a in whole],
-            out_specs=[grid_out, grid_out]
-            + [pl.BlockSpec(s, lambda i, *_, n=len(s): (0,) * n) for s in sums],
+            out_specs=[grid_out, grid_out] + [all_of(a) for a in out_shape[2:]],
             scratch_shapes=[
+                pltpu.VMEM((3, 128, 128), BF),
+                pltpu.VMEM((128, 128), BF),
+                pltpu.VMEM((128, ff), F32),
+                pltpu.VMEM((128, ff), BF),
+                pltpu.VMEM((2560, 128), F32),
+                pltpu.VMEM((9, 128), F32),
+                pltpu.VMEM((9, ff), F32),
+                pltpu.VMEM((2, 128, ff), F32),
+                pltpu.VMEM((4, 128, 128), F32),
+                pltpu.VMEM((3, 128, 128), F32),
+                pltpu.VMEM((128, 128), F32),
+                pltpu.VMEM((128, ff), F32),
+                pltpu.VMEM((2560, 128), F32),
+                pltpu.VMEM((8, 128), F32),
+                pltpu.VMEM((9, 128), F32),
                 pltpu.VMEM((1152, ff), BF),
                 pltpu.VMEM((2, 128, 256), BF),
                 pltpu.VMEM((1024, 1152), BF),
@@ -541,13 +648,370 @@
                 pltpu.VMEM((4, 160, 256), F32),
                 pltpu.VMEM((1024, 128), BF),
                 pltpu.VMEM((1024, 128), BF),
+                pltpu.VMEM((2560, 128), BF),
             ],
         ),
         compiler_params=pltpu.CompilerParams(
-            dimension_semantics=("arbitrary",), vmem_limit_bytes=60 * 1024 * 1024
+            dimension_semantics=("arbitrary",), vmem_limit_bytes=LIMIT
         ),
         name="block",
-    )(info, offset, tokens, cotangent, *whole)
+    )(resolution, live_images, head, tokens, cotangent, *whole)
+
+
+def line_of(devices):
+    return 4 if devices % 4 == 0 else 1
+
+
+def rows_of_block(devices):
+    return -(-20 * (128 // devices) // 16) * 16
+
+
+def pack_kernel(entry, mixing, expand, shrink, reduce_w, values, hidden, block, filters, held):
+    width, ff = expand.shape
+    top, chunk = 12 * width, ff // 128
+    held[...] = jnp.zeros_like(held)
+    held[:top, :64] = reduce_w[:top, :]
+    held[: 8 * width, 64:] = reduce_w[top:, :]
+    for e in range(3):
+        held[(8 + e) * width : (9 + e) * width, 64:] = entry[e]
+    held[11 * width : top, 64:] = mixing[...].T
+    turned = shrink[...].T
+    for u in range(chunk):
+        cols = slice(u * 128, (u + 1) * 128)
+        held[top + u * width : top + (u + 1) * width, :] = expand[:, cols]
+        held[top + (chunk + u) * width : top + (chunk + u + 1) * width, :] = turned[:, cols]
+    block[...] = held[...].astype(BF)
+    filters[...] = jnp.zeros_like(filters)
+    filters[:9, :ff] = hidden[...]
+    for g in range(2):
+        filters[:9, ff + 32 * g : ff + 32 * g + 32] = values[g]
+
+
+def run_pack(devices, entry, mixing, expand, shrink, reduce_w, values, hidden):
+    rows = rows_of_block(devices)
+    return pl.pallas_call(
+        pack_kernel,
+        out_shape=[
+            jax.ShapeDtypeStruct((rows, 128), BF),
+            jax.ShapeDtypeStruct((16, hidden.shape[1] + 128), F32),
+        ],
+        scratch_shapes=[pltpu.VMEM((rows, 128), F32)],
+        compiler_params=pltpu.CompilerParams(vmem_limit_bytes=LIMIT),
+        name="pack",
+    )(entry, mixing, expand, shrink, reduce_w, values, hidden)
+
+
+def greet(peers):
+    barrier = pltpu.get_barrier_semaphore()
+    for peer in peers:
+        pl.semaphore_signal(barrier, inc=1, device_id=peer, device_id_type=MESH)
+    pl.semaphore_wait(barrier, len(peers))
+
+
+def places(devices):
+    lines = line_of(devices)
+    planes = devices // lines
+    me, head = lax.axis_index("dp"), lax.axis_index("head")
+    z, p = me // planes, me % planes
+    line_peers = [((z + k) % lines) for k in range(1, lines)]
+    plane_peers = [((p + k) % planes) for k in range(1, planes)]
+    return lines, planes, z, p, head, line_peers, plane_peers
+
+
+def gather_kernel(devices, block, filters, blocks, both, send_sem, recv_sem, filter_sem, local_sem):
+    lines, planes, z, p, head, line_peers, plane_peers = places(devices)
+
+    def slot(line, plane, core):
+        return (line * planes + plane) * 2 + core
+
+    def at(line, plane, core):
+        return (line * planes + plane, core)
+
+    sibling = at(z, p, 1 - head)
+    greet(
+        [at(k, p, head) for k in line_peers] + [at(z, k, head) for k in plane_peers] + [sibling]
+    )
+    sends = []
+
+    def send(source, index, target):
+        copy = pltpu.make_async_remote_copy(
+            src_ref=source,
+            dst_ref=blocks.at[index],
+            send_sem=send_sem.at[len(sends)],
+            recv_sem=recv_sem.at[index],
+            device_id=target,
+            device_id_type=MESH,
+        )
+        copy.start()
+        sends.append(copy)
+
+    def arrived(index):
+        pltpu.make_async_remote_copy(
+            src_ref=block,
+            dst_ref=blocks.at[index],
+            send_sem=send_sem.at[0],
+            recv_sem=recv_sem.at[index],
+            device_id=sibling,
+            device_id_type=MESH,
+        ).wait_recv()
+
+    own = slot(z, p, head)
+    for k in line_peers:
+        send(block, own, at(k, p, head))
+    for k in plane_peers:
+        send(block, own, at(z, k, head))
+    send(block, own, sibling)
+    swap = pltpu.make_async_remote_copy(
+        src_ref=filters,
+        dst_ref=both.at[head],
+        send_sem=filter_sem.at[0],
+        recv_sem=filter_sem.at[1],
+        device_id=sibling,
+        device_id_type=MESH,
+    )
+    swap.start()
+    keep = [
+        pltpu.make_async_copy(block, blocks.at[own], local_sem.at[0]),
+        pltpu.make_async_copy(filters, both.at[head], local_sem.at[1]),
+    ]
+    for copy in keep:
+        copy.start()
+    for k in line_peers:
+        index = slot(k, p, head)
+        arrived(index)
+        for j in plane_peers:
+            send(blocks.at[index], index, at(z, j, head))
+        send(blocks.at[index], index, sibling)
+    for line in [z] + line_peers:
+        for j in plane_peers:
+            index = slot(line, j, head)
+            arrived(index)
+            send(blocks.at[index], index, sibling)
+    for line in [z] + line_peers:
+        for j in [p] + plane_peers:
+            arrived(slot(line, j, 1 - head))
+    for copy in sends:
+        copy.wait_send()
+    swap.wait_send()
+    pltpu.make_async_remote_copy(
+        src_ref=filters,
+        dst_ref=both.at[1 - head],
+        send_sem=filter_sem.at[0],
+        recv_sem=filter_sem.at[1],
+        device_id=sibling,
+        device_id_type=MESH,
+    ).wait_recv()
+    for copy in keep:
+        copy.wait()
+
+
+def run_gather(devices, block, filters):
+    lines = line_of(devices)
+    planes = devices // lines
+    copies = (lines - 1) + lines * (planes - 1) + lines * planes
+    anywhere = pl.BlockSpec(memory_space=pl.ANY)
+
+    def kernel(*refs):
+        gather_kernel(devices, *refs)
+
+    return pl.pallas_call(
+        kernel,
+        out_shape=[
+            jax.ShapeDtypeStruct((2 * devices,) + block.shape, BF),
+            jax.ShapeDtypeStruct((2,) + filters.shape, F32),
+        ],
+        in_specs=[anywhere, anywhere],
+        out_specs=[anywhere, anywhere],
+        scratch_shapes=[
+            pltpu.SemaphoreType.DMA((copies,)),
+            pltpu.SemaphoreType.DMA((2 * devices,)),
+            pltpu.SemaphoreType.DMA((2,)),
+            pltpu.SemaphoreType.DMA((2,)),
+        ],
+        compiler_params=pltpu.CompilerParams(collective_id=0, has_side_effects=True),
+        name="gather",
+    )(block, filters)
+
+
+def reduce_kernel(
+    devices,
+    mine,
+    theirs,
+    small_mine,
+    small_theirs,
+    out_half,
+    input_half,
+    grad,
+    small,
+    out_other,
+    input_other,
+    core_in,
+    core_small,
+    plane_out,
+    plane_in,
+    plane_small,
+    line_sum,
+    line_out,
+    line_in,
+    line_small,
+    core_send,
+    core_recv,
+    plane_send,
+    plane_recv,
+    line_send,
+    line_recv,
+):
+    lines, planes, z, p, head, line_peers, plane_peers = places(devices)
+
+    def at(line, plane, core):
+        return (line * planes + plane, core)
+
+    sibling = at(z, p, 1 - head)
+    greet(
+        [at(k, p, head) for k in line_peers] + [at(z, k, head) for k in plane_peers] + [sibling]
+    )
+
+    def remote(source, target, send, recv, device):
+        return pltpu.make_async_remote_copy(
+            src_ref=source,
+            dst_ref=target,
+            send_sem=send,
+            recv_sem=recv,
+            device_id=device,
+            device_id_type=MESH,
+        )
+
+    started = []
+
+    def go(*args):
+        copy = remote(*args)
+        copy.start()
+        started.append(copy)
+
+    go(small_theirs, core_small, core_send.at[planes], core_recv.at[planes], sibling)
+    for k in plane_peers + [p]:
+        go(theirs.at[k], core_in.at[k], core_send.at[k], core_recv.at[k], sibling)
+    remote(
+        small_theirs, core_small, core_send.at[planes], core_recv.at[planes], sibling
+    ).wait_recv()
+    plane_small[pl.ds(p, 1)] = (small_mine[...] + core_small[...])[None]
+    for n, k in enumerate(plane_peers):
+        go(
+            plane_small.at[p],
+            plane_small.at[p],
+            plane_send.at[planes + n],
+            plane_recv.at[planes + p],
+            at(z, k, head),
+        )
+    for n, k in enumerate(plane_peers):
+        remote(
+            theirs.at[k], core_in.at[k], core_send.at[k], core_recv.at[k], sibling
+        ).wait_recv()
+        plane_out[pl.ds(k, 1)] = (mine[pl.ds(k, 1)] + core_in[pl.ds(k, 1)].astype(F32)).astype(BF)
+        go(plane_out.at[k], plane_in.at[p], plane_send.at[n], plane_recv.at[p], at(z, k, head))
+    remote(theirs.at[p], core_in.at[p], core_send.at[p], core_recv.at[p], sibling).wait_recv()
+    go(out_half, out_other, core_send.at[planes + 1], core_recv.at[planes + 1], sibling)
+    go(input_half, input_other, core_send.at[planes + 2], core_recv.at[planes + 2], sibling)
+    total = mine[pl.ds(p, 1)][0] + core_in[pl.ds(p, 1)][0].astype(F32)
+    for k in plane_peers:
+        remote(
+            plane_out.at[k], plane_in.at[k], plane_send.at[0], plane_recv.at[k], sibling
+        ).wait_recv()
+        total = total + plane_in[pl.ds(k, 1)][0].astype(F32)
+    line_sum[...] = total
+    for n, k in enumerate(line_peers):
+        line_out[pl.ds(k, 1)] = line_sum[pl.ds(k, 1)].astype(BF)
+        go(line_out.at[k], line_in.at[z], line_send.at[n], line_recv.at[z], at(k, p, head))
+    for k in plane_peers:
+        remote(
+            plane_small.at[p],
+            plane_small.at[k],
+            plane_send.at[0],
+            plane_recv.at[planes + k],
+            sibling,
+        ).wait_recv()
+    part = plane_small[0]
+    for k in range(1, planes):
+        part = part + plane_small[k]
+    line_small[pl.ds(z, 1)] = part[None]
+    for n, k in enumerate(line_peers):
+        go(
+            line_small.at[z],
+            line_small.at[z],
+            line_send.at[lines + n],
+            line_recv.at[lines + z],
+            at(k, p, head),
+        )
+    own = line_sum[pl.ds(z, 1)][0]
+    for k in line_peers:
+        remote(
+            line_out.at[k], line_in.at[k], line_send.at[0], line_recv.at[k], sibling
+        ).wait_recv()
+        own = own + line_in[pl.ds(k, 1)][0].astype(F32)
+    grad[...] = own
+    for k in line_peers:
+        remote(
+            line_small.at[z],
+            line_small.at[k],
+            line_send.at[0],
+            line_recv.at[lines + k],
+            sibling,
+        ).wait_recv()
+    part = line_small[0]
+    for k in range(1, lines):
+        part = part + line_small[k]
+    small[...] = part
+    remote(
+        out_half, out_other, core_send.at[planes + 1], core_recv.at[planes + 1], sibling
+    ).wait_recv()
+    remote(
+        input_half, input_other, core_send.at[planes + 2], core_recv.at[planes + 2], sibling
+    ).wait_recv()
+    for copy in started:
+        copy.wait_send()
+
+
+def run_reduce(devices, mine, theirs, small_mine, small_theirs, out_half, input_half):
+    planes, lines, rows = mine.shape[:3]
+    anywhere = pl.BlockSpec(memory_space=pl.ANY)
+    vmem = pl.BlockSpec(memory_space=pltpu.VMEM)
+    sem = pltpu.SemaphoreType.DMA
+
+    def kernel(*refs):
+        reduce_kernel(devices, *refs)
+
+    return pl.pallas_call(
+        kernel,
+        out_shape=[
+            jax.ShapeDtypeStruct((rows, 128), F32),
+            jax.ShapeDtypeStruct((SMALL, 128), F32),
+            jax.ShapeDtypeStruct(out_half.shape, BF),
+            jax.ShapeDtypeStruct(input_half.shape, BF),
+        ],
+        in_specs=[vmem] * 4 + [anywhere] * 2,
+        out_specs=[vmem] * 2 + [anywhere] * 2,
+        scratch_shapes=[
+            pltpu.VMEM((planes, lines, rows, 128), BF),
+            pltpu.VMEM((SMALL, 128), F32),
+            pltpu.VMEM((planes, lines, rows, 128), BF),
+            pltpu.VMEM((planes, lines, rows, 128), BF),
+            pltpu.VMEM((planes, SMALL, 128), F32),
+            pltpu.VMEM((lines, rows, 128), F32),
+            pltpu.VMEM((lines, rows, 128), BF),
+            pltpu.VMEM((lines, rows, 128), BF),
+            pltpu.VMEM((lines, SMALL, 128), F32),
+            sem((planes + 3,)),
+            sem((planes + 3,)),
+            sem((2 * planes,)),
+            sem((2 * planes,)),
+            sem((2 * lines,)),
+            sem((2 * lines,)),
+        ],
+        compiler_params=pltpu.CompilerParams(
+            collective_id=1, has_side_effects=True, vmem_limit_bytes=LIMIT
+        ),
+        name="reduce",
+    )(mine, theirs, small_mine, small_theirs, out_half, input_half)
 
 
 def advance(weight, moment, average, gradient, step_rate, weight_decay):
@@ -555,6 +1019,112 @@
     moment = 0.9 * moment + gradient
     weight = weight - step_rate * (gradient + 0.9 * moment)
     return (moment, weight, 0.8 * average + 0.2 * weight)
+
+
+RATES = (0.3, 0.12, 0.12, 0.03, 0.1, 0.2, 0.4, 0.5)
+
+
+def update_kernel(head, *refs, tokens_all):
+    out_own, out_other, in_own, in_other, grad, small = refs[:6]
+    state = refs[6:30]
+    output, input_grad = refs[30:32]
+    results = refs[32:]
+    step = pl.program_id(0)
+    half = pl.num_programs(0) // 2
+    factor = tokens_all / small[17:18, :]
+    is_own = (step // half) == head[0]
+
+    @pl.when(is_own)
+    def own():
+        output[...] = out_own[...]
+        input_grad[...] = in_own[...].astype(F32) * factor
+
+    @pl.when(jnp.logical_not(is_own))
+    def other():
+        output[...] = out_other[...]
+        input_grad[...] = in_other[...].astype(F32) * factor
+
+    @pl.when(step == 0)
+    def update():
+        width, ff = state[6].shape
+        top, chunk = 12 * width, ff // 128
+        rate_unit = tokens_all**-0.5
+
+        def apply(n, place, raw, scale):
+            new = advance(
+                state[3 * n][place],
+                state[3 * n + 1][place],
+                state[3 * n + 2][place],
+                scale * raw,
+                RATES[n] * rate_unit,
+                0.0 if n == 5 else 0.05,
+            )
+            for k in range(3):
+                results[3 * n + k][place] = new[k]
+
+        scale = factor[:, :64]
+        for e in range(3):
+            apply(0, e, grad[(8 + e) * width : (9 + e) * width, 64:], scale)
+        apply(1, Ellipsis, grad[11 * width : top, 64:].T, factor[:, :width])
+        for u in range(chunk):
+            cols = slice(u * 128, (u + 1) * 128)
+            apply(2, (slice(None), cols), grad[top + u * width : top + (u + 1) * width, :], factor)
+            apply(
+                3,
+                (cols, slice(None)),
+                grad[top + (chunk + u) * width : top + (chunk + u + 1) * width, :].T,
+                factor[:, :width],
+            )
+        apply(4, (slice(0, top), slice(None)), grad[:top, :64], scale)
+        apply(4, (slice(top, 20 * width), slice(None)), grad[: 8 * width, 64:], scale)
+        for n in range(2):
+            apply(5, n, small[4 * n : 4 * n + 4, :], factor)
+        values = small[8:17, :]
+        values = jnp.where(head[0] == 1, pltpu.roll(values, 64, 1), values)
+        for g in range(2):
+            apply(6, g, values[:, 32 * g : 32 * g + 32], factor[:, :32])
+        for u in range(chunk):
+            apply(
+                7,
+                (slice(None), slice(u * 128, (u + 1) * 128)),
+                small[18 + 9 * u : 27 + 9 * u, :],
+                factor,
+            )
+
+
+def run_update(tokens_all, head, out_own, out_other, in_own, in_other, grad, small, state):
+    half = out_own.shape[0]
+
+    def all_of(a):
+        return pl.BlockSpec(a.shape, lambda i, *_, n=a.ndim: (0,) * n)
+
+    block = (1,) + out_own.shape[1:]
+    own = pl.BlockSpec(block, lambda i, head: (jnp.clip(i - head[0] * half, 0, half - 1), 0, 0, 0))
+    other = pl.BlockSpec(
+        block, lambda i, head: (jnp.clip(i - (1 - head[0]) * half, 0, half - 1), 0, 0, 0)
+    )
+    final = pl.BlockSpec(block, lambda i, *_: (i, 0, 0, 0))
+    whole = (2 * half,) + out_own.shape[1:]
+
+    def kernel(*refs):
+        update_kernel(*refs, tokens_all=tokens_all)
+
+    return pl.pallas_call(
+        kernel,
+        out_shape=[jax.ShapeDtypeStruct(whole, BF), jax.ShapeDtypeStruct(whole, F32)]
+        + [jax.ShapeDtypeStruct(a.shape, F32) for a in state],
+        grid_spec=pltpu.PrefetchScalarGridSpec(
+            num_scalar_prefetch=1,
+            grid=(2 * half,),
+            in_specs=[own, other, own, other, all_of(grad), all_of(small)]
+            + [all_of(a) for a in state],
+            out_specs=[final, final] + [all_of(a) for a in state],
+        ),
+        compiler_params=pltpu.CompilerParams(
+            dimension_semantics=("arbitrary",), vmem_limit_bytes=LIMIT
+        ),
+        name="update",
+    )(head, out_own, out_other, in_own, in_other, grad, small, *state)
 
 
 def per_device(
@@ -588,112 +1158,56 @@
     hidden_average,
 ):
     devices = lax.axis_size("dp")
-    head = lax.axis_index("head")
-    swap = [(0, 1), (1, 0)]
-    grids = tokens.shape[0]
-    half = grids // 2
-    ff = 2 * expand_weight.shape[1]
-
-    def pair(own, axis):
-        other = lax.ppermute(own, "head", swap)
-        return jnp.where(
-            head == 0, jnp.concatenate([own, other], axis), jnp.concatenate([other, own], axis)
+    head = lax.axis_index("head").reshape(1).astype(jnp.int32)
+    block, filters = run_pack(
+        devices,
+        entry_weight,
+        mixing_weight,
+        expand_weight,
+        shrink_weight,
+        reduce_weight,
+        value_filter,
+        hidden_filter,
+    )
+    blocks, filters = run_gather(devices, block, filters)
+    out_half, input_half, mine, theirs, small_mine, small_theirs = run_block(
+        resolution, live_images, head, tokens, cotangent, blocks, filters, norm_params
+    )
+    grad, small, out_other, input_other = run_reduce(
+        devices, mine, theirs, small_mine, small_theirs, out_half, input_half
+    )
+    state = (
+        entry_weight,
+        entry_momentum,
+        entry_average,
+        mixing_weight,
+        mixing_momentum,
+        mixing_average,
+        expand_weight,
+        expand_momentum,
+        expand_average,
+        shrink_weight,
+        shrink_momentum,
+        shrink_average,
+        reduce_weight,
+        reduce_momentum,
+        reduce_average,
+        norm_params,
+        norm_momentum,
+        norm_average,
+        value_filter,
+        value_momentum,
+        value_average,
+        hidden_filter,
+        hidden_momentum,
+        hidden_average,
+    )
+    tokens_all = devices * tokens.shape[0] * tokens.shape[1] * tokens.shape[2]
+    return tuple(
+        run_update(
+            tokens_all, head, out_half, out_other, input_half, input_other, grad, small, state
         )
-
-    shards = (entry_weight, mixing_weight.T, expand_weight, shrink_weight.T, reduce_weight)
-    shapes = [s.shape for s in shards]
-    sizes = [s.size for s in shards]
-    starts = [sum(sizes[:n]) for n in range(6)]
-    packed = jnp.concatenate([s.astype(BF).reshape(-1) for s in shards]).reshape(-1, 128)
-    gathered = lax.all_gather(packed, ("dp", "head")).reshape(devices, 2, -1)
-    parts = [
-        gathered[:, :, starts[n] : starts[n + 1]].reshape((devices, 2) + shapes[n]) for n in range(5)
-    ]
-    entry = parts[0].transpose(2, 0, 3, 1, 4).reshape(3, 128, 128)
-    mixing_t, expand, shrink_t, reduce_w = [
-        p.transpose(0, 2, 1, 3).reshape(devices * p.shape[2], -1) for p in parts[1:]
-    ]
-    values_here = value_filter.transpose(1, 0, 2).reshape(9, 64)
-    filters = pair(jnp.concatenate([values_here, hidden_filter], 1)[None], 0)
-    values_full = filters[:, :, :64].transpose(1, 0, 2).reshape(9, 128)
-    hidden_full = filters[:, :, 64:].transpose(1, 0, 2).reshape(9, ff)
-
-    fine = (resolution == 8).astype(jnp.int32)
-    info = lax.dynamic_slice_in_dim(jnp.stack([fine, live_images]), head * half, half, 1)
-    offset = (head * half).reshape(1).astype(jnp.int32)
-    (
-        out_half,
-        input_half,
-        d_entry,
-        d_mixing_t,
-        d_expand,
-        d_shrink_t,
-        d_reduce,
-        d_norm,
-        d_value,
-        d_hidden,
-    ) = run_block(
-        info,
-        offset,
-        tokens,
-        cotangent,
-        entry,
-        mixing_t,
-        expand,
-        shrink_t,
-        reduce_w,
-        norm_params,
-        values_full,
-        hidden_full,
-    )
-    live_here = jnp.sum(info[1] * jnp.where(info[0] == 1, 64, 256)).astype(F32)
-
-    small = jnp.concatenate(
-        [d_norm.reshape(-1), d_value.reshape(-1), d_hidden.reshape(-1), live_here.reshape(1)]
-    )
-    small = lax.psum(small, ("dp", "head"))
-    norm_grad = small[:1024].reshape(2, 4, 128)
-    value_grad = small[1024 : 1024 + 1152].reshape(9, 2, 2, 32)
-    value_grad = lax.dynamic_index_in_dim(value_grad, head, 1, False).transpose(1, 0, 2)
-    hidden_grad = small[2176 : 2176 + 9 * ff].reshape(9, 2, ff // 2)
-    hidden_grad = lax.dynamic_index_in_dim(hidden_grad, head, 1, False)
-    live_total = small[-1]
-
-    d_entry = d_entry.reshape(3, devices, -1, 2, 64).transpose(3, 1, 0, 2, 4)
-    d_rest = [
-        d.reshape(devices, -1, 2, d.shape[1] // 2).transpose(2, 0, 1, 3)
-        for d in (d_mixing_t, d_expand, d_shrink_t, d_reduce)
-    ]
-    grads = jnp.concatenate([d.reshape(2, devices, -1) for d in [d_entry] + d_rest], 2)
-    mine = lax.dynamic_index_in_dim(grads, head, 0, False)
-    theirs = lax.dynamic_index_in_dim(grads, 1 - head, 0, False)
-    mine = mine + lax.ppermute(theirs, "head", swap)
-    mine = lax.psum_scatter(mine.reshape(devices, -1, 128), "dp", scatter_dimension=0)
-    mine = mine.reshape(-1)
-    entry_grad, mixing_grad, expand_grad, shrink_grad, reduce_grad = [
-        mine[starts[n] : starts[n + 1]].reshape(shapes[n]) for n in range(5)
-    ]
-    mixing_grad, shrink_grad = mixing_grad.T, shrink_grad.T
-
-    output = pair(out_half, 0)
-    input_raw = pair(input_half, 0)
-    tokens_all = devices * grids * tokens.shape[1] * tokens.shape[2]
-    factor = tokens_all / live_total
-    rate_unit = tokens_all ** (-0.5)
-    input_grad = factor * input_raw.astype(F32)
-    results = []
-    for weight, moment, average, grad, rate, decay in (
-        (entry_weight, entry_momentum, entry_average, entry_grad, 0.3, 0.05),
-        (mixing_weight, mixing_momentum, mixing_average, mixing_grad, 0.12, 0.05),
-        (expand_weight, expand_momentum, expand_average, expand_grad, 0.12, 0.05),
-        (shrink_weight, shrink_momentum, shrink_average, shrink_grad, 0.03, 0.05),
-        (reduce_weight, reduce_momentum, reduce_average, reduce_grad, 0.1, 0.05),
-        (norm_params, norm_momentum, norm_average, norm_grad, 0.2, 0.0),
-        (value_filter, value_momentum, value_average, value_grad, 0.4, 0.05),
-        (hidden_filter, hidden_momentum, hidden_average, hidden_grad, 0.5, 0.05),
-    ):
-        results.extend(advance(weight, moment, average, factor * grad, rate * rate_unit, decay))
-    return (output, input_grad, *results)
+    )
 
 
 def solution(mesh):

time: 366 us -> 258 us (0.70)
  waiting for transfers between devices: 75.9 us -> 0 us
  Pallas kernels: 161 us -> 221 us
  blocking collectives: 39.9 us -> 0 us
  other arithmetic: 26 us -> 0 us
  between operations: 16.1 us -> 0.71 us
  local copies, waits for them, and re-layouts: 44.6 us -> 35.4 us
    pallas_call x0 -> x4, Pallas kernels: none -> 59.5 us  [the longest x1 24.2 us: run_reduce(): pl.pallas_call(kernel, out_shape=[jax.ShapeDtypeStruct((rows, 128), F32),...]
    all_gather x1 -> x0, waiting for transfers between devices: 51.5 us -> none  [per_device(): gathered = lax.all_gather(packed, ('dp', 'head')).reshape(devices, 2, -1)]
    psum x1 -> x0, blocking collectives: 39.9 us -> none  [per_device(): small = lax.psum(small, ('dp', 'head'))]
    reshape x28 -> x0, local copies, waits for them, and re-layouts: 24.3 us -> none  [the longest x3 6.53 us: per_device(): p.transpose(0, 2, 1, 3).reshape(devices * p.shape[2], -1)]
    reduce_scatter x1 -> x0, waiting for transfers between devices: 21.4 us -> none  [per_device(): lax.psum_scatter(mine.reshape(devices, -1, 128), 'dp', scatter_dimension=0)]
    pallas_call x1 -> x12, local copies, waits for them, and re-layouts: 0.4 us -> 18 us  [run_update(): pl.pallas_call(kernel, out_shape=[jax.ShapeDtypeStruct(whole, BF), jax.Sh...]
    mul x7 -> x0, other arithmetic: 8.43 us -> none  [the longest x1 5.5 us: per_device(): input_grad = factor * input_raw.astype(F32)]
    unnamed x91 -> x12, local copies, waits for them, and re-layouts: 10.8 us -> 17.4 us
  transfers between devices with their start and end apart: 6 -> 0, of which waited for: 3 -> 0; matrix products, arithmetic and copies ran while one was open for 6% -> 0% of each run, Pallas kernels for 0% -> 0%
where the time goes in v2:
time: 258 us; the launch traced here: 257 us
  Pallas kernels  221 us (86%)
  local copies, waits for them, and re-layouts  35.4 us (14%)
    pallas_call x1, Pallas kernels, run_block(): pl.pallas_call(kernel, out_shape=out_shape, grid_spec=pltpu.PrefetchScala...  161 us
    pallas_call x1, Pallas kernels, run_reduce(): pl.pallas_call(kernel, out_shape=[jax.ShapeDtypeStruct((rows, 128), F32),...  24.2 us
    pallas_call x1, Pallas kernels, run_gather(): pl.pallas_call(kernel, out_shape=[jax.ShapeDtypeStruct((2 * devices,) + b...  18.7 us
    pallas_call x12, local copies, waits for them, and re-layouts, run_update(): pl.pallas_call(kernel, out_shape=[jax.ShapeDtypeStruct(whole, BF), jax.Sh...  18 us
    unnamed x12, local copies, waits for them, and re-layouts  17.4 us
    pallas_call x1, Pallas kernels, run_update(): pl.pallas_call(kernel, out_shape=[jax.ShapeDtypeStruct(whole, BF), jax.Sh...  14.7 us

profile of v2, /device:TPU:0, one launch (start us, length us, event | category | flops | bytes accessed | tf_op | source)
XLA Modules:
  0.0 256.7 jit_solution(17577002227703523817)
XLA Ops:
  0.7 1.3 copy.62.values.refs_25_
  2.0 1.3 copy.73.refs_26_
  3.3 1.3 copy.74.refs_27_
  4.6 1.4 copy.59.mixing.refs_10_
  6.0 1.4 copy.64.refs_11_
  7.3 1.4 copy.65.refs_12_
  8.7 1.6 copy.61.reduce_w.refs_19_
  10.3 1.6 copy.70.refs_20_
  11.8 1.6 copy.71.refs_21_
  13.4 1.6 copy.60.shrink.refs_16_
  15.0 1.9 pack.1
  16.9 1.6 copy.67.refs_17_
  18.5 1.6 copy.68.refs_18_
  20.0 18.7 %gather.1 = (bf16[32,160,128]{2,1,0:T(8,128)(2,1)}, f32[2,16,640]{2,1,0:T(8,128)}) custom-call(bf16[160,128]{1,0:T(8,128)(2,1)} %get-tuple-element.40.refs_0_, f32[16,640]{1,0:T(8,128)} %get-tuple-element.41.refs_1_), custom_call_target="tpu_custom_call" | custom-call | tf_op jit(solution)/shard_map/gather/pallas_call | solution.py:817
  38.8 161.0 %block.1 = (bf16[8,32,32,128]{3,2,1,0:T(8,128)(2,1)}, bf16[8,32,32,128]{3,2,1,0:T(8,128)(2,1)}, f32[4,4,160,128]{3,2,1,0:T(8,128)}, bf16[4,4,160,128]{3,2,1,0:T(...) custom-call(s32[16]{0:T(128)} %refs_0_.1, s32[16]{0:T(128)} %refs_1_.1, s32[1]{0:T(128)} %bitcast.refs_2_.refs_0_, ...), custom_call_target="tpu_custom_call" | custom-call | tf_op jit(solution)/shard_map/block/pallas_call | solution.py:616
  199.8 24.2 %reduce.1 = (f32[160,128]{1,0:T(8,128)}, f32[64,128]{1,0:T(8,128)}, bf16[8,32,32,128]{3,2,1,0:T(8,128)(2,1)}, bf16[8,32,32,128]{3,2,1,0:T(8,128)(2,1)}) custom-call(f32[4,4,160,128]{3,2,1,0:T(8,128)} %get-tuple-element.45.refs_0_, bf16[4,4,160,128]{3,2,1,0:T(8,128)(2,1)} %get-tuple-element.46.refs_1_, f32[64,128]{1,0:T(8,128)} %get-tuple-element.47.refs_2_, ...), custom_call_target="tpu_custom_call" | custom-call | tf_op jit(solution)/shard_map/reduce/pallas_call | solution.py:983
  224.0 14.7 %update.1 = (bf16[16,32,32,128]{3,2,1,0:T(8,128)(2,1)}, f32[16,32,32,128]{3,2,1,0:T(8,128)}, f32[3,8,64]{2,1,0:T(8,128)}, f32[3,8,64]{2,1,0:T(8,128)}, f32[3,8,6...) custom-call(s32[1]{0:T(128)} %bitcast.refs_2_.refs_0_, ...), custom_call_target="tpu_custom_call" | custom-call | tf_op jit(solution)/shard_map/update/pallas_call | solution.py:1112
  238.7 1.4 copy.75
  240.1 1.4 copy.76
  241.5 1.4 copy.77
  243.0 1.3 copy.84
  244.3 1.3 copy.85
  245.6 1.3 copy.86
  246.9 1.7 copy.78
  248.6 1.7 copy.79
  250.2 1.7 copy.80
  251.9 1.6 copy.81
  253.5 1.6 copy.82
  255.1 1.6 copy.83

commit v3 on v2

--- a/solution.py
+++ b/solution.py
@@ -18,7 +18,9 @@
 TN = (((0,), (0,)), ((), ()))
 MESH = pl.DeviceIdType.MESH
 SMALL = 64
+PAIR = 2
 LIMIT = 60 * 1024 * 1024
+ROOT = math.sqrt(0.5)
 
 
 def mm(a, b, dims=NN):
@@ -62,7 +64,8 @@
                 shifts[0, tap, n, other] = 1
                 if places[other][3:] == (si, sk):
                     shifts[1, tap, n, other] = 1
-    return shifts.reshape(2, 720, 80)
+    shifts = shifts.reshape(2, 720, 80)
+    return np.concatenate([shifts, shifts], 2)
 
 
 def score_bias():
@@ -105,14 +108,15 @@
 
 
 def gelu_pair(h):
-    density = jnp.exp(-0.5 * (h * h))
-    t = 1.0 / (1.0 + (0.3275911 * math.sqrt(0.5)) * jnp.abs(h))
-    poly = 1.061405429 * 0.5
-    for c in (-1.453152027, 1.421413741, -0.284496736, 0.254829592):
-        poly = poly * t + c * 0.5
-    tail = poly * t * density
-    below = jnp.where(h >= 0, 1.0 - tail, tail)
+    below = 0.5 + 0.5 * lax.erf(h * math.sqrt(0.5))
+    density = jnp.exp2(h * h * (-0.5 * math.log2(math.e)))
     return h * below, below + h * density * (1.0 / math.sqrt(2 * math.pi))
+
+
+def scaled_gelu_pair(u):
+    below = math.sqrt(0.5) + math.sqrt(0.5) * lax.erf(u)
+    density = jnp.exp2(u * u * (-math.log2(math.e)))
+    return u * below, below + u * density * (2.0 / math.sqrt(2 * math.pi))
 
 
 def block_kernel(
@@ -147,25 +151,42 @@
     d_entry,
     d_mixing_t,
     d_shrink_t,
-    d_reduce,
+    d_reduce_t,
     d_norm,
     d_value,
     conv_w,
     key_value_w,
-    im2col,
-    im2col_t,
     g_low,
     m_sum,
     folds,
     d_key_value,
-    probs,
+    reduce_low,
+    im2col,
+    im2col_t,
+    middle_s,
+    up_s,
+    unit1_s,
+    scale1_s,
+    unit2_s,
+    scale2_s,
     normed_s,
     queries_s,
-    reduce_low,
+    mixed_s,
+    probs,
+    keys_s,
+    enhanced_s,
+    values_s,
+    wide_cells,
+    wide_scale,
+    narrow_cells,
+    narrow_scale,
+    second_grad_s,
     *,
     steps,
 ):
     step = pl.program_id(0)
+    last = pl.num_programs(0) - 1
+    first_grid = head[0] * steps
     devices = packed.shape[0] // 2
     width = 128 // devices
     ff = expand.shape[1]
@@ -212,7 +233,7 @@
             gain = hidden_filter[tap : tap + 1, :]
             if tap == 4:
                 gain = gain + 1.0
-            conv_w[tap * 128 : (tap + 1) * 128, :] = (expand[...] * gain).astype(BF)
+            conv_w[tap * 128 : (tap + 1) * 128, :] = (expand[...] * (gain * ROOT)).astype(BF)
         for g in range(2):
             w = entry[1 + g].astype(F32)
             if g == 0:
@@ -223,17 +244,12 @@
                 keep = jnp.logical_not(first_lanes)
             key_value_w[g, :, :128] = jnp.where(keep, keys, 0.0).astype(BF)
             key_value_w[g, :, 128:] = jnp.where(keep, vals, 0.0).astype(BF)
-        for ref in (d_entry, d_mixing_t, d_shrink_t, d_reduce, d_norm, d_value, m_sum, d_key_value):
+        for ref in (d_entry, d_mixing_t, d_shrink_t, d_reduce_t, d_norm, d_value, m_sum, d_key_value):
             ref[...] = jnp.zeros_like(ref)
 
-    grid = head[0] * steps + step
-    fine = (resolution[grid] == 8).astype(jnp.int32)
-    alive = live_images[grid]
-    fine_f = fine.astype(F32)
-
-    def ordered(ref):
+    def ordered(ref, place):
         parts = [
-            ref[0, a * 16 : a * 16 + 16, b * 16 : b * 16 + 16, :].reshape(256, 128)
+            ref[place, a * 16 : a * 16 + 16, b * 16 : b * 16 + 16, :].reshape(256, 128)
             for a in range(2)
             for b in range(2)
         ]
@@ -242,7 +258,7 @@
             [rows[:, q * 128 : q * 128 + 128].reshape(16, 16, 128) for q in range(4)], 1
         ).reshape(1024, 128)
 
-    def restore(value, ref):
+    def restore(value, ref, place):
         blocks = value.reshape(16, 4, 16, 128)
         rows = mm(
             perm_t[...],
@@ -250,9 +266,9 @@
         ).astype(BF)
         for q in range(4):
             a, b = q // 2, q % 2
-            ref[0, a * 16 : a * 16 + 16, b * 16 : b * 16 + 16, :] = rows[
+            ref[pl.ds(place, 1), a * 16 : a * 16 + 16, b * 16 : b * 16 + 16, :] = rows[
                 :, q * 128 : q * 128 + 128
-            ].reshape(16, 16, 128)
+            ].reshape(1, 16, 16, 128)
 
     def of_quadrant(value, q, blocks):
         return value.reshape(blocks, 4, 16, 128)[:, q].reshape(blocks * 16, 128)
@@ -272,86 +288,26 @@
         d_norm[n : n + 1, :] += jnp.sum(grad * unit, 0, keepdims=True)
         d_norm[4 + n : 5 + n, :] += jnp.sum(grad, 0, keepdims=True)
 
-    x = ordered(tokens)
-    unit1, scale1 = normalise(x)
-    normed = (unit1 * gain(0) + shift_by(0)).astype(BF)
-    normed_s[...] = normed
-    queries_s[...] = mm(normed, entry[0]).astype(BF)
-    patches = (
-        jnp.concatenate(
-            [
-                normed_s[block_of(t // 4, t % 4) * 64 : block_of(t // 4, t % 4) * 64 + 64, :]
-                for t in range(16)
-            ],
-            1,
-        ),
-        jnp.concatenate([normed_s[t * 256 : t * 256 + 256, :] for t in range(4)], 1),
-    )
-    rows_of = (slice(0, 2048), slice(2048, 2560))
-    cell_saved = []
-    keys, values = [], []
-    for g in range(2):
-        reduced = mm(patches[g], reduce_low[rows_of[g], :])
-        unit, scale = normalise(reduced)
-        act, slope = gelu_pair(unit * gain(1 + g) + shift_by(1 + g))
-        cell_low = act.astype(BF)
-        pair = mm(cell_low, key_value_w[g])
-        keys.append(pair[:, :128].astype(BF))
-        values.append(pair[:, 128:])
-        cell_saved.append((unit, scale, slope, cell_low))
-    keys_all = [
-        jnp.concatenate([keys[0][q * 16 : q * 16 + 16], of_quadrant(keys[1], q, 4)], 0)
-        for q in range(4)
-    ]
-    values_all = jnp.concatenate(
-        [
-            jnp.concatenate([values[0][q * 16 : q * 16 + 16], of_quadrant(values[1], q, 4)], 0)
-            for q in range(4)
-        ],
-        1,
-    )
-    moves = shifts[pl.ds(fine, 1)][0]
-    high = values_all.astype(BF)
-    rest = (values_all - high.astype(F32)).astype(BF)
-    moved = mm(moves, high) + mm(moves, rest)
-    taps4 = jnp.concatenate([value_filter[...]] * 4, 1)
-    enhanced = values_all
-    for tap in range(9):
-        enhanced = enhanced + moved[tap * 80 : tap * 80 + 80] * taps4[tap : tap + 1]
-    enhanced = enhanced.astype(BF)
     lane80 = lax.broadcasted_iota(jnp.int32, (80, 128), 1)
     zero80 = jnp.zeros((80, 128), BF)
-
-    def both_heads(rows):
-        return jnp.concatenate(
-            [jnp.where(lane80 < 64, rows, zero80), jnp.where(lane80 < 64, zero80, rows)], 0
-        )
-
     segments = ((0, 16), (16, 80), (80, 96), (96, 160))
-    queries = queries_s[...]
-    query_q = [of_quadrant(queries, q, 16) for q in range(4)]
-    keys_q = [both_heads(keys_all[q]) for q in range(4)]
-    enhanced_q = [both_heads(enhanced[:, q * 128 : q * 128 + 128]) for q in range(4)]
-    mixed_parts = []
     scaling = 32**-0.5
-    for q in range(4):
-        scores = mm(keys_q[q], query_q[q], NT) * scaling + fine_f * bias[...]
-        weights = []
-        for lo, hi in segments:
-            part = scores[lo:hi]
-            part = jnp.exp(part - jnp.max(part, 0, keepdims=True))
-            weights.append(part / jnp.sum(part, 0, keepdims=True))
-        weights = jnp.concatenate(weights, 0)
-        probs[q] = weights
-        mixed_parts.append(mm(weights.astype(BF), enhanced_q[q], TN))
-    mixed = of_quadrants(mixed_parts, 16).astype(BF)
-    middle = x + mm(mixed, mixing_t[...], NT)
-    unit2, scale2 = normalise(middle)
-    second = unit2 * gain(3) + shift_by(3)
-    second_low = second.astype(BF)
-    second_f = second_low.astype(F32)
-
-    def move(value, rows, columns):
+    rows_of = (slice(0, 2048), slice(2048, 2560))
+    cells_f = (wide_cells, narrow_cells)
+    cells_scale = (wide_scale, narrow_scale)
+
+    def fine_of(grid):
+        return (resolution[first_grid + grid] == 8).astype(jnp.int32)
+
+    def patches_of(slot, g):
+        if g == 0:
+            blocks = [block_of(t // 4, t % 4) for t in range(16)]
+            parts = [normed_s[slot, b * 64 : b * 64 + 64, :] for b in blocks]
+        else:
+            parts = [normed_s[slot, t * 256 : t * 256 + 256, :] for t in range(4)]
+        return jnp.concatenate(parts, 1)
+
+    def move(value, fine, rows, columns):
         size = value.shape[0]
         if rows:
             n = 0 if rows > 0 else 1
@@ -370,158 +326,305 @@
     def wrap(a4, d):
         return (a4 + d) % 4, (a4 + d) // 4
 
-    moved_blocks = {}
-    for block in range(16):
-        a4, b4 = place_of(block)
+    def attend(slot, grid):
+        fine = fine_of(grid)
+        alive = live_images[first_grid + grid]
+        x = ordered(tokens, slot)
+        unit1, scale1 = normalise(x)
+        unit1_s[slot] = unit1
+        scale1_s[slot] = scale1
+        normed = (unit1 * gain(0) + shift_by(0)).astype(BF)
+        normed_s[slot] = normed
+        yield
+        queries_s[slot] = mm(normed, entry[0]).astype(BF)
+        keys, values = [], []
+        for g in range(2):
+            reduced = mm(patches_of(slot, g), reduce_low[rows_of[g], :])
+            unit, scale = normalise(reduced)
+            act, slope = gelu_pair(unit * gain(1 + g) + shift_by(1 + g))
+            cells_f[g][slot, 0] = unit
+            cells_f[g][slot, 1] = slope
+            cells_f[g][slot, 2] = act
+            cells_scale[g][slot] = scale
+            pair = mm(act.astype(BF), key_value_w[g])
+            keys.append(pair[:, :128].astype(BF))
+            values.append(pair[:, 128:])
+            yield
+        keys_all = [
+            jnp.concatenate([keys[0][q * 16 : q * 16 + 16], of_quadrant(keys[1], q, 4)], 0)
+            for q in range(4)
+        ]
+        values_all = jnp.concatenate(
+            [
+                jnp.concatenate(
+                    [values[0][q * 16 : q * 16 + 16], of_quadrant(values[1], q, 4)], 0
+                )
+                for q in range(4)
+            ],
+            1,
+        )
+        values_s[slot] = values_all
+        moves = shifts[pl.ds(fine, 1)][0]
+        high = values_all.astype(BF)
+        rest = (values_all - high.astype(F32)).astype(BF)
+        moved = mm(moves, jnp.concatenate([high, rest], 0))
+        taps4 = jnp.concatenate([value_filter[...]] * 4, 1)
+        enhanced = values_all
         for tap in range(9):
-            na, wa = wrap(a4, tap // 3 - 1)
-            nb, wb = wrap(b4, tap % 3 - 1)
-            source = block_of(na, nb)
-            key = (source, wa, wb)
-            if key not in moved_blocks:
-                rows = slice(source * 64, source * 64 + 64)
+            enhanced = enhanced + moved[tap * 80 : tap * 80 + 80] * taps4[tap : tap + 1]
+        enhanced = enhanced.astype(BF)
+        yield
+
+        def both_heads(rows):
+            return jnp.concatenate(
+                [jnp.where(lane80 < 64, rows, zero80), jnp.where(lane80 < 64, zero80, rows)], 0
+            )
+
+        queries = queries_s[slot]
+        scores = []
+        for q in range(4):
+            keys_s[slot, q] = both_heads(keys_all[q])
+            enhanced_s[slot, q] = both_heads(enhanced[:, q * 128 : q * 128 + 128])
+            scores.append(mm(keys_s[slot, q], of_quadrant(queries, q, 16), NT))
+        yield
+        for q in range(4):
+            biased = scores[q] * scaling + fine.astype(F32) * bias[...]
+            for lo, hi in segments:
+                part = biased[lo:hi]
+                part = jnp.exp(part - jnp.max(part, 0, keepdims=True))
+                probs[slot, q, lo:hi, :] = part * (1.0 / jnp.sum(part, 0, keepdims=True))
+        yield
+        mixed_parts = [
+            mm(probs[slot, q].astype(BF), enhanced_s[slot, q], TN) for q in range(4)
+        ]
+        yield
+        mixed = of_quadrants(mixed_parts, 16).astype(BF)
+        mixed_s[slot] = mixed
+        middle = x + mm(mixed, mixing_t[...], NT)
+        middle_s[slot] = middle
+        yield
+        unit2, scale2 = normalise(middle)
+        unit2_s[slot] = unit2
+        scale2_s[slot] = scale2
+        second_low = (unit2 * gain(3) + shift_by(3)).astype(BF)
+        second_f = second_low.astype(F32)
+        yield
+        moved_blocks = {}
+        for block in range(16):
+            a4, b4 = place_of(block)
+            for tap in range(9):
+                na, wa = wrap(a4, tap // 3 - 1)
+                nb, wb = wrap(b4, tap % 3 - 1)
+                source = block_of(na, nb)
+                key = (source, wa, wb)
+                if key not in moved_blocks:
+                    rows = slice(source * 64, source * 64 + 64)
+                    if wa or wb:
+                        moved_blocks[key] = move(second_f[rows], fine, wa, wb).astype(BF)
+                    else:
+                        moved_blocks[key] = second_low[rows]
+                im2col[slot, block * 64 : block * 64 + 64, tap * 128 : tap * 128 + 128] = (
+                    moved_blocks[key]
+                )
+            yield
+        row16 = lax.broadcasted_iota(jnp.int32, (16, 128), 0)
+        within = (row16 // 8) * 4 + (row16 % 4) // 2
+        live = jnp.stack(
+            [
+                jnp.where(
+                    jnp.where(fine == 1, within + (q // 2) * 8 + (q % 2) * 2, q) < alive, 1.0, 0.0
+                )
+                for q in range(4)
+            ],
+            0,
+        )
+        up_low = (
+            (ordered(cotangent, slot).reshape(16, 4, 16, 128) * live[None])
+            .reshape(1024, 128)
+            .astype(BF)
+        )
+        up_s[slot] = up_low
+        yield
+
+    def feed(slot, grid):
+        fine = fine_of(grid)
+        total = middle_s[slot]
+        wide = 256
+        held = None
+        for c in range(0, ff + wide, wide):
+            if c < ff:
+                cols = slice(c, c + wide)
+                hidden = mm(im2col[slot], conv_w[:, cols])
+                grad = mm(up_s[slot], shrink_t[:, cols])
+            if c == 0:
+                for tap in range(9):
+                    im2col_t[tap * 128 : tap * 128 + 128, :] = im2col[
+                        slot, :, tap * 128 : tap * 128 + 128
+                    ].T
+                up_t = up_s[slot].T
+            if held:
+                before, act, back = held
+                total = total + mm(act, shrink_t[:, before], NT)
+                d_shrink_t[:, before] += mm(up_t, act)
+                m_sum[:, before] += mm(im2col_t[...], back)
+            if c < ff:
+                act, slope = scaled_gelu_pair(hidden)
+                act = act.astype(BF)
+                grad = (grad * slope).astype(BF)
+                g_low[:, cols] = grad
+                held = (cols, act, grad)
+        restore(total.astype(BF), out, slot)
+        for t in range(0, 9, 2):
+            rows = slice(t * 128, min(t + 2, 9) * 128)
+            folds[:, rows] = mm(g_low[...], conv_w[rows, :], NT)
+        sums = {}
+        for block in range(16):
+            a4, b4 = place_of(block)
+            for tap in range(9):
+                na, wa = wrap(a4, tap // 3 - 1)
+                nb, wb = wrap(b4, tap % 3 - 1)
+                key = (block_of(na, nb), wa, wb)
+                sums.setdefault(key, []).append((block, tap))
+        for block in range(16):
+            total = None
+            for (source, wa, wb), terms in sums.items():
+                if source != block:
+                    continue
+                part = None
+                for other, tap in terms:
+                    term = folds[other * 64 : other * 64 + 64, tap * 128 : tap * 128 + 128]
+                    part = term if part is None else part + term
                 if wa or wb:
-                    moved_blocks[key] = move(second_f[rows], wa, wb).astype(BF)
-                else:
-                    moved_blocks[key] = second_low[rows]
-            im2col[block * 64 : block * 64 + 64, tap * 128 : tap * 128 + 128] = moved_blocks[key]
-    for tap in range(9):
-        im2col_t[tap * 128 : tap * 128 + 128, :] = im2col[:, tap * 128 : tap * 128 + 128].T
-
-    row16 = lax.broadcasted_iota(jnp.int32, (16, 128), 0)
-    within = (row16 // 8) * 4 + (row16 % 4) // 2
-    live = jnp.stack(
-        [
-            jnp.where(
-                jnp.where(fine == 1, within + (q // 2) * 8 + (q % 2) * 2, q) < alive, 1.0, 0.0
+                    part = move(part, fine, -wa, -wb)
+                total = part if total is None else total + part
+            second_grad_s[slot, block * 64 : block * 64 + 64, :] = total
+
+    def back(slot, grid):
+        fine = fine_of(grid)
+        second_grad = second_grad_s[slot]
+        unit2 = unit2_s[slot]
+        add_norm(3, second_grad, unit2)
+        middle_grad = up_s[slot].astype(F32) + normalise_back(
+            second_grad * gain(3), unit2, scale2_s[slot]
+        )
+        middle_low = middle_grad.astype(BF)
+        yield
+        mixed = mixed_s[slot]
+        d_mixing_t[...] += mm(middle_low, mixed, TN)
+        mixed_grad = mm(middle_low, mixing_t[...]).astype(BF)
+        queries = queries_s[slot]
+        yield
+        out_grads = [of_quadrant(mixed_grad, q, 16) for q in range(4)]
+        prob_grads = [mm(enhanced_s[slot, q], out_grads[q], NT) for q in range(4)]
+        yield
+        enhanced_parts = []
+        for q in range(4):
+            full = mm(probs[slot, q].astype(BF), out_grads[q])
+            enhanced_parts.append(jnp.where(lane80 < 64, full[:80], full[80:]).astype(BF))
+        yield
+        score_lows = []
+        for q in range(4):
+            weights = probs[slot, q]
+            product = weights * prob_grads[q]
+            score_grad = []
+            for lo, hi in segments:
+                score_grad.append(
+                    product[lo:hi] - weights[lo:hi] * jnp.sum(product[lo:hi], 0, keepdims=True)
+                )
+            score_lows.append((scaling * jnp.concatenate(score_grad, 0)).astype(BF))
+        yield
+        query_parts = [mm(score_lows[q], keys_s[slot, q], TN) for q in range(4)]
+        yield
+        key_parts = []
+        for q in range(4):
+            full = mm(score_lows[q], of_quadrant(queries, q, 16))
+            key_parts.append(jnp.where(lane80 < 64, full[:80], full[80:]).astype(BF))
+        yield
+        query_low = of_quadrants(query_parts, 16).astype(BF)
+        enhanced_grad = jnp.concatenate(enhanced_parts, 1)
+        moved = mm(shifts[pl.ds(fine, 1)][0][:, :80], enhanced_grad)
+        taps4 = jnp.concatenate([value_filter[...]] * 4, 1)
+        value_grad = enhanced_grad.astype(F32)
+        values_all = values_s[slot]
+        for tap in range(9):
+            part = moved[(8 - tap) * 80 : (8 - tap) * 80 + 80]
+            value_grad = value_grad + part * taps4[tap : tap + 1]
+            row = jnp.sum(part * values_all, 0, keepdims=True)
+            d_value[tap : tap + 1, :] += (
+                row[:, :128] + row[:, 128:256] + row[:, 256:384] + row[:, 384:]
             )
-            for q in range(4)
-        ],
-        0,
-    )
-    upstream = (ordered(cotangent).reshape(16, 4, 16, 128) * live[None]).reshape(1024, 128)
-    up_low = upstream.astype(BF)
-    up_t = up_low.T
-
-    feed = jnp.zeros((1024, 128), F32)
-    wide = 256
-    for c in range(0, ff, wide):
-        cols = slice(c, c + wide)
-        hidden = mm(im2col[...], conv_w[:, cols])
-        act, slope = gelu_pair(hidden)
-        act = act.astype(BF)
-        grad = mm(up_low, shrink_t[:, cols]) * slope
-        grad = grad.astype(BF)
-        g_low[:, cols] = grad
-        feed = feed + mm(act, shrink_t[:, cols], NT)
-        d_shrink_t[:, cols] += mm(up_t, act)
-        m_sum[:, cols] += mm(im2col_t[...], grad)
-    restore((middle + feed).astype(BF), out)
-
-    for t in range(0, 9, 2):
-        rows = slice(t * 128, min(t + 2, 9) * 128)
-        folds[:, rows] = mm(g_low[...], conv_w[rows, :], NT)
-    sums = {}
-    for block in range(16):
-        a4, b4 = place_of(block)
-        for tap in range(9):
-            na, wa = wrap(a4, tap // 3 - 1)
-            nb, wb = wrap(b4, tap % 3 - 1)
-            key = (block_of(na, nb), wa, wb)
-            sums.setdefault(key, []).append((block, tap))
-    second_parts = []
-    for block in range(16):
-        total = None
-        for (source, wa, wb), terms in sums.items():
-            if source != block:
-                continue
-            part = None
-            for other, tap in terms:
-                term = folds[other * 64 : other * 64 + 64, tap * 128 : tap * 128 + 128]
-                part = term if part is None else part + term
-            if wa or wb:
-                part = move(part, -wa, -wb)
-            total = part if total is None else total + part
-        second_parts.append(total)
-    second_grad = jnp.concatenate(second_parts, 0)
-    add_norm(3, second_grad, unit2)
-    middle_grad = upstream + normalise_back(second_grad * gain(3), unit2, scale2)
-    middle_low = middle_grad.astype(BF)
-    d_mixing_t[...] += mm(middle_low, mixed, TN)
-    mixed_grad = mm(middle_low, mixing_t[...]).astype(BF)
-
-    query_parts, key_parts, enhanced_parts = [], [], []
-    for q in range(4):
-        out_grad = of_quadrant(mixed_grad, q, 16)
-        weights = probs[q]
-        prob_grad = mm(enhanced_q[q], out_grad, NT)
-        product = weights * prob_grad
-        score_grad = []
-        for lo, hi in segments:
-            score_grad.append(
-                product[lo:hi] - weights[lo:hi] * jnp.sum(product[lo:hi], 0, keepdims=True)
+        value_grad = value_grad.astype(BF)
+        value_parts = [value_grad[:, q * 128 : q * 128 + 128] for q in range(4)]
+        yield
+        normed = normed_s[slot]
+        normed_grad = mm(query_low, entry[0], NT)
+        d_entry[0] += mm(normed, query_low, TN)
+        yield
+        for g in range(2):
+            if g == 0:
+                sides = [
+                    jnp.concatenate([p[:16] for p in parts], 0)
+                    for parts in (key_parts, value_parts)
+                ]
+            else:
+                sides = [
+                    of_quadrants([p[16:] for p in parts], 4) for parts in (key_parts, value_parts)
+                ]
+            pair = jnp.concatenate(sides, 1)
+            unit, slope = cells_f[g][slot, 0], cells_f[g][slot, 1]
+            cell_low = cells_f[g][slot, 2].astype(BF)
+            d_key_value[g] += mm(cell_low, pair, TN)
+            cell_grad = mm(pair, key_value_w[g], NT) * slope
+            add_norm(1 + g, cell_grad, unit)
+            reduced_low = normalise_back(
+                cell_grad * gain(1 + g), unit, cells_scale[g][slot]
+            ).astype(BF)
+            d_reduce_t[:, rows_of[g]] += mm(reduced_low, patches_of(slot, g), TN)
+            spread = mm(reduced_low, reduce_low[rows_of[g], :], NT)
+            if g == 0:
+                order = [place_of(block) for block in range(16)]
+                order = [a4 * 4 + b4 for a4, b4 in order]
+            else:
+                order = range(4)
+            normed_grad = normed_grad + jnp.concatenate(
+                [spread[:, t * 128 : t * 128 + 128] for t in order], 0
             )
-        score_low = (scaling * jnp.concatenate(score_grad, 0)).astype(BF)
-        query_parts.append(mm(score_low, keys_q[q], TN))
-        key_full = mm(score_low, query_q[q])
-        enhanced_full = mm(weights.astype(BF), out_grad)
-        key_parts.append(jnp.where(lane80 < 64, key_full[:80], key_full[80:]).astype(BF))
-        enhanced_parts.append(
-            jnp.where(lane80 < 64, enhanced_full[:80], enhanced_full[80:]).astype(BF)
-        )
-    query_low = of_quadrants(query_parts, 16).astype(BF)
-    enhanced_grad = jnp.concatenate(enhanced_parts, 1)
-    moved = mm(moves, enhanced_grad)
-    value_grad = enhanced_grad.astype(F32)
-    for tap in range(9):
-        part = moved[(8 - tap) * 80 : (8 - tap) * 80 + 80]
-        value_grad = value_grad + part * taps4[tap : tap + 1]
-        row = jnp.sum(part * values_all, 0, keepdims=True)
-        d_value[tap : tap + 1, :] += (
-            row[:, :128] + row[:, 128:256] + row[:, 256:384] + row[:, 384:]
-        )
-    value_grad = value_grad.astype(BF)
-    value_parts = [value_grad[:, q * 128 : q * 128 + 128] for q in range(4)]
-    normed = normed_s[...]
-    normed_grad = mm(query_low, entry[0], NT)
-    d_entry[0] += mm(normed, query_low, TN)
-    for g in range(2):
-        if g == 0:
-            sides = [jnp.concatenate([p[:16] for p in parts], 0) for parts in (key_parts, value_parts)]
-        else:
-            sides = [of_quadrants([p[16:] for p in parts], 4) for parts in (key_parts, value_parts)]
-        pair = jnp.concatenate(sides, 1)
-        unit, scale, slope, cell_low = cell_saved[g]
-        d_key_value[g] += mm(cell_low, pair, TN)
-        cell_grad = mm(pair, key_value_w[g], NT) * slope
-        add_norm(1 + g, cell_grad, unit)
-        reduced_low = normalise_back(cell_grad * gain(1 + g), unit, scale).astype(BF)
-        d_reduce[rows_of[g], :] += mm(patches[g], reduced_low, TN)
-        back = mm(reduced_low, reduce_low[rows_of[g], :], NT)
-        if g == 0:
-            order = [place_of(block) for block in range(16)]
-            order = [a4 * 4 + b4 for a4, b4 in order]
-        else:
-            order = range(4)
-        normed_grad = normed_grad + jnp.concatenate(
-            [back[:, t * 128 : t * 128 + 128] for t in order], 0
-        )
-    add_norm(0, normed_grad, unit1)
-    raw = middle_grad + normalise_back(normed_grad * gain(0), unit1, scale1)
-    restore(raw.astype(BF), input_grad)
-
-    @pl.when(step == steps - 1)
+            yield
+        unit1 = unit1_s[slot]
+        add_norm(0, normed_grad, unit1)
+        raw = middle_grad + normalise_back(normed_grad * gain(0), unit1, scale1_s[slot])
+        restore(raw.astype(BF), input_grad, slot)
+        yield
+
+    def together(*parts):
+        parts = list(parts)
+        while parts:
+            parts = [part for part in parts if next(part, parts) is not parts]
+
+    first = PAIR * step
+    together(*[attend(k, first + k) for k in range(PAIR)])
+
+    def feed_one(k, carry):
+        feed(k, first + k)
+        return carry
+
+    lax.fori_loop(0, PAIR, feed_one, 0)
+    together(*[back(k, first + k) for k in range(PAIR)])
+
+    @pl.when(step == last)
     def finish():
-        weight = expand[...]
-        total = None
-        for tap in range(9):
-            part = m_sum[tap * 128 : tap * 128 + 128, :]
-            factor = hidden_filter[tap : tap + 1, :]
-            if tap == 4:
-                factor = factor + 1.0
-            hidden_filter[tap : tap + 1, :] = jnp.sum(part * weight, 0, keepdims=True)
-            total = part * factor if total is None else total + part * factor
-        wide_s[0] = total
+        for c in range(0, ff, 256):
+            cols = slice(c, c + 256)
+            weight = expand[:, cols]
+            total = None
+            for tap in range(9):
+                part = m_sum[tap * 128 : tap * 128 + 128, cols] * ROOT
+                factor = hidden_filter[tap : tap + 1, cols]
+                if tap == 4:
+                    factor = factor + 1.0
+                hidden_filter[tap : tap + 1, cols] = jnp.sum(part * weight, 0, keepdims=True)
+                total = part * factor if total is None else total + part * factor
+            wide_s[0, :, cols] = total
         wide_s[1] = d_shrink_t[...]
         d_entry[1] = jnp.where(
             first_lanes, d_key_value[0, :, :128], pltpu.roll(d_key_value[0, :, 128:], 32, 1)
@@ -530,6 +633,10 @@
             first_lanes, pltpu.roll(d_key_value[1, :, :128], 96, 1), d_key_value[1, :, 128:]
         )
         is_second = head[0] == 1
+        d_reduce = reduce_w
+        for n in range(20):
+            rows = slice(n * 128, n * 128 + 128)
+            d_reduce[rows, :] = d_reduce_t[:, rows].T
         top, chunk = 12 * width, ff // 256
         planes, lines = mine.shape[0], mine.shape[1]
 
@@ -599,8 +706,10 @@
     def all_of(a):
         return pl.BlockSpec(a.shape, lambda i, *_, n=a.ndim: (0,) * n)
 
-    grid_in = pl.BlockSpec((1, 32, 32, 128), lambda i, res, live, head: (head[0] * steps + i, 0, 0, 0))
-    grid_out = pl.BlockSpec((1, 32, 32, 128), lambda i, *_: (i, 0, 0, 0))
+    grid_in = pl.BlockSpec(
+        (PAIR, 32, 32, 128), lambda i, res, live, head: (head[0] * (steps // PAIR) + i, 0, 0, 0)
+    )
+    grid_out = pl.BlockSpec((PAIR, 32, 32, 128), lambda i, *_: (i, 0, 0, 0))
     out_shape = [
         jax.ShapeDtypeStruct((steps, 32, 32, 128), BF),
         jax.ShapeDtypeStruct((steps, 32, 32, 128), BF),
@@ -618,7 +727,7 @@
         out_shape=out_shape,
         grid_spec=pltpu.PrefetchScalarGridSpec(
             num_scalar_prefetch=3,
-            grid=(steps,),
+            grid=(steps // PAIR,),
             in_specs=[grid_in, grid_in] + [all_of(a) for a in whole],
             out_specs=[grid_out, grid_out] + [all_of(a) for a in out_shape[2:]],
             scratch_shapes=[
@@ -634,21 +743,36 @@
                 pltpu.VMEM((3, 128, 128), F32),
                 pltpu.VMEM((128, 128), F32),
                 pltpu.VMEM((128, ff), F32),
-                pltpu.VMEM((2560, 128), F32),
+                pltpu.VMEM((128, 2560), F32),
                 pltpu.VMEM((8, 128), F32),
                 pltpu.VMEM((9, 128), F32),
                 pltpu.VMEM((1152, ff), BF),
                 pltpu.VMEM((2, 128, 256), BF),
-                pltpu.VMEM((1024, 1152), BF),
-                pltpu.VMEM((1152, 1024), BF),
                 pltpu.VMEM((1024, ff), BF),
                 pltpu.VMEM((1152, ff), F32),
                 pltpu.VMEM((1024, 1152), F32),
                 pltpu.VMEM((2, 128, 256), F32),
-                pltpu.VMEM((4, 160, 256), F32),
-                pltpu.VMEM((1024, 128), BF),
-                pltpu.VMEM((1024, 128), BF),
                 pltpu.VMEM((2560, 128), BF),
+                pltpu.VMEM((2, 1024, 1152), BF),
+                pltpu.VMEM((1152, 1024), BF),
+                pltpu.VMEM((2, 1024, 128), F32),
+                pltpu.VMEM((2, 1024, 128), BF),
+                pltpu.VMEM((2, 1024, 128), F32),
+                pltpu.VMEM((2, 1024, 1), F32),
+                pltpu.VMEM((2, 1024, 128), F32),
+                pltpu.VMEM((2, 1024, 1), F32),
+                pltpu.VMEM((2, 1024, 128), BF),
+                pltpu.VMEM((2, 1024, 128), BF),
+                pltpu.VMEM((2, 1024, 128), BF),
+                pltpu.VMEM((2, 4, 160, 256), F32),
+                pltpu.VMEM((2, 4, 160, 128), BF),
+                pltpu.VMEM((2, 4, 160, 128), BF),
+                pltpu.VMEM((2, 80, 512), F32),
+                pltpu.VMEM((2, 3, 64, 128), F32),
+                pltpu.VMEM((2, 64, 1), F32),
+                pltpu.VMEM((2, 3, 256, 128), F32),
+                pltpu.VMEM((2, 256, 1), F32),
+                pltpu.VMEM((2, 1024, 128), F32),
             ],
         ),
         compiler_params=pltpu.CompilerParams(
@@ -666,28 +790,28 @@
     return -(-20 * (128 // devices) // 16) * 16
 
 
-def pack_kernel(entry, mixing, expand, shrink, reduce_w, values, hidden, block, filters, held):
+def pack_kernel(entry, mixing_t, expand, shrink_t, reduce_t, values, hidden, block, filters, held):
     width, ff = expand.shape
     top, chunk = 12 * width, ff // 128
     held[...] = jnp.zeros_like(held)
-    held[:top, :64] = reduce_w[:top, :]
-    held[: 8 * width, 64:] = reduce_w[top:, :]
+    rows = reduce_t[...].T
+    held[:top, :64] = rows[:top, :]
+    held[: 8 * width, 64:] = rows[top:, :]
     for e in range(3):
         held[(8 + e) * width : (9 + e) * width, 64:] = entry[e]
-    held[11 * width : top, 64:] = mixing[...].T
-    turned = shrink[...].T
+    held[11 * width : top, 64:] = mixing_t[...]
     for u in range(chunk):
         cols = slice(u * 128, (u + 1) * 128)
         held[top + u * width : top + (u + 1) * width, :] = expand[:, cols]
-        held[top + (chunk + u) * width : top + (chunk + u + 1) * width, :] = turned[:, cols]
+        held[top + (chunk + u) * width : top + (chunk + u + 1) * width, :] = shrink_t[:, cols]
     block[...] = held[...].astype(BF)
     filters[...] = jnp.zeros_like(filters)
     filters[:9, :ff] = hidden[...]
     for g in range(2):
-        filters[:9, ff + 32 * g : ff + 32 * g + 32] = values[g]
-
-
-def run_pack(devices, entry, mixing, expand, shrink, reduce_w, values, hidden):
+        filters[:9, ff + 32 * g : ff + 32 * g + 32] = values[:, g]
+
+
+def run_pack(devices, entry, mixing_t, expand, shrink_t, reduce_t, values, hidden):
     rows = rows_of_block(devices)
     return pl.pallas_call(
         pack_kernel,
@@ -698,7 +822,7 @@
         scratch_shapes=[pltpu.VMEM((rows, 128), F32)],
         compiler_params=pltpu.CompilerParams(vmem_limit_bytes=LIMIT),
         name="pack",
-    )(entry, mixing, expand, shrink, reduce_w, values, hidden)
+    )(entry, mixing_t, expand, shrink_t, reduce_t, values, hidden)
 
 
 def greet(peers):
@@ -1065,24 +1189,25 @@
         scale = factor[:, :64]
         for e in range(3):
             apply(0, e, grad[(8 + e) * width : (9 + e) * width, 64:], scale)
-        apply(1, Ellipsis, grad[11 * width : top, 64:].T, factor[:, :width])
+        apply(1, Ellipsis, grad[11 * width : top, 64:], scale)
         for u in range(chunk):
             cols = slice(u * 128, (u + 1) * 128)
             apply(2, (slice(None), cols), grad[top + u * width : top + (u + 1) * width, :], factor)
             apply(
                 3,
-                (cols, slice(None)),
-                grad[top + (chunk + u) * width : top + (chunk + u + 1) * width, :].T,
-                factor[:, :width],
+                (slice(None), cols),
+                grad[top + (chunk + u) * width : top + (chunk + u + 1) * width, :],
+                factor,
             )
-        apply(4, (slice(0, top), slice(None)), grad[:top, :64], scale)
-        apply(4, (slice(top, 20 * width), slice(None)), grad[: 8 * width, 64:], scale)
+        turned = grad[:top, :].T
+        apply(4, (slice(None), slice(0, top)), turned[:64, :], factor[:, :1])
+        apply(4, (slice(None), slice(top, 20 * width)), turned[64:, : 8 * width], factor[:, :1])
         for n in range(2):
             apply(5, n, small[4 * n : 4 * n + 4, :], factor)
         values = small[8:17, :]
         values = jnp.where(head[0] == 1, pltpu.roll(values, 64, 1), values)
         for g in range(2):
-            apply(6, g, values[:, 32 * g : 32 * g + 32], factor[:, :32])
+            apply(6, (slice(None), g), values[:, 32 * g : 32 * g + 32], factor[:, :32])
         for u in range(chunk):
             apply(
                 7,
@@ -1159,14 +1284,27 @@
 ):
     devices = lax.axis_size("dp")
     head = lax.axis_index("head").reshape(1).astype(jnp.int32)
+    turns = ((1, 0), (1, 0), (1, 0), (1, 0, 2))
+    mixing, shrink, reduced, values = [
+        tuple(a.transpose(turn) for a in arrays)
+        for turn, arrays in zip(
+            turns,
+            (
+                (mixing_weight, mixing_momentum, mixing_average),
+                (shrink_weight, shrink_momentum, shrink_average),
+                (reduce_weight, reduce_momentum, reduce_average),
+                (value_filter, value_momentum, value_average),
+            ),
+        )
+    ]
     block, filters = run_pack(
         devices,
         entry_weight,
-        mixing_weight,
+        mixing[0],
         expand_weight,
-        shrink_weight,
-        reduce_weight,
-        value_filter,
+        shrink[0],
+        reduced[0],
+        values[0],
         hidden_filter,
     )
     blocks, filters = run_gather(devices, block, filters)
@@ -1180,34 +1318,30 @@
         entry_weight,
         entry_momentum,
         entry_average,
-        mixing_weight,
-        mixing_momentum,
-        mixing_average,
+        *mixing,
         expand_weight,
         expand_momentum,
         expand_average,
-        shrink_weight,
-        shrink_momentum,
-        shrink_average,
-        reduce_weight,
-        reduce_momentum,
-        reduce_average,
+        *shrink,
+        *reduced,
         norm_params,
         norm_momentum,
         norm_average,
-        value_filter,
-        value_momentum,
-        value_average,
+        *values,
         hidden_filter,
         hidden_momentum,
         hidden_average,
     )
     tokens_all = devices * tokens.shape[0] * tokens.shape[1] * tokens.shape[2]
-    return tuple(
+    results = list(
         run_update(
             tokens_all, head, out_half, out_other, input_half, input_other, grad, small, state
         )
     )
+    for n, turn in zip((1, 3, 4, 6), turns):
+        for k in range(2 + 3 * n, 5 + 3 * n):
+            results[k] = results[k].transpose(turn)
+    return tuple(results)
 
 
 def solution(mesh):

time: 258 us -> 190 us (0.74)
  local copies, waits for them, and re-layouts: 35.4 us -> 0 us
  Pallas kernels: 221 us -> 189 us
    pallas_call x1, Pallas kernels: 161 us -> 130 us  [run_block(): pl.pallas_call(kernel, out_shape=out_shape, grid_spec=pltpu.PrefetchScala...]
    pallas_call x12 -> x0, local copies, waits for them, and re-layouts: 18 us -> none  [run_update(): pl.pallas_call(kernel, out_shape=[jax.ShapeDtypeStruct(whole, BF), jax.Sh...]
    unnamed x12 -> x0, local copies, waits for them, and re-layouts: 17.4 us -> none
where the time goes in v3:
time: 190 us
  Pallas kernels  189 us (99%)
    pallas_call x1, Pallas kernels, run_block(): pl.pallas_call(kernel, out_shape=out_shape, grid_spec=pltpu.PrefetchScala...  130 us
    pallas_call x1, Pallas kernels, run_reduce(): pl.pallas_call(kernel, out_shape=[jax.ShapeDtypeStruct((rows, 128), F32),...  24.1 us
    pallas_call x1, Pallas kernels, run_gather(): pl.pallas_call(kernel, out_shape=[jax.ShapeDtypeStruct((2 * devices,) + b...  18.7 us
    pallas_call x1, Pallas kernels, run_update(): pl.pallas_call(kernel, out_shape=[jax.ShapeDtypeStruct(whole, BF), jax.Sh...  14.3 us

profile of v3, /device:TPU:0, one launch (start us, length us, event | category | flops | bytes accessed | tf_op | source)
XLA Modules:
  0.0 189.5 jit_solution(11054044027565125959)
XLA Ops:
  0.7 1.7 pack.1
  2.4 18.7 %gather.1 = (bf16[32,160,128]{2,1,0:T(8,128)(2,1)}, f32[2,16,640]{2,1,0:T(8,128)}) custom-call(bf16[160,128]{1,0:T(8,128)(2,1)} %get-tuple-element.66.refs_0_, f32[16,640]{1,0:T(8,128)} %get-tuple-element.67.refs_1_), custom_call_target="tpu_custom_call" | custom-call | tf_op jit(solution)/shard_map/gather/pallas_call | solution.py:941
  21.1 130.0 %block.1 = (bf16[8,32,32,128]{3,2,1,0:T(8,128)(2,1)}, bf16[8,32,32,128]{3,2,1,0:T(8,128)(2,1)}, f32[4,4,160,128]{3,2,1,0:T(8,128)}, bf16[4,4,160,128]{3,2,1,0:T(...) custom-call(s32[16]{0:T(128)} %refs_0_.1, s32[16]{0:T(128)} %refs_1_.1, s32[1]{0:T(128)} %bitcast.refs_2_.refs_0_, ...), custom_call_target="tpu_custom_call" | custom-call | tf_op jit(solution)/shard_map/block/pallas_call | solution.py:725
  151.2 24.1 %reduce.1 = (f32[160,128]{1,0:T(8,128)}, f32[64,128]{1,0:T(8,128)}, bf16[8,32,32,128]{3,2,1,0:T(8,128)(2,1)}, bf16[8,32,32,128]{3,2,1,0:T(8,128)(2,1)}) custom-call(f32[4,4,160,128]{3,2,1,0:T(8,128)} %get-tuple-element.71.refs_0_, bf16[4,4,160,128]{3,2,1,0:T(8,128)(2,1)} %get-tuple-element.72.refs_1_, f32[64,128]{1,0:T(8,128)} %get-tuple-element.73.refs_2_, ...), custom_call_target="tpu_custom_call" | custom-call | tf_op jit(solution)/shard_map/reduce/pallas_call | solution.py:1107
  175.3 14.3 %update.1 = (bf16[16,32,32,128]{3,2,1,0:T(8,128)(2,1)}, f32[16,32,32,128]{3,2,1,0:T(8,128)}, f32[3,8,64]{2,1,0:T(8,128)}, f32[3,8,64]{2,1,0:T(8,128)}, f32[3,8,6...) custom-call(s32[1]{0:T(128)} %bitcast.refs_2_.refs_0_, ...), custom_call_target="tpu_custom_call" | custom-call | tf_op jit(solution)/shard_map/update/pallas_call | solution.py:1237

commit v4 on v3

--- a/solution.py
+++ b/solution.py
@@ -135,6 +135,7 @@
     edge,
     out,
     input_grad,
+    input_low,
     mine,
     theirs,
     small_mine,
@@ -161,8 +162,8 @@
     folds,
     d_key_value,
     reduce_low,
-    im2col,
-    im2col_t,
+    rows_in,
+    rows_in_t,
     middle_s,
     up_s,
     unit1_s,
@@ -181,6 +182,7 @@
     narrow_cells,
     narrow_scale,
     second_grad_s,
+    factor_s,
     *,
     steps,
 ):
@@ -199,6 +201,12 @@
     @pl.when(step == 0)
     def prepare():
         top, chunk = 12 * width, ff // 256
+        counts = jnp.zeros((1, 128), F32)
+        last_rows = packed.shape[1] - 16
+        for n in range(2 * devices):
+            pair = packed[n, last_rows : last_rows + 16, :].astype(F32)
+            counts = counts + (pair[:1] + 256.0 * pair[1:2])
+        factor_s[...] = (devices * 2 * steps * 1024 / 64) / counts
         for d in range(devices):
             one, two = [packed[2 * d + h].astype(F32) for h in range(2)]
             mask = left(top)
@@ -229,11 +237,17 @@
             filters[0, :9, ff // 2 :],
             pltpu.roll(filters[1, :9, ff // 2 :], 64, 1),
         )
-        for tap in range(9):
-            gain = hidden_filter[tap : tap + 1, :]
-            if tap == 4:
-                gain = gain + 1.0
-            conv_w[tap * 128 : (tap + 1) * 128, :] = (expand[...] * (gain * ROOT)).astype(BF)
+        for column in range(3):
+            top, mid, low = [
+                hidden_filter[3 * a + column : 3 * a + column + 1, :] * ROOT for a in range(3)
+            ]
+            if column == 1:
+                mid = mid + ROOT
+            rows = slice(column * 128, column * 128 + 128)
+            for n, gain in enumerate(
+                (top, 0.5 * (top + mid + low), 0.5 * (top - mid + low), low)
+            ):
+                conv_w[n, rows, :] = (expand[...] * gain).astype(BF)
         for g in range(2):
             w = entry[1 + g].astype(F32)
             if g == 0:
@@ -258,17 +272,19 @@
             [rows[:, q * 128 : q * 128 + 128].reshape(16, 16, 128) for q in range(4)], 1
         ).reshape(1024, 128)
 
-    def restore(value, ref, place):
+    def restore(value, ref, place, wide=None):
         blocks = value.reshape(16, 4, 16, 128)
         rows = mm(
             perm_t[...],
             jnp.concatenate([blocks[:, q].reshape(256, 128) for q in range(4)], 1),
-        ).astype(BF)
+        )
         for q in range(4):
             a, b = q // 2, q % 2
-            ref[pl.ds(place, 1), a * 16 : a * 16 + 16, b * 16 : b * 16 + 16, :] = rows[
-                :, q * 128 : q * 128 + 128
-            ].reshape(1, 16, 16, 128)
+            index = (pl.ds(place, 1), slice(a * 16, a * 16 + 16), slice(b * 16, b * 16 + 16))
+            part = rows[:, q * 128 : q * 128 + 128]
+            ref[index] = part.astype(BF).reshape(1, 16, 16, 128)
+            if wide is not None:
+                wide[index] = (part * factor_s[...]).reshape(1, 16, 16, 128)
 
     def of_quadrant(value, q, blocks):
         return value.reshape(blocks, 4, 16, 128)[:, q].reshape(blocks * 16, 128)
@@ -330,26 +346,49 @@
         fine = fine_of(grid)
         alive = live_images[first_grid + grid]
         x = ordered(tokens, slot)
+        yield
+        raised = ordered(cotangent, slot)
+        yield
         unit1, scale1 = normalise(x)
         unit1_s[slot] = unit1
         scale1_s[slot] = scale1
+        yield
         normed = (unit1 * gain(0) + shift_by(0)).astype(BF)
         normed_s[slot] = normed
         yield
+        reduced = [mm(patches_of(slot, g), reduce_low[rows_of[g], :]) for g in range(2)]
+        yield
         queries_s[slot] = mm(normed, entry[0]).astype(BF)
-        keys, values = [], []
+        yield
+        cells = [normalise(reduced[g]) for g in range(2)]
+        yield
+        row16 = lax.broadcasted_iota(jnp.int32, (16, 128), 0)
+        within = (row16 // 8) * 4 + (row16 % 4) // 2
+        live = jnp.stack(
+            [
+                jnp.where(
+                    jnp.where(fine == 1, within + (q // 2) * 8 + (q % 2) * 2, q) < alive, 1.0, 0.0
+                )
+                for q in range(4)
+            ],
+            0,
+        )
+        up_s[slot] = (raised.reshape(16, 4, 16, 128) * live[None]).reshape(1024, 128).astype(BF)
+        yield
+        acts = []
         for g in range(2):
-            reduced = mm(patches_of(slot, g), reduce_low[rows_of[g], :])
-            unit, scale = normalise(reduced)
+            unit, scale = cells[g]
             act, slope = gelu_pair(unit * gain(1 + g) + shift_by(1 + g))
             cells_f[g][slot, 0] = unit
             cells_f[g][slot, 1] = slope
             cells_f[g][slot, 2] = act
             cells_scale[g][slot] = scale
-            pair = mm(act.astype(BF), key_value_w[g])
-            keys.append(pair[:, :128].astype(BF))
-            values.append(pair[:, 128:])
-            yield
+            acts.append(act.astype(BF))
+        yield
+        pairs = [mm(acts[g], key_value_w[g]) for g in range(2)]
+        yield
+        keys = [pair[:, :128].astype(BF) for pair in pairs]
+        values = [pair[:, 128:] for pair in pairs]
         keys_all = [
             jnp.concatenate([keys[0][q * 16 : q * 16 + 16], of_quadrant(keys[1], q, 4)], 0)
             for q in range(4)
@@ -410,42 +449,28 @@
         second_f = second_low.astype(F32)
         yield
         moved_blocks = {}
-        for block in range(16):
+
+        def neighbour(block, down, across):
             a4, b4 = place_of(block)
-            for tap in range(9):
-                na, wa = wrap(a4, tap // 3 - 1)
-                nb, wb = wrap(b4, tap % 3 - 1)
-                source = block_of(na, nb)
-                key = (source, wa, wb)
-                if key not in moved_blocks:
-                    rows = slice(source * 64, source * 64 + 64)
-                    if wa or wb:
-                        moved_blocks[key] = move(second_f[rows], fine, wa, wb).astype(BF)
-                    else:
-                        moved_blocks[key] = second_low[rows]
-                im2col[slot, block * 64 : block * 64 + 64, tap * 128 : tap * 128 + 128] = (
-                    moved_blocks[key]
-                )
+            na, wa = wrap(a4, down)
+            nb, wb = wrap(b4, across)
+            key = (block_of(na, nb), wa, wb)
+            if key not in moved_blocks:
+                rows = second_f[key[0] * 64 : key[0] * 64 + 64]
+                moved_blocks[key] = move(rows, fine, wa, wb) if wa or wb else rows
+            return moved_blocks[key]
+
+        for block in range(8):
+            for column in range(3):
+                above, first, second = [neighbour(block, d, column - 1) for d in (-1, 0, 1)]
+                below = neighbour(block + 8, 1, column - 1)
+                for n, part in enumerate(
+                    (above - second, first + second, second - first, below - first)
+                ):
+                    rows_in[
+                        slot, n, block * 64 : block * 64 + 64, column * 128 : column * 128 + 128
+                    ] = part.astype(BF)
             yield
-        row16 = lax.broadcasted_iota(jnp.int32, (16, 128), 0)
-        within = (row16 // 8) * 4 + (row16 % 4) // 2
-        live = jnp.stack(
-            [
-                jnp.where(
-                    jnp.where(fine == 1, within + (q // 2) * 8 + (q % 2) * 2, q) < alive, 1.0, 0.0
-                )
-                for q in range(4)
-            ],
-            0,
-        )
-        up_low = (
-            (ordered(cotangent, slot).reshape(16, 4, 16, 128) * live[None])
-            .reshape(1024, 128)
-            .astype(BF)
-        )
-        up_s[slot] = up_low
-        yield
-
     def feed(slot, grid):
         fine = fine_of(grid)
         total = middle_s[slot]
@@ -454,46 +479,68 @@
         for c in range(0, ff + wide, wide):
             if c < ff:
                 cols = slice(c, c + wide)
-                hidden = mm(im2col[slot], conv_w[:, cols])
-                grad = mm(up_s[slot], shrink_t[:, cols])
+                m = [mm(rows_in[slot, n], conv_w[n, :, cols]) for n in range(4)]
+                inner = m[1] + m[0]
+                hidden = (inner + m[2], m[1] - m[2] + m[3])
+                grads = [
+                    mm(up_s[slot, h * 512 : h * 512 + 512, :], shrink_t[:, cols]) for h in range(2)
+                ]
             if c == 0:
-                for tap in range(9):
-                    im2col_t[tap * 128 : tap * 128 + 128, :] = im2col[
-                        slot, :, tap * 128 : tap * 128 + 128
-                    ].T
+                for n in range(4):
+                    for column in range(3):
+                        rows = slice(column * 128, column * 128 + 128)
+                        rows_in_t[n, rows, :] = rows_in[slot, n, :, rows].T
                 up_t = up_s[slot].T
             if held:
-                before, act, back = held
+                before, act, backs = held
                 total = total + mm(act, shrink_t[:, before], NT)
                 d_shrink_t[:, before] += mm(up_t, act)
-                m_sum[:, before] += mm(im2col_t[...], back)
+                for n in range(4):
+                    m_sum[n, :, before] += mm(rows_in_t[n], backs[n])
             if c < ff:
-                act, slope = scaled_gelu_pair(hidden)
-                act = act.astype(BF)
-                grad = (grad * slope).astype(BF)
-                g_low[:, cols] = grad
-                held = (cols, act, grad)
+                acts, gs = [], []
+                for h in range(2):
+                    act, slope = scaled_gelu_pair(hidden[h])
+                    acts.append(act.astype(BF))
+                    gs.append(grads[h] * slope)
+                act = jnp.concatenate(acts, 0)
+                backs = [
+                    v.astype(BF) for v in (gs[0], gs[0] + gs[1], gs[0] - gs[1], gs[1])
+                ]
+                for n in range(4):
+                    g_low[n, :, cols] = backs[n]
+                held = (cols, act, backs)
         restore(total.astype(BF), out, slot)
-        for t in range(0, 9, 2):
-            rows = slice(t * 128, min(t + 2, 9) * 128)
-            folds[:, rows] = mm(g_low[...], conv_w[rows, :], NT)
+        for n in range(4):
+            folds[n] = mm(g_low[n], conv_w[n], NT)
         sums = {}
-        for block in range(16):
-            a4, b4 = place_of(block)
-            for tap in range(9):
-                na, wa = wrap(a4, tap // 3 - 1)
-                nb, wb = wrap(b4, tap % 3 - 1)
-                key = (block_of(na, nb), wa, wb)
-                sums.setdefault(key, []).append((block, tap))
+        for block in range(8):
+            for column in range(3):
+                for down, other, terms in (
+                    (-1, block, ((0, 1),)),
+                    (0, block, ((1, 1), (2, -1), (3, -1))),
+                    (1, block, ((1, 1), (2, 1), (0, -1))),
+                    (1, block + 8, ((3, 1),)),
+                ):
+                    a4, b4 = place_of(other)
+                    na, wa = wrap(a4, down)
+                    nb, wb = wrap(b4, column - 1)
+                    key = (block_of(na, nb), wa, wb)
+                    sums.setdefault(key, []).extend((block, column, n, sign) for n, sign in terms)
         for block in range(16):
             total = None
             for (source, wa, wb), terms in sums.items():
                 if source != block:
                     continue
                 part = None
-                for other, tap in terms:
-                    term = folds[other * 64 : other * 64 + 64, tap * 128 : tap * 128 + 128]
-                    part = term if part is None else part + term
+                for other, column, n, sign in terms:
+                    term = folds[
+                        n, other * 64 : other * 64 + 64, column * 128 : column * 128 + 128
+                    ]
+                    if part is None:
+                        part = term if sign > 0 else -term
+                    else:
+                        part = part + term if sign > 0 else part - term
                 if wa or wb:
                     part = move(part, fine, -wa, -wb)
                 total = part if total is None else total + part
@@ -509,10 +556,10 @@
         )
         middle_low = middle_grad.astype(BF)
         yield
-        mixed = mixed_s[slot]
-        d_mixing_t[...] += mm(middle_low, mixed, TN)
         mixed_grad = mm(middle_low, mixing_t[...]).astype(BF)
         queries = queries_s[slot]
+        yield
+        d_mixing_t[...] += mm(middle_low, mixed_s[slot], TN)
         yield
         out_grads = [of_quadrant(mixed_grad, q, 16) for q in range(4)]
         prob_grads = [mm(enhanced_s[slot, q], out_grads[q], NT) for q in range(4)]
@@ -556,44 +603,46 @@
         value_grad = value_grad.astype(BF)
         value_parts = [value_grad[:, q * 128 : q * 128 + 128] for q in range(4)]
         yield
-        normed = normed_s[slot]
+        narrow = [jnp.concatenate([p[:16] for p in parts], 0) for parts in (key_parts, value_parts)]
+        wide = [of_quadrants([p[16:] for p in parts], 4) for parts in (key_parts, value_parts)]
+        pairs = [jnp.concatenate(sides, 1) for sides in (narrow, wide)]
+        cell_grads = [mm(pairs[g], key_value_w[g], NT) for g in range(2)]
+        yield
         normed_grad = mm(query_low, entry[0], NT)
-        d_entry[0] += mm(normed, query_low, TN)
-        yield
+        yield
+        reduced_lows = []
         for g in range(2):
-            if g == 0:
-                sides = [
-                    jnp.concatenate([p[:16] for p in parts], 0)
-                    for parts in (key_parts, value_parts)
-                ]
-            else:
-                sides = [
-                    of_quadrants([p[16:] for p in parts], 4) for parts in (key_parts, value_parts)
-                ]
-            pair = jnp.concatenate(sides, 1)
             unit, slope = cells_f[g][slot, 0], cells_f[g][slot, 1]
-            cell_low = cells_f[g][slot, 2].astype(BF)
-            d_key_value[g] += mm(cell_low, pair, TN)
-            cell_grad = mm(pair, key_value_w[g], NT) * slope
+            cell_grad = cell_grads[g] * slope
             add_norm(1 + g, cell_grad, unit)
-            reduced_low = normalise_back(
-                cell_grad * gain(1 + g), unit, cells_scale[g][slot]
-            ).astype(BF)
-            d_reduce_t[:, rows_of[g]] += mm(reduced_low, patches_of(slot, g), TN)
-            spread = mm(reduced_low, reduce_low[rows_of[g], :], NT)
+            reduced_lows.append(
+                normalise_back(cell_grad * gain(1 + g), unit, cells_scale[g][slot]).astype(BF)
+            )
+        yield
+        d_entry[0] += mm(normed_s[slot], query_low, TN)
+        yield
+        spreads = [mm(reduced_lows[g], reduce_low[rows_of[g], :], NT) for g in range(2)]
+        yield
+        for g in range(2):
+            d_key_value[g] += mm(cells_f[g][slot, 2].astype(BF), pairs[g], TN)
+        yield
+        for g in range(2):
             if g == 0:
                 order = [place_of(block) for block in range(16)]
                 order = [a4 * 4 + b4 for a4, b4 in order]
             else:
                 order = range(4)
             normed_grad = normed_grad + jnp.concatenate(
-                [spread[:, t * 128 : t * 128 + 128] for t in order], 0
+                [spreads[g][:, t * 128 : t * 128 + 128] for t in order], 0
             )
-            yield
+        yield
+        for g in range(2):
+            d_reduce_t[:, rows_of[g]] += mm(reduced_lows[g], patches_of(slot, g), TN)
+        yield
         unit1 = unit1_s[slot]
         add_norm(0, normed_grad, unit1)
         raw = middle_grad + normalise_back(normed_grad * gain(0), unit1, scale1_s[slot])
-        restore(raw.astype(BF), input_grad, slot)
+        restore(raw.astype(BF), input_low, slot, input_grad)
         yield
 
     def together(*parts):
@@ -613,18 +662,31 @@
 
     @pl.when(step == last)
     def finish():
-        for c in range(0, ff, 256):
-            cols = slice(c, c + 256)
-            weight = expand[:, cols]
-            total = None
+        gains = [hidden_filter[tap : tap + 1, :] * ROOT for tap in range(9)]
+        gains[4] = gains[4] + ROOT
+        for c in range(0, ff, 128):
+            cols = slice(c, c + 128)
+            taps = [None] * 9
+            for r in range(0, 128, 64):
+                weight = expand[r : r + 64, cols]
+                total = None
+                for column in range(3):
+                    rows = slice(column * 128 + r, column * 128 + r + 64)
+                    one, two = m_sum[1, rows, cols], m_sum[2, rows, cols]
+                    both = (one + two) * 0.5
+                    for a in range(3):
+                        if a == 1:
+                            part = (one - two) * 0.5
+                        else:
+                            part = m_sum[a // 2 * 3, rows, cols] + both
+                        tap = 3 * a + column
+                        row = jnp.sum(part * weight, 0, keepdims=True)
+                        taps[tap] = row if taps[tap] is None else taps[tap] + row
+                        part = part * gains[tap][:, cols]
+                        total = part if total is None else total + part
+                wide_s[0, r : r + 64, cols] = total
             for tap in range(9):
-                part = m_sum[tap * 128 : tap * 128 + 128, cols] * ROOT
-                factor = hidden_filter[tap : tap + 1, cols]
-                if tap == 4:
-                    factor = factor + 1.0
-                hidden_filter[tap : tap + 1, cols] = jnp.sum(part * weight, 0, keepdims=True)
-                total = part * factor if total is None else total + part * factor
-            wide_s[0, :, cols] = total
+                hidden_filter[tap : tap + 1, cols] = taps[tap] * ROOT
         wide_s[1] = d_shrink_t[...]
         d_entry[1] = jnp.where(
             first_lanes, d_key_value[0, :, :128], pltpu.roll(d_key_value[0, :, 128:], 32, 1)
@@ -638,10 +700,10 @@
             rows = slice(n * 128, n * 128 + 128)
             d_reduce[rows, :] = d_reduce_t[:, rows].T
         top, chunk = 12 * width, ff // 256
-        planes, lines = mine.shape[0], mine.shape[1]
+        planes = mine.shape[1]
 
         def put(d, rows, first, second):
-            place = (d % planes, d // planes, rows)
+            place = (d // planes, d % planes, rows)
             mine[place] = jnp.where(is_second, second, first)
             theirs[place] = jnp.where(is_second, first, second).astype(BF)
 
@@ -691,7 +753,7 @@
 
 def run_block(resolution, live_images, head, tokens, cotangent, packed, filters, norms):
     steps = tokens.shape[0] // 2
-    devices, rows = packed.shape[0] // 2, packed.shape[1]
+    devices, rows = packed.shape[0] // 2, packed.shape[1] - 16
     ff = 2 * (filters.shape[2] - 128)
     lines = line_of(devices)
     consts = [
@@ -711,10 +773,11 @@
     )
     grid_out = pl.BlockSpec((PAIR, 32, 32, 128), lambda i, *_: (i, 0, 0, 0))
     out_shape = [
+        jax.ShapeDtypeStruct((2 * steps, 32, 32, 128), BF),
+        jax.ShapeDtypeStruct((2 * steps, 32, 32, 128), F32),
         jax.ShapeDtypeStruct((steps, 32, 32, 128), BF),
-        jax.ShapeDtypeStruct((steps, 32, 32, 128), BF),
-        jax.ShapeDtypeStruct((devices // lines, lines, rows, 128), F32),
-        jax.ShapeDtypeStruct((devices // lines, lines, rows, 128), BF),
+        jax.ShapeDtypeStruct((lines, devices // lines, rows, 128), F32),
+        jax.ShapeDtypeStruct((lines, devices // lines, rows, 128), BF),
         jax.ShapeDtypeStruct((SMALL, 128), F32),
         jax.ShapeDtypeStruct((SMALL, 128), F32),
     ]
@@ -729,7 +792,7 @@
             num_scalar_prefetch=3,
             grid=(steps // PAIR,),
             in_specs=[grid_in, grid_in] + [all_of(a) for a in whole],
-            out_specs=[grid_out, grid_out] + [all_of(a) for a in out_shape[2:]],
+            out_specs=[grid_in, grid_in, grid_out] + [all_of(a) for a in out_shape[3:]],
             scratch_shapes=[
                 pltpu.VMEM((3, 128, 128), BF),
                 pltpu.VMEM((128, 128), BF),
@@ -746,15 +809,15 @@
                 pltpu.VMEM((128, 2560), F32),
                 pltpu.VMEM((8, 128), F32),
                 pltpu.VMEM((9, 128), F32),
-                pltpu.VMEM((1152, ff), BF),
+                pltpu.VMEM((4, 384, ff), BF),
                 pltpu.VMEM((2, 128, 256), BF),
-                pltpu.VMEM((1024, ff), BF),
-                pltpu.VMEM((1152, ff), F32),
-                pltpu.VMEM((1024, 1152), F32),
+                pltpu.VMEM((4, 512, ff), BF),
+                pltpu.VMEM((4, 384, ff), F32),
+                pltpu.VMEM((4, 512, 384), F32),
                 pltpu.VMEM((2, 128, 256), F32),
                 pltpu.VMEM((2560, 128), BF),
-                pltpu.VMEM((2, 1024, 1152), BF),
-                pltpu.VMEM((1152, 1024), BF),
+                pltpu.VMEM((2, 4, 512, 384), BF),
+                pltpu.VMEM((4, 384, 512), BF),
                 pltpu.VMEM((2, 1024, 128), F32),
                 pltpu.VMEM((2, 1024, 128), BF),
                 pltpu.VMEM((2, 1024, 128), F32),
@@ -773,6 +836,7 @@
                 pltpu.VMEM((2, 3, 256, 128), F32),
                 pltpu.VMEM((2, 256, 1), F32),
                 pltpu.VMEM((2, 1024, 128), F32),
+                pltpu.VMEM((1, 128), F32),
             ],
         ),
         compiler_params=pltpu.CompilerParams(
@@ -790,7 +854,7 @@
     return -(-20 * (128 // devices) // 16) * 16
 
 
-def pack_kernel(entry, mixing_t, expand, shrink_t, reduce_t, values, hidden, block, filters, held):
+def pack_kernel(resolution, live_images, head, entry, mixing_t, expand, shrink_t, reduce_t, values, hidden, block, filters, held):
     width, ff = expand.shape
     top, chunk = 12 * width, ff // 128
     held[...] = jnp.zeros_like(held)
@@ -804,6 +868,15 @@
         cols = slice(u * 128, (u + 1) * 128)
         held[top + u * width : top + (u + 1) * width, :] = expand[:, cols]
         held[top + (chunk + u) * width : top + (chunk + u + 1) * width, :] = shrink_t[:, cols]
+    half = live_images.shape[0] // 2
+    count = jnp.int32(0)
+    for n in range(half):
+        side = resolution[head[0] * half + n]
+        count = count + side * side * live_images[head[0] * half + n]
+    count = count // 64
+    last = held.shape[0] - 16
+    held[last : last + 1, :] = jnp.full((1, 128), count % 256, jnp.int32).astype(F32)
+    held[last + 1 : last + 2, :] = jnp.full((1, 128), count // 256, jnp.int32).astype(F32)
     block[...] = held[...].astype(BF)
     filters[...] = jnp.zeros_like(filters)
     filters[:9, :ff] = hidden[...]
@@ -811,18 +884,24 @@
         filters[:9, ff + 32 * g : ff + 32 * g + 32] = values[:, g]
 
 
-def run_pack(devices, entry, mixing_t, expand, shrink_t, reduce_t, values, hidden):
-    rows = rows_of_block(devices)
+def run_pack(
+    devices, resolution, live_images, head, entry, mixing_t, expand, shrink_t, reduce_t, values, hidden
+):
+    rows = rows_of_block(devices) + 16
+    smem = pl.BlockSpec(memory_space=pltpu.SMEM)
+    vmem = pl.BlockSpec(memory_space=pltpu.VMEM)
     return pl.pallas_call(
         pack_kernel,
         out_shape=[
             jax.ShapeDtypeStruct((rows, 128), BF),
             jax.ShapeDtypeStruct((16, hidden.shape[1] + 128), F32),
         ],
+        in_specs=[smem] * 3 + [vmem] * 7,
+        out_specs=[vmem] * 2,
         scratch_shapes=[pltpu.VMEM((rows, 128), F32)],
         compiler_params=pltpu.CompilerParams(vmem_limit_bytes=LIMIT),
         name="pack",
-    )(entry, mixing_t, expand, shrink_t, reduce_t, values, hidden)
+    )(resolution, live_images, head, entry, mixing_t, expand, shrink_t, reduce_t, values, hidden)
 
 
 def greet(peers):
@@ -974,7 +1053,6 @@
     plane_out,
     plane_in,
     plane_small,
-    line_sum,
     line_out,
     line_in,
     line_small,
@@ -986,6 +1064,7 @@
     line_recv,
 ):
     lines, planes, z, p, head, line_peers, plane_peers = places(devices)
+    half = input_half.shape[0]
 
     def at(line, plane, core):
         return (line * planes + plane, core)
@@ -1012,46 +1091,45 @@
         copy.start()
         started.append(copy)
 
-    go(small_theirs, core_small, core_send.at[planes], core_recv.at[planes], sibling)
-    for k in plane_peers + [p]:
-        go(theirs.at[k], core_in.at[k], core_send.at[k], core_recv.at[k], sibling)
+    order = line_peers + [z]
+    go(small_theirs, core_small, core_send.at[lines], core_recv.at[lines], sibling)
+    for a in order:
+        go(theirs.at[a], core_in.at[a], core_send.at[a], core_recv.at[a], sibling)
     remote(
-        small_theirs, core_small, core_send.at[planes], core_recv.at[planes], sibling
+        small_theirs, core_small, core_send.at[lines], core_recv.at[lines], sibling
     ).wait_recv()
     plane_small[pl.ds(p, 1)] = (small_mine[...] + core_small[...])[None]
     for n, k in enumerate(plane_peers):
         go(
             plane_small.at[p],
             plane_small.at[p],
-            plane_send.at[planes + n],
-            plane_recv.at[planes + p],
+            plane_send.at[lines * (planes - 1) + n],
+            plane_recv.at[lines * planes + p],
             at(z, k, head),
         )
-    for n, k in enumerate(plane_peers):
+    for m, a in enumerate(order):
         remote(
-            theirs.at[k], core_in.at[k], core_send.at[k], core_recv.at[k], sibling
+            theirs.at[a], core_in.at[a], core_send.at[a], core_recv.at[a], sibling
         ).wait_recv()
-        plane_out[pl.ds(k, 1)] = (mine[pl.ds(k, 1)] + core_in[pl.ds(k, 1)].astype(F32)).astype(BF)
-        go(plane_out.at[k], plane_in.at[p], plane_send.at[n], plane_recv.at[p], at(z, k, head))
-    remote(theirs.at[p], core_in.at[p], core_send.at[p], core_recv.at[p], sibling).wait_recv()
-    go(out_half, out_other, core_send.at[planes + 1], core_recv.at[planes + 1], sibling)
-    go(input_half, input_other, core_send.at[planes + 2], core_recv.at[planes + 2], sibling)
-    total = mine[pl.ds(p, 1)][0] + core_in[pl.ds(p, 1)][0].astype(F32)
-    for k in plane_peers:
-        remote(
-            plane_out.at[k], plane_in.at[k], plane_send.at[0], plane_recv.at[k], sibling
-        ).wait_recv()
-        total = total + plane_in[pl.ds(k, 1)][0].astype(F32)
-    line_sum[...] = total
-    for n, k in enumerate(line_peers):
-        line_out[pl.ds(k, 1)] = line_sum[pl.ds(k, 1)].astype(BF)
-        go(line_out.at[k], line_in.at[z], line_send.at[n], line_recv.at[z], at(k, p, head))
+        both = mine[pl.ds(a, 1)] + core_in[pl.ds(a, 1)].astype(F32)
+        plane_out[pl.ds(a, 1)] = both.astype(BF)
+        for n, k in enumerate(plane_peers):
+            go(
+                plane_out.at[a, k],
+                plane_in.at[a, p],
+                plane_send.at[m * (planes - 1) + n],
+                plane_recv.at[a * planes + p],
+                at(z, k, head),
+            )
+    own_out = out_half.at[pl.ds(head * half, half)]
+    go(own_out, out_other, core_send.at[lines + 1], core_recv.at[lines + 1], sibling)
+    go(input_half, input_other, core_send.at[lines + 2], core_recv.at[lines + 2], sibling)
     for k in plane_peers:
         remote(
             plane_small.at[p],
             plane_small.at[k],
             plane_send.at[0],
-            plane_recv.at[planes + k],
+            plane_recv.at[lines * planes + k],
             sibling,
         ).wait_recv()
     part = plane_small[0]
@@ -1066,7 +1144,25 @@
             line_recv.at[lines + z],
             at(k, p, head),
         )
-    own = line_sum[pl.ds(z, 1)][0]
+    own = None
+    for m, a in enumerate(order):
+        total = (
+            mine[pl.ds(a, 1), pl.ds(p, 1)] + core_in[pl.ds(a, 1), pl.ds(p, 1)].astype(F32)
+        )[0, 0]
+        for k in plane_peers:
+            remote(
+                plane_out.at[a, k],
+                plane_in.at[a, k],
+                plane_send.at[0],
+                plane_recv.at[a * planes + k],
+                sibling,
+            ).wait_recv()
+            total = total + plane_in[pl.ds(a, 1), pl.ds(k, 1)][0, 0].astype(F32)
+        if m < lines - 1:
+            line_out[pl.ds(a, 1)] = total.astype(BF)[None]
+            go(line_out.at[a], line_in.at[z], line_send.at[m], line_recv.at[z], at(a, p, head))
+        else:
+            own = total
     for k in line_peers:
         remote(
             line_out.at[k], line_in.at[k], line_send.at[0], line_recv.at[k], sibling
@@ -1086,17 +1182,17 @@
         part = part + line_small[k]
     small[...] = part
     remote(
-        out_half, out_other, core_send.at[planes + 1], core_recv.at[planes + 1], sibling
+        own_out, out_other, core_send.at[lines + 1], core_recv.at[lines + 1], sibling
     ).wait_recv()
     remote(
-        input_half, input_other, core_send.at[planes + 2], core_recv.at[planes + 2], sibling
+        input_half, input_other, core_send.at[lines + 2], core_recv.at[lines + 2], sibling
     ).wait_recv()
     for copy in started:
         copy.wait_send()
 
 
 def run_reduce(devices, mine, theirs, small_mine, small_theirs, out_half, input_half):
-    planes, lines, rows = mine.shape[:3]
+    lines, planes, rows = mine.shape[:3]
     anywhere = pl.BlockSpec(memory_space=pl.ANY)
     vmem = pl.BlockSpec(memory_space=pltpu.VMEM)
     sem = pltpu.SemaphoreType.DMA
@@ -1109,25 +1205,24 @@
         out_shape=[
             jax.ShapeDtypeStruct((rows, 128), F32),
             jax.ShapeDtypeStruct((SMALL, 128), F32),
-            jax.ShapeDtypeStruct(out_half.shape, BF),
+            jax.ShapeDtypeStruct(input_half.shape, BF),
             jax.ShapeDtypeStruct(input_half.shape, BF),
         ],
         in_specs=[vmem] * 4 + [anywhere] * 2,
         out_specs=[vmem] * 2 + [anywhere] * 2,
         scratch_shapes=[
-            pltpu.VMEM((planes, lines, rows, 128), BF),
+            pltpu.VMEM((lines, planes, rows, 128), BF),
             pltpu.VMEM((SMALL, 128), F32),
-            pltpu.VMEM((planes, lines, rows, 128), BF),
-            pltpu.VMEM((planes, lines, rows, 128), BF),
+            pltpu.VMEM((lines, planes, rows, 128), BF),
+            pltpu.VMEM((lines, planes, rows, 128), BF),
             pltpu.VMEM((planes, SMALL, 128), F32),
-            pltpu.VMEM((lines, rows, 128), F32),
             pltpu.VMEM((lines, rows, 128), BF),
             pltpu.VMEM((lines, rows, 128), BF),
             pltpu.VMEM((lines, SMALL, 128), F32),
-            sem((planes + 3,)),
-            sem((planes + 3,)),
-            sem((2 * planes,)),
-            sem((2 * planes,)),
+            sem((lines + 3,)),
+            sem((lines + 3,)),
+            sem((lines * (planes - 1) + planes,)),
+            sem((lines * planes + planes,)),
             sem((2 * lines,)),
             sem((2 * lines,)),
         ],
@@ -1149,24 +1244,14 @@
 
 
 def update_kernel(head, *refs, tokens_all):
-    out_own, out_other, in_own, in_other, grad, small = refs[:6]
+    out_other, in_other, grad, small = refs[:4]
     state = refs[6:30]
     output, input_grad = refs[30:32]
     results = refs[32:]
     step = pl.program_id(0)
-    half = pl.num_programs(0) // 2
     factor = tokens_all / small[17:18, :]
-    is_own = (step // half) == head[0]
-
-    @pl.when(is_own)
-    def own():
-        output[...] = out_own[...]
-        input_grad[...] = in_own[...].astype(F32) * factor
-
-    @pl.when(jnp.logical_not(is_own))
-    def other():
-        output[...] = out_other[...]
-        input_grad[...] = in_other[...].astype(F32) * factor
+    output[...] = out_other[...]
+    input_grad[...] = in_other[...].astype(F32) * factor
 
     @pl.when(step == 0)
     def update():
@@ -1217,39 +1302,37 @@
             )
 
 
-def run_update(tokens_all, head, out_own, out_other, in_own, in_other, grad, small, state):
-    half = out_own.shape[0]
+def run_update(tokens_all, head, output, input_grad, out_other, in_other, grad, small, state):
+    half = out_other.shape[0]
+    steps = half // PAIR
 
     def all_of(a):
         return pl.BlockSpec(a.shape, lambda i, *_, n=a.ndim: (0,) * n)
 
-    block = (1,) + out_own.shape[1:]
-    own = pl.BlockSpec(block, lambda i, head: (jnp.clip(i - head[0] * half, 0, half - 1), 0, 0, 0))
-    other = pl.BlockSpec(
-        block, lambda i, head: (jnp.clip(i - (1 - head[0]) * half, 0, half - 1), 0, 0, 0)
-    )
-    final = pl.BlockSpec(block, lambda i, *_: (i, 0, 0, 0))
-    whole = (2 * half,) + out_own.shape[1:]
+    block = (PAIR,) + out_other.shape[1:]
+    other = pl.BlockSpec(block, lambda i, *_: (i, 0, 0, 0))
+    final = pl.BlockSpec(block, lambda i, head: ((1 - head[0]) * steps + i, 0, 0, 0))
+    anywhere = pl.BlockSpec(memory_space=pl.ANY)
 
     def kernel(*refs):
         update_kernel(*refs, tokens_all=tokens_all)
 
     return pl.pallas_call(
         kernel,
-        out_shape=[jax.ShapeDtypeStruct(whole, BF), jax.ShapeDtypeStruct(whole, F32)]
-        + [jax.ShapeDtypeStruct(a.shape, F32) for a in state],
+        out_shape=[jax.ShapeDtypeStruct(a.shape, a.dtype) for a in (output, input_grad, *state)],
         grid_spec=pltpu.PrefetchScalarGridSpec(
             num_scalar_prefetch=1,
-            grid=(2 * half,),
-            in_specs=[own, other, own, other, all_of(grad), all_of(small)]
+            grid=(steps,),
+            in_specs=[other, other, all_of(grad), all_of(small), anywhere, anywhere]
             + [all_of(a) for a in state],
             out_specs=[final, final] + [all_of(a) for a in state],
         ),
+        input_output_aliases={5: 0, 6: 1},
         compiler_params=pltpu.CompilerParams(
             dimension_semantics=("arbitrary",), vmem_limit_bytes=LIMIT
         ),
         name="update",
-    )(head, out_own, out_other, in_own, in_other, grad, small, *state)
+    )(head, out_other, in_other, grad, small, output, input_grad, *state)
 
 
 def per_device(
@@ -1299,6 +1382,9 @@
     ]
     block, filters = run_pack(
         devices,
+        resolution,
+        live_images,
+        head,
         entry_weight,
         mixing[0],
         expand_weight,
@@ -1308,11 +1394,11 @@
         hidden_filter,
     )
     blocks, filters = run_gather(devices, block, filters)
-    out_half, input_half, mine, theirs, small_mine, small_theirs = run_block(
+    output, input_grad, input_low, mine, theirs, small_mine, small_theirs = run_block(
         resolution, live_images, head, tokens, cotangent, blocks, filters, norm_params
     )
     grad, small, out_other, input_other = run_reduce(
-        devices, mine, theirs, small_mine, small_theirs, out_half, input_half
+        devices, mine, theirs, small_mine, small_theirs, output, input_low
     )
     state = (
         entry_weight,
@@ -1335,7 +1421,7 @@
     tokens_all = devices * tokens.shape[0] * tokens.shape[1] * tokens.shape[2]
     results = list(
         run_update(
-            tokens_all, head, out_half, out_other, input_half, input_other, grad, small, state
+            tokens_all, head, output, input_grad, out_other, input_other, grad, small, state
         )
     )
     for n, turn in zip((1, 3, 4, 6), turns):

time: 190 us -> 160 us (0.84)
  Pallas kernels: 189 us -> 159 us
    pallas_call x1, Pallas kernels: 130 us -> 114 us  [run_block(): pl.pallas_call(kernel, out_shape=out_shape, grid_spec=pltpu.PrefetchScala...]
    pallas_call x1, Pallas kernels: 14.3 us -> 6.29 us  [run_update(): pl.pallas_call(kernel, out_shape=[jax.ShapeDtypeStruct(a.shape, a.dtype)...]
    pallas_call x1, Pallas kernels: 24.1 us -> 18.2 us  [run_reduce(): pl.pallas_call(kernel, out_shape=[jax.ShapeDtypeStruct((rows, 128), F32),...]
where the time goes in v4:
time: 160 us
  Pallas kernels  159 us (99%)
    pallas_call x1, Pallas kernels, run_block(): pl.pallas_call(kernel, out_shape=out_shape, grid_spec=pltpu.PrefetchScala...  114 us
    pallas_call x1, Pallas kernels, run_gather(): pl.pallas_call(kernel, out_shape=[jax.ShapeDtypeStruct((2 * devices,) + b...  19.5 us
    pallas_call x1, Pallas kernels, run_reduce(): pl.pallas_call(kernel, out_shape=[jax.ShapeDtypeStruct((rows, 128), F32),...  18.2 us
    pallas_call x1, Pallas kernels, run_update(): pl.pallas_call(kernel, out_shape=[jax.ShapeDtypeStruct(a.shape, a.dtype)...  6.29 us

profile of v4, /device:TPU:0, one launch (start us, length us, event | category | flops | bytes accessed | tf_op | source)
XLA Modules:
  0.0 160.0 jit_solution(18316182716328453810)
XLA Ops:
  0.7 1.8 %pack.1 = (bf16[176,128]{1,0:T(8,128)(2,1)}, f32[16,640]{1,0:T(8,128)}) custom-call(s32[16]{0:T(128)} %refs_0_.1, s32[16]{0:T(128)} %refs_1_.1, s32[1]{0:T(128)} %bitcast.head.refs_2_.refs_0_, f32[3,8,64]{2,1,0:T(8,128)} %refs_7_.3, f32[8,64]{1,0:T(8,128)} %bitcast.35, f32[8,512]{1,0:T(8,128)} %refs_13_.1, f32[8,512]{1,0:T(8,128)} %bitcast.29, ...), custom_call_target="tpu_custom_call" | custom-call | tf_op jit(solution)/shard_map/pack/pallas_call | solution.py:893
  2.4 19.5 %gather.1 = (bf16[32,176,128]{2,1,0:T(8,128)(2,1)}, f32[2,16,640]{2,1,0:T(8,128)}) custom-call(bf16[176,128]{1,0:T(8,128)(2,1)} %get-tuple-element.67.refs_0_, f32[16,640]{1,0:T(8,128)} %get-tuple-element.68.refs_1_), custom_call_target="tpu_custom_call" | custom-call | tf_op jit(solution)/shard_map/gather/pallas_call | solution.py:1020
  22.0 113.6 %block.1 = (bf16[16,32,32,128]{3,2,1,0:T(8,128)(2,1)}, f32[16,32,32,128]{3,2,1,0:T(8,128)}, bf16[8,32,32,128]{3,2,1,0:T(8,128)(2,1)}, f32[4,4,160,128]{3,2,1,0:T...) custom-call(s32[16]{0:T(128)} %refs_0_.1, s32[16]{0:T(128)} %refs_1_.1, ...), custom_call_target="tpu_custom_call" | custom-call | tf_op jit(solution)/shard_map/block/pallas_call | solution.py:788
  135.6 18.2 %reduce.1 = (f32[160,128]{1,0:T(8,128)}, f32[64,128]{1,0:T(8,128)}, bf16[8,32,32,128]{3,2,1,0:T(8,128)(2,1)}, bf16[8,32,32,128]{3,2,1,0:T(8,128)(2,1)}) custom-call(f32[4,4,160,128]{3,2,1,0:T(8,128)} %get-tuple-element.71.refs_0_, bf16[4,4,160,128]{3,2,1,0:T(8,128)(2,1)} %get-tuple-element.72.refs_1_, f32[64,128]{1,0:T(8,128)} %get-tuple-element.73.refs_2_, ...), custom_call_target="tpu_custom_call" | custom-call | tf_op jit(solution)/shard_map/reduce/pallas_call | solution.py:1203
  153.8 6.3 %update.1 = (bf16[16,32,32,128]{3,2,1,0:T(8,128)(2,1)}, f32[16,32,32,128]{3,2,1,0:T(8,128)}, f32[3,8,64]{2,1,0:T(8,128)}, f32[3,8,64]{2,1,0:T(8,128)}, f32[3,8,6...) custom-call(s32[1]{0:T(128)} %bitcast.head.refs_2_.refs_0_, ...), custom_call_target="tpu_custom_call", output_to_operand_aliasing={{0}: (5, {}), {1}: (6, {})} | custom-call | tf_op jit(solution)/shard_map/update/pallas_call | solution.py:1320

commit v5 on v4

--- a/solution.py
+++ b/solution.py
@@ -468,33 +468,38 @@
                     (above - second, first + second, second - first, below - first)
                 ):
                     rows_in[
-                        slot, n, block * 64 : block * 64 + 64, column * 128 : column * 128 + 128
+                        n,
+                        slot * 512 + block * 64 : slot * 512 + block * 64 + 64,
+                        column * 128 : column * 128 + 128,
                     ] = part.astype(BF)
             yield
-    def feed(slot, grid):
-        fine = fine_of(grid)
-        total = middle_s[slot]
+    def feed():
+        def halves(ref):
+            return [
+                jnp.concatenate([ref[k, h * 512 : h * 512 + 512, :] for k in range(PAIR)], 0)
+                for h in range(2)
+            ]
+
+        totals, ups = halves(middle_s), halves(up_s)
         wide = 256
         held = None
         for c in range(0, ff + wide, wide):
             if c < ff:
                 cols = slice(c, c + wide)
-                m = [mm(rows_in[slot, n], conv_w[n, :, cols]) for n in range(4)]
-                inner = m[1] + m[0]
-                hidden = (inner + m[2], m[1] - m[2] + m[3])
-                grads = [
-                    mm(up_s[slot, h * 512 : h * 512 + 512, :], shrink_t[:, cols]) for h in range(2)
-                ]
+                m = [mm(rows_in[n], conv_w[n, :, cols]) for n in range(4)]
+                hidden = (m[1] + m[0] + m[2], m[1] - m[2] + m[3])
+                grads = [mm(ups[h], shrink_t[:, cols]) for h in range(2)]
             if c == 0:
                 for n in range(4):
                     for column in range(3):
                         rows = slice(column * 128, column * 128 + 128)
-                        rows_in_t[n, rows, :] = rows_in[slot, n, :, rows].T
-                up_t = up_s[slot].T
+                        rows_in_t[n, rows, :] = rows_in[n, :, rows].T
+                ups_t = [ups[h].T for h in range(2)]
             if held:
-                before, act, backs = held
-                total = total + mm(act, shrink_t[:, before], NT)
-                d_shrink_t[:, before] += mm(up_t, act)
+                before, acts, backs = held
+                for h in range(2):
+                    totals[h] = totals[h] + mm(acts[h], shrink_t[:, before], NT)
+                d_shrink_t[:, before] += mm(ups_t[0], acts[0]) + mm(ups_t[1], acts[1])
                 for n in range(4):
                     m_sum[n, :, before] += mm(rows_in_t[n], backs[n])
             if c < ff:
@@ -503,16 +508,20 @@
                     act, slope = scaled_gelu_pair(hidden[h])
                     acts.append(act.astype(BF))
                     gs.append(grads[h] * slope)
-                act = jnp.concatenate(acts, 0)
                 backs = [
                     v.astype(BF) for v in (gs[0], gs[0] + gs[1], gs[0] - gs[1], gs[1])
                 ]
                 for n in range(4):
                     g_low[n, :, cols] = backs[n]
-                held = (cols, act, backs)
-        restore(total.astype(BF), out, slot)
+                held = (cols, acts, backs)
+        for k in range(PAIR):
+            total = jnp.concatenate([totals[h][k * 512 : k * 512 + 512] for h in range(2)], 0)
+            restore(total.astype(BF), out, k)
         for n in range(4):
             folds[n] = mm(g_low[n], conv_w[n], NT)
+
+    def gather_folds(slot, grid):
+        fine = fine_of(grid)
         sums = {}
         for block in range(8):
             for column in range(3):
@@ -535,7 +544,9 @@
                 part = None
                 for other, column, n, sign in terms:
                     term = folds[
-                        n, other * 64 : other * 64 + 64, column * 128 : column * 128 + 128
+                        n,
+                        slot * 512 + other * 64 : slot * 512 + other * 64 + 64,
+                        column * 128 : column * 128 + 128,
                     ]
                     if part is None:
                         part = term if sign > 0 else -term
@@ -653,11 +664,9 @@
     first = PAIR * step
     together(*[attend(k, first + k) for k in range(PAIR)])
 
-    def feed_one(k, carry):
-        feed(k, first + k)
-        return carry
-
-    lax.fori_loop(0, PAIR, feed_one, 0)
+    feed()
+    for k in range(PAIR):
+        gather_folds(k, first + k)
     together(*[back(k, first + k) for k in range(PAIR)])
 
     @pl.when(step == last)
@@ -811,13 +820,13 @@
                 pltpu.VMEM((9, 128), F32),
                 pltpu.VMEM((4, 384, ff), BF),
                 pltpu.VMEM((2, 128, 256), BF),
-                pltpu.VMEM((4, 512, ff), BF),
+                pltpu.VMEM((4, PAIR * 512, ff), BF),
                 pltpu.VMEM((4, 384, ff), F32),
-                pltpu.VMEM((4, 512, 384), F32),
+                pltpu.VMEM((4, PAIR * 512, 384), F32),
                 pltpu.VMEM((2, 128, 256), F32),
                 pltpu.VMEM((2560, 128), BF),
-                pltpu.VMEM((2, 4, 512, 384), BF),
-                pltpu.VMEM((4, 384, 512), BF),
+                pltpu.VMEM((4, PAIR * 512, 384), BF),
+                pltpu.VMEM((4, 384, PAIR * 512), BF),
                 pltpu.VMEM((2, 1024, 128), F32),
                 pltpu.VMEM((2, 1024, 128), BF),
                 pltpu.VMEM((2, 1024, 128), F32),
@@ -854,7 +863,21 @@
     return -(-20 * (128 // devices) // 16) * 16
 
 
-def pack_kernel(resolution, live_images, head, entry, mixing_t, expand, shrink_t, reduce_t, values, hidden, block, filters, held):
+def pack(
+    head,
+    resolution,
+    live_images,
+    entry,
+    mixing_t,
+    expand,
+    shrink_t,
+    reduce_t,
+    values,
+    hidden,
+    block,
+    filters,
+    held,
+):
     width, ff = expand.shape
     top, chunk = 12 * width, ff // 128
     held[...] = jnp.zeros_like(held)
@@ -871,8 +894,8 @@
     half = live_images.shape[0] // 2
     count = jnp.int32(0)
     for n in range(half):
-        side = resolution[head[0] * half + n]
-        count = count + side * side * live_images[head[0] * half + n]
+        side = resolution[head * half + n]
+        count = count + side * side * live_images[head * half + n]
     count = count // 64
     last = held.shape[0] - 16
     held[last : last + 1, :] = jnp.full((1, 128), count % 256, jnp.int32).astype(F32)
@@ -884,30 +907,12 @@
         filters[:9, ff + 32 * g : ff + 32 * g + 32] = values[:, g]
 
 
-def run_pack(
-    devices, resolution, live_images, head, entry, mixing_t, expand, shrink_t, reduce_t, values, hidden
-):
-    rows = rows_of_block(devices) + 16
-    smem = pl.BlockSpec(memory_space=pltpu.SMEM)
-    vmem = pl.BlockSpec(memory_space=pltpu.VMEM)
-    return pl.pallas_call(
-        pack_kernel,
-        out_shape=[
-            jax.ShapeDtypeStruct((rows, 128), BF),
-            jax.ShapeDtypeStruct((16, hidden.shape[1] + 128), F32),
-        ],
-        in_specs=[smem] * 3 + [vmem] * 7,
-        out_specs=[vmem] * 2,
-        scratch_shapes=[pltpu.VMEM((rows, 128), F32)],
-        compiler_params=pltpu.CompilerParams(vmem_limit_bytes=LIMIT),
-        name="pack",
-    )(resolution, live_images, head, entry, mixing_t, expand, shrink_t, reduce_t, values, hidden)
-
-
-def greet(peers):
+def greet(peers, meanwhile=None):
     barrier = pltpu.get_barrier_semaphore()
     for peer in peers:
         pl.semaphore_signal(barrier, inc=1, device_id=peer, device_id_type=MESH)
+    if meanwhile is not None:
+        meanwhile()
     pl.semaphore_wait(barrier, len(peers))
 
 
@@ -921,7 +926,27 @@
     return lines, planes, z, p, head, line_peers, plane_peers
 
 
-def gather_kernel(devices, block, filters, blocks, both, send_sem, recv_sem, filter_sem, local_sem):
+def gather_kernel(
+    devices,
+    resolution,
+    live_images,
+    entry,
+    mixing_t,
+    expand,
+    shrink_t,
+    reduce_t,
+    values,
+    hidden,
+    blocks,
+    both,
+    block,
+    filters,
+    held,
+    send_sem,
+    recv_sem,
+    filter_sem,
+    local_sem,
+):
     lines, planes, z, p, head, line_peers, plane_peers = places(devices)
 
     def slot(line, plane, core):
@@ -932,7 +957,22 @@
 
     sibling = at(z, p, 1 - head)
     greet(
-        [at(k, p, head) for k in line_peers] + [at(z, k, head) for k in plane_peers] + [sibling]
+        [at(k, p, head) for k in line_peers] + [at(z, k, head) for k in plane_peers] + [sibling],
+        lambda: pack(
+            head,
+            resolution,
+            live_images,
+            entry,
+            mixing_t,
+            expand,
+            shrink_t,
+            reduce_t,
+            values,
+            hidden,
+            block,
+            filters,
+            held,
+        ),
     )
     sends = []
 
@@ -1008,11 +1048,14 @@
         copy.wait()
 
 
-def run_gather(devices, block, filters):
+def run_gather(devices, resolution, live_images, *weights):
     lines = line_of(devices)
     planes = devices // lines
     copies = (lines - 1) + lines * (planes - 1) + lines * planes
-    anywhere = pl.BlockSpec(memory_space=pl.ANY)
+    rows = rows_of_block(devices) + 16
+    filters = (16, weights[-1].shape[1] + 128)
+    smem = pl.BlockSpec(memory_space=pltpu.SMEM)
+    vmem = pl.BlockSpec(memory_space=pltpu.VMEM)
 
     def kernel(*refs):
         gather_kernel(devices, *refs)
@@ -1020,20 +1063,25 @@
     return pl.pallas_call(
         kernel,
         out_shape=[
-            jax.ShapeDtypeStruct((2 * devices,) + block.shape, BF),
-            jax.ShapeDtypeStruct((2,) + filters.shape, F32),
+            jax.ShapeDtypeStruct((2 * devices, rows, 128), BF),
+            jax.ShapeDtypeStruct((2,) + filters, F32),
         ],
-        in_specs=[anywhere, anywhere],
-        out_specs=[anywhere, anywhere],
+        in_specs=[smem] * 2 + [vmem] * len(weights),
+        out_specs=[pl.BlockSpec(memory_space=pl.ANY)] * 2,
         scratch_shapes=[
+            pltpu.VMEM((rows, 128), BF),
+            pltpu.VMEM(filters, F32),
+            pltpu.VMEM((rows, 128), F32),
             pltpu.SemaphoreType.DMA((copies,)),
             pltpu.SemaphoreType.DMA((2 * devices,)),
             pltpu.SemaphoreType.DMA((2,)),
             pltpu.SemaphoreType.DMA((2,)),
         ],
-        compiler_params=pltpu.CompilerParams(collective_id=0, has_side_effects=True),
+        compiler_params=pltpu.CompilerParams(
+            collective_id=0, has_side_effects=True, vmem_limit_bytes=LIMIT
+        ),
         name="gather",
-    )(block, filters)
+    )(resolution, live_images, *weights)
 
 
 def reduce_kernel(
@@ -1380,11 +1428,10 @@
             ),
         )
     ]
-    block, filters = run_pack(
+    blocks, filters = run_gather(
         devices,
         resolution,
         live_images,
-        head,
         entry_weight,
         mixing[0],
         expand_weight,
@@ -1393,7 +1440,6 @@
         values[0],
         hidden_filter,
     )
-    blocks, filters = run_gather(devices, block, filters)
     output, input_grad, input_low, mine, theirs, small_mine, small_theirs = run_block(
         resolution, live_images, head, tokens, cotangent, blocks, filters, norm_params
     )

time: 160 us -> 151 us (0.944)
  Pallas kernels: 159 us -> 150 us
    pallas_call x1, Pallas kernels: 114 us -> 105 us  [run_block(): pl.pallas_call(kernel, out_shape=out_shape, grid_spec=pltpu.PrefetchScala...]
    pallas_call x2 -> x1, Pallas kernels: 21.3 us -> 20.3 us  [run_gather(): pl.pallas_call(kernel, out_shape=[jax.ShapeDtypeStruct((2 * devices, rows...]
where the time goes in v5:
time: 151 us
  Pallas kernels  150 us (99%)
    pallas_call x1, Pallas kernels, run_block(): pl.pallas_call(kernel, out_shape=out_shape, grid_spec=pltpu.PrefetchScala...  105 us
    pallas_call x1, Pallas kernels, run_gather(): pl.pallas_call(kernel, out_shape=[jax.ShapeDtypeStruct((2 * devices, rows...  20.3 us
    pallas_call x1, Pallas kernels, run_reduce(): pl.pallas_call(kernel, out_shape=[jax.ShapeDtypeStruct((rows, 128), F32),...  18.5 us
    pallas_call x1, Pallas kernels, run_update(): pl.pallas_call(kernel, out_shape=[jax.ShapeDtypeStruct(a.shape, a.dtype)...  6.29 us

profile of v5, /device:TPU:0, one launch (start us, length us, event | category | flops | bytes accessed | tf_op | source)
XLA Modules:
  0.0 151.0 jit_solution(8118184405553800760)
XLA Ops:
  0.7 20.3 %gather.1 = (bf16[32,176,128]{2,1,0:T(8,128)(2,1)}, f32[2,16,640]{2,1,0:T(8,128)}) custom-call(s32[16]{0:T(128)} %refs_0_.3, s32[16]{0:T(128)} %refs_1_.3, f32[3,8,64]{2,1,0:T(8,128)} %refs_7_.3, f32[8,64]{1,0:T(8,128)} %bitcast.35, f32[8,512]{1,0:T(8,128)} %refs_13_.1, f32[8,512]{1,0:T(8,128)} %bitcast.29, f32[64,160]{1,0:T(8,128)} %bitcast.25, ...), custom_call_target="tpu_custom_call" | custom-call | tf_op jit(solution)/shard_map/gather/pallas_call | solution.py:1063
  21.0 105.2 %block.1 = (bf16[16,32,32,128]{3,2,1,0:T(8,128)(2,1)}, f32[16,32,32,128]{3,2,1,0:T(8,128)}, bf16[8,32,32,128]{3,2,1,0:T(8,128)(2,1)}, f32[4,4,160,128]{3,2,1,0:T...) custom-call(s32[16]{0:T(128)} %refs_0_.3, s32[16]{0:T(128)} %refs_1_.3, ...), custom_call_target="tpu_custom_call" | custom-call | tf_op jit(solution)/shard_map/block/pallas_call | solution.py:797
  126.2 18.5 %reduce.1 = (f32[160,128]{1,0:T(8,128)}, f32[64,128]{1,0:T(8,128)}, bf16[8,32,32,128]{3,2,1,0:T(8,128)(2,1)}, bf16[8,32,32,128]{3,2,1,0:T(8,128)(2,1)}) custom-call(f32[4,4,160,128]{3,2,1,0:T(8,128)} %get-tuple-element.67.refs_0_, bf16[4,4,160,128]{3,2,1,0:T(8,128)(2,1)} %get-tuple-element.68.refs_1_, f32[64,128]{1,0:T(8,128)} %get-tuple-element.69.refs_2_, ...), custom_call_target="tpu_custom_call" | custom-call | tf_op jit(solution)/shard_map/reduce/pallas_call | solution.py:1251
  144.7 6.3 %update.1 = (bf16[16,32,32,128]{3,2,1,0:T(8,128)(2,1)}, f32[16,32,32,128]{3,2,1,0:T(8,128)}, f32[3,8,64]{2,1,0:T(8,128)}, f32[3,8,64]{2,1,0:T(8,128)}, f32[3,8,6...) custom-call(s32[1]{0:T(128)} %bitcast.refs_2_.refs_0_, ...), custom_call_target="tpu_custom_call", output_to_operand_aliasing={{0}: (5, {}), {1}: (6, {})} | custom-call | tf_op jit(solution)/shard_map/update/pallas_call | solution.py:1368

commit v6 on v5

--- a/solution.py
+++ b/solution.py
@@ -45,29 +45,6 @@
     return perm
 
 
-def cell_shifts():
-    places = []
-    for ci in range(4):
-        for ck in range(4):
-            places.append((0, ci, ck, ci // 2, ck // 2))
-    for ah in range(2):
-        for bh in range(2):
-            for ci in range(4):
-                for ck in range(4):
-                    places.append((1, 2 * ci + ah, 2 * ck + bh, ci // 2, ck // 2))
-    index = {p[:3]: n for n, p in enumerate(places)}
-    shifts = np.zeros((2, 9, 80, 80), np.float32)
-    for n, (g, i, k, si, sk) in enumerate(places):
-        for tap in range(9):
-            other = index.get((g, i + tap // 3 - 1, k + tap % 3 - 1))
-            if other is not None:
-                shifts[0, tap, n, other] = 1
-                if places[other][3:] == (si, sk):
-                    shifts[1, tap, n, other] = 1
-    shifts = shifts.reshape(2, 720, 80)
-    return np.concatenate([shifts, shifts], 2)
-
-
 def score_bias():
     rows = np.array([(n % 16) for _ in range(2) for n in list(range(16)) + list(range(64))])
     cols = np.arange(256) % 16
@@ -130,7 +107,6 @@
     norms,
     perm,
     perm_t,
-    shifts,
     bias,
     edge,
     out,
@@ -339,8 +315,41 @@
             ).reshape(size, 128)
         return value
 
+    def cell_moves(value, fine):
+        masks = [
+            jnp.concatenate([edge[pl.ds(fine, 1), n : n + 1][0, 0]] * 4, 1) for n in range(4)
+        ]
+        made = {}
+
+        def of(source, rows, columns):
+            if (source, rows, columns) not in made:
+                part = value[source * 16 : source * 16 + 16]
+                if rows:
+                    part = pltpu.roll(part, (-4 * rows) % 16, 0) * masks[0 if rows > 0 else 1]
+                if columns:
+                    part = pltpu.roll(part, -columns % 16, 0) * masks[2 if columns > 0 else 3]
+                made[source, rows, columns] = part
+            return made[source, rows, columns]
+
+        moved = []
+        for tap in range(9):
+            down, across = tap // 3 - 1, tap % 3 - 1
+            blocks = [of(0, down, across)]
+            for a in range(2):
+                for b in range(2):
+                    na, nb = a + down, b + across
+                    blocks.append(of(1 + na % 2 * 2 + nb % 2, na // 2, nb // 2))
+            moved.append(blocks)
+        return moved
+
     def wrap(a4, d):
         return (a4 + d) % 4, (a4 + d) // 4
+
+    def shared(rows, weight, dims=NN):
+        return None, None, rows, weight, dims
+
+    def summed(ref, place, left, right):
+        return ref, place, left, right, TN
 
     def attend(slot, grid):
         fine = fine_of(grid)
@@ -356,8 +365,9 @@
         normed = (unit1 * gain(0) + shift_by(0)).astype(BF)
         normed_s[slot] = normed
         yield
-        reduced = [mm(patches_of(slot, g), reduce_low[rows_of[g], :]) for g in range(2)]
-        yield
+        reduced = []
+        for g in range(2):
+            reduced.append((yield shared(patches_of(slot, g), reduce_low[rows_of[g], :])))
         queries_s[slot] = mm(normed, entry[0]).astype(BF)
         yield
         cells = [normalise(reduced[g]) for g in range(2)]
@@ -385,8 +395,9 @@
             cells_scale[g][slot] = scale
             acts.append(act.astype(BF))
         yield
-        pairs = [mm(acts[g], key_value_w[g]) for g in range(2)]
-        yield
+        pairs = []
+        for g in range(2):
+            pairs.append((yield shared(acts[g], key_value_w[g])))
         keys = [pair[:, :128].astype(BF) for pair in pairs]
         values = [pair[:, 128:] for pair in pairs]
         keys_all = [
@@ -403,15 +414,17 @@
             1,
         )
         values_s[slot] = values_all
-        moves = shifts[pl.ds(fine, 1)][0]
-        high = values_all.astype(BF)
-        rest = (values_all - high.astype(F32)).astype(BF)
-        moved = mm(moves, jnp.concatenate([high, rest], 0))
+        yield
+        moved = cell_moves(values_all, fine)
         taps4 = jnp.concatenate([value_filter[...]] * 4, 1)
-        enhanced = values_all
-        for tap in range(9):
-            enhanced = enhanced + moved[tap * 80 : tap * 80 + 80] * taps4[tap : tap + 1]
-        enhanced = enhanced.astype(BF)
+        yield
+        enhanced = []
+        for block in range(5):
+            total = values_all[block * 16 : block * 16 + 16]
+            for tap in range(9):
+                total = total + moved[tap][block] * taps4[tap : tap + 1]
+            enhanced.append(total)
+        enhanced = jnp.concatenate(enhanced, 0).astype(BF)
         yield
 
         def both_heads(rows):
@@ -514,11 +527,11 @@
                 for n in range(4):
                     g_low[n, :, cols] = backs[n]
                 held = (cols, acts, backs)
+        for n in range(4):
+            folds[n] = mm(g_low[n], conv_w[n], NT)
         for k in range(PAIR):
             total = jnp.concatenate([totals[h][k * 512 : k * 512 + 512] for h in range(2)], 0)
             restore(total.astype(BF), out, k)
-        for n in range(4):
-            folds[n] = mm(g_low[n], conv_w[n], NT)
 
     def gather_folds(slot, grid):
         fine = fine_of(grid)
@@ -600,25 +613,35 @@
         yield
         query_low = of_quadrants(query_parts, 16).astype(BF)
         enhanced_grad = jnp.concatenate(enhanced_parts, 1)
-        moved = mm(shifts[pl.ds(fine, 1)][0][:, :80], enhanced_grad)
+        yield
+        enhanced_grad = enhanced_grad.astype(F32)
+        moved = cell_moves(enhanced_grad, fine)
         taps4 = jnp.concatenate([value_filter[...]] * 4, 1)
-        value_grad = enhanced_grad.astype(F32)
+        yield
+        value_grad = []
+        for block in range(5):
+            total = enhanced_grad[block * 16 : block * 16 + 16]
+            for tap in range(9):
+                total = total + moved[8 - tap][block] * taps4[tap : tap + 1]
+            value_grad.append(total)
+        value_grad = jnp.concatenate(value_grad, 0).astype(BF)
+        yield
         values_all = values_s[slot]
         for tap in range(9):
-            part = moved[(8 - tap) * 80 : (8 - tap) * 80 + 80]
-            value_grad = value_grad + part * taps4[tap : tap + 1]
-            row = jnp.sum(part * values_all, 0, keepdims=True)
-            d_value[tap : tap + 1, :] += (
-                row[:, :128] + row[:, 128:256] + row[:, 256:384] + row[:, 384:]
-            )
-        value_grad = value_grad.astype(BF)
+            part = None
+            for block in range(5):
+                product = moved[8 - tap][block] * values_all[block * 16 : block * 16 + 16]
+                part = product if part is None else part + product
+            part = part[:, :128] + part[:, 128:256] + part[:, 256:384] + part[:, 384:]
+            d_value[tap : tap + 1, :] += jnp.sum(part, 0, keepdims=True)
         value_parts = [value_grad[:, q * 128 : q * 128 + 128] for q in range(4)]
         yield
         narrow = [jnp.concatenate([p[:16] for p in parts], 0) for parts in (key_parts, value_parts)]
         wide = [of_quadrants([p[16:] for p in parts], 4) for parts in (key_parts, value_parts)]
         pairs = [jnp.concatenate(sides, 1) for sides in (narrow, wide)]
-        cell_grads = [mm(pairs[g], key_value_w[g], NT) for g in range(2)]
-        yield
+        cell_grads = []
+        for g in range(2):
+            cell_grads.append((yield shared(pairs[g], key_value_w[g], NT)))
         normed_grad = mm(query_low, entry[0], NT)
         yield
         reduced_lows = []
@@ -632,11 +655,11 @@
         yield
         d_entry[0] += mm(normed_s[slot], query_low, TN)
         yield
-        spreads = [mm(reduced_lows[g], reduce_low[rows_of[g], :], NT) for g in range(2)]
-        yield
+        spreads = []
         for g in range(2):
-            d_key_value[g] += mm(cells_f[g][slot, 2].astype(BF), pairs[g], TN)
-        yield
+            spreads.append((yield shared(reduced_lows[g], reduce_low[rows_of[g], :], NT)))
+        for g in range(2):
+            yield summed(d_key_value, g, cells_f[g][slot, 2].astype(BF), pairs[g])
         for g in range(2):
             if g == 0:
                 order = [place_of(block) for block in range(16)]
@@ -648,8 +671,8 @@
             )
         yield
         for g in range(2):
-            d_reduce_t[:, rows_of[g]] += mm(reduced_lows[g], patches_of(slot, g), TN)
-        yield
+            columns = (slice(None), rows_of[g])
+            yield summed(d_reduce_t, columns, reduced_lows[g], patches_of(slot, g))
         unit1 = unit1_s[slot]
         add_norm(0, normed_grad, unit1)
         raw = middle_grad + normalise_back(normed_grad * gain(0), unit1, scale1_s[slot])
@@ -657,9 +680,27 @@
         yield
 
     def together(*parts):
-        parts = list(parts)
-        while parts:
-            parts = [part for part in parts if next(part, parts) is not parts]
+        answers = [None] * len(parts)
+        while True:
+            asked = []
+            for part, answer in zip(parts, answers):
+                try:
+                    asked.append(part.send(answer))
+                except StopIteration:
+                    pass
+            if not asked:
+                return
+            answers = [None] * len(parts)
+            if asked[0] is None:
+                continue
+            ref, place, left, right, dims = asked[0]
+            left = jnp.concatenate([ask[2] for ask in asked], 0)
+            if ref is None:
+                whole = mm(left, right, dims)
+                size = whole.shape[0] // len(asked)
+                answers = [whole[n * size : (n + 1) * size] for n in range(len(asked))]
+            else:
+                ref[place] += mm(left, jnp.concatenate([ask[3] for ask in asked], 0), dims)
 
     first = PAIR * step
     together(*[attend(k, first + k) for k in range(PAIR)])
@@ -768,7 +809,6 @@
     consts = [
         jnp.asarray(order_matrix(), BF),
         jnp.asarray(order_matrix().T, BF),
-        jnp.asarray(cell_shifts(), BF),
         jnp.asarray(score_bias(), F32),
         jnp.asarray(shift_masks(), F32),
     ]
@@ -1086,7 +1126,7 @@
 
 def reduce_kernel(
     devices,
-    mine,
+    mine_far,
     theirs,
     small_mine,
     small_theirs,
@@ -1096,6 +1136,7 @@
     small,
     out_other,
     input_other,
+    mine,
     core_in,
     core_small,
     plane_out,
@@ -1110,9 +1151,12 @@
     plane_recv,
     line_send,
     line_recv,
+    local_sem,
 ):
     lines, planes, z, p, head, line_peers, plane_peers = places(devices)
     half = input_half.shape[0]
+    fetch = pltpu.make_async_copy(mine_far, mine, local_sem.at[0])
+    fetch.start()
 
     def at(line, plane, core):
         return (line * planes + plane, core)
@@ -1155,6 +1199,7 @@
             plane_recv.at[lines * planes + p],
             at(z, k, head),
         )
+    fetch.wait()
     for m, a in enumerate(order):
         remote(
             theirs.at[a], core_in.at[a], core_send.at[a], core_recv.at[a], sibling
@@ -1256,9 +1301,10 @@
             jax.ShapeDtypeStruct(input_half.shape, BF),
             jax.ShapeDtypeStruct(input_half.shape, BF),
         ],
-        in_specs=[vmem] * 4 + [anywhere] * 2,
+        in_specs=[anywhere] * 2 + [vmem] * 2 + [anywhere] * 2,
         out_specs=[vmem] * 2 + [anywhere] * 2,
         scratch_shapes=[
+            pltpu.VMEM((lines, planes, rows, 128), F32),
             pltpu.VMEM((lines, planes, rows, 128), BF),
             pltpu.VMEM((SMALL, 128), F32),
             pltpu.VMEM((lines, planes, rows, 128), BF),
@@ -1273,6 +1319,7 @@
             sem((lines * planes + planes,)),
             sem((2 * lines,)),
             sem((2 * lines,)),
+            sem((1,)),
         ],
         compiler_params=pltpu.CompilerParams(
             collective_id=1, has_side_effects=True, vmem_limit_bytes=LIMIT
@@ -1352,12 +1399,12 @@
 
 def run_update(tokens_all, head, output, input_grad, out_other, in_other, grad, small, state):
     half = out_other.shape[0]
-    steps = half // PAIR
+    steps = 2
 
     def all_of(a):
         return pl.BlockSpec(a.shape, lambda i, *_, n=a.ndim: (0,) * n)
 
-    block = (PAIR,) + out_other.shape[1:]
+    block = (half // steps,) + out_other.shape[1:]
     other = pl.BlockSpec(block, lambda i, *_: (i, 0, 0, 0))
     final = pl.BlockSpec(block, lambda i, head: ((1 - head[0]) * steps + i, 0, 0, 0))
     anywhere = pl.BlockSpec(memory_space=pl.ANY)

time: 151 us -> 148 us (0.980)
  Pallas kernels: 150 us -> 147 us
    pallas_call x1, Pallas kernels: 105 us -> 104 us  [run_block(): pl.pallas_call(kernel, out_shape=out_shape, grid_spec=pltpu.PrefetchScala...]
where the time goes in v6:
time: 148 us
  Pallas kernels  147 us (99%)
    pallas_call x1, Pallas kernels, run_block(): pl.pallas_call(kernel, out_shape=out_shape, grid_spec=pltpu.PrefetchScala...  104 us
    pallas_call x1, Pallas kernels, run_gather(): pl.pallas_call(kernel, out_shape=[jax.ShapeDtypeStruct((2 * devices, rows...  20.3 us
    pallas_call x1, Pallas kernels, run_reduce(): pl.pallas_call(kernel, out_shape=[jax.ShapeDtypeStruct((rows, 128), F32),...  17.9 us
    pallas_call x1, Pallas kernels, run_update(): pl.pallas_call(kernel, out_shape=[jax.ShapeDtypeStruct(a.shape, a.dtype)...  5.36 us

profile of v6, /device:TPU:0, one launch (start us, length us, event | category | flops | bytes accessed | tf_op | source)
XLA Modules:
  0.0 147.8 jit_solution(6553733816209194637)
XLA Ops:
  0.7 20.3 %gather.1 = (bf16[32,176,128]{2,1,0:T(8,128)(2,1)}, f32[2,16,640]{2,1,0:T(8,128)}) custom-call(s32[16]{0:T(128)} %refs_0_.3, s32[16]{0:T(128)} %refs_1_.3, f32[3,8,64]{2,1,0:T(8,128)} %refs_7_.3, f32[8,64]{1,0:T(8,128)} %bitcast.35, f32[8,512]{1,0:T(8,128)} %refs_13_.1, f32[8,512]{1,0:T(8,128)} %bitcast.29, f32[64,160]{1,0:T(8,128)} %bitcast.25, ...), custom_call_target="tpu_custom_call" | custom-call | tf_op jit(solution)/shard_map/gather/pallas_call | solution.py:1103
  21.0 103.5 %block.1 = (bf16[16,32,32,128]{3,2,1,0:T(8,128)(2,1)}, f32[16,32,32,128]{3,2,1,0:T(8,128)}, bf16[8,32,32,128]{3,2,1,0:T(8,128)(2,1)}, f32[4,4,160,128]{3,2,1,0:T...) custom-call(s32[16]{0:T(128)} %refs_0_.3, s32[16]{0:T(128)} %refs_1_.3, ...), custom_call_target="tpu_custom_call" | custom-call | tf_op jit(solution)/shard_map/block/pallas_call | solution.py:837
  124.5 17.9 %reduce.1 = (f32[160,128]{1,0:T(8,128)}, f32[64,128]{1,0:T(8,128)}, bf16[8,32,32,128]{3,2,1,0:T(8,128)(2,1)}, bf16[8,32,32,128]{3,2,1,0:T(8,128)(2,1)}) custom-call(f32[4,4,160,128]{3,2,1,0:T(8,128)} %get-tuple-element.67.refs_0_, bf16[4,4,160,128]{3,2,1,0:T(8,128)(2,1)} %get-tuple-element.68.refs_1_, f32[64,128]{1,0:T(8,128)} %get-tuple-element.69.refs_2_, ...), custom_call_target="tpu_custom_call" | custom-call | tf_op jit(solution)/shard_map/reduce/pallas_call | solution.py:1296
  142.4 5.4 %update.1 = (bf16[16,32,32,128]{3,2,1,0:T(8,128)(2,1)}, f32[16,32,32,128]{3,2,1,0:T(8,128)}, f32[3,8,64]{2,1,0:T(8,128)}, f32[3,8,64]{2,1,0:T(8,128)}, f32[3,8,6...) custom-call(s32[1]{0:T(128)} %bitcast.refs_2_.refs_0_, ...), custom_call_target="tpu_custom_call", output_to_operand_aliasing={{0}: (5, {}), {1}: (6, {})} | custom-call | tf_op jit(solution)/shard_map/update/pallas_call | solution.py:1415

commit v7 on v6

--- a/solution.py
+++ b/solution.py
@@ -116,6 +116,7 @@
     theirs,
     small_mine,
     small_theirs,
+    factor,
     entry,
     mixing_t,
     expand,
@@ -183,6 +184,7 @@
             pair = packed[n, last_rows : last_rows + 16, :].astype(F32)
             counts = counts + (pair[:1] + 256.0 * pair[1:2])
         factor_s[...] = (devices * 2 * steps * 1024 / 64) / counts
+        factor[...] = jnp.broadcast_to(factor_s[...], factor.shape)
         for d in range(devices):
             one, two = [packed[2 * d + h].astype(F32) for h in range(2)]
             mask = left(top)
@@ -439,11 +441,12 @@
             enhanced_s[slot, q] = both_heads(enhanced[:, q * 128 : q * 128 + 128])
             scores.append(mm(keys_s[slot, q], of_quadrant(queries, q, 16), NT))
         yield
+        offset = fine.astype(F32) * bias[...]
         for q in range(4):
-            biased = scores[q] * scaling + fine.astype(F32) * bias[...]
+            biased = scores[q] * (scaling * math.log2(math.e)) + offset
             for lo, hi in segments:
                 part = biased[lo:hi]
-                part = jnp.exp(part - jnp.max(part, 0, keepdims=True))
+                part = jnp.exp2(part - jnp.max(part, 0, keepdims=True))
                 probs[slot, q, lo:hi, :] = part * (1.0 / jnp.sum(part, 0, keepdims=True))
         yield
         mixed_parts = [
@@ -829,6 +832,7 @@
         jax.ShapeDtypeStruct((lines, devices // lines, rows, 128), BF),
         jax.ShapeDtypeStruct((SMALL, 128), F32),
         jax.ShapeDtypeStruct((SMALL, 128), F32),
+        jax.ShapeDtypeStruct((8, 128), F32),
     ]
 
     def kernel(*refs):
@@ -1190,7 +1194,7 @@
     remote(
         small_theirs, core_small, core_send.at[lines], core_recv.at[lines], sibling
     ).wait_recv()
-    plane_small[pl.ds(p, 1)] = (small_mine[...] + core_small[...])[None]
+    plane_small[pl.ds(p, 1)] = (small_mine[...] + core_small[...]).astype(BF)[None]
     for n, k in enumerate(plane_peers):
         go(
             plane_small.at[p],
@@ -1225,10 +1229,10 @@
             plane_recv.at[lines * planes + k],
             sibling,
         ).wait_recv()
-    part = plane_small[0]
+    part = plane_small[0].astype(F32)
     for k in range(1, planes):
-        part = part + plane_small[k]
-    line_small[pl.ds(z, 1)] = part[None]
+        part = part + plane_small[k].astype(F32)
+    line_small[pl.ds(z, 1)] = part.astype(BF)[None]
     for n, k in enumerate(line_peers):
         go(
             line_small.at[z],
@@ -1270,9 +1274,9 @@
             line_recv.at[lines + k],
             sibling,
         ).wait_recv()
-    part = line_small[0]
+    part = line_small[0].astype(F32)
     for k in range(1, lines):
-        part = part + line_small[k]
+        part = part + line_small[k].astype(F32)
     small[...] = part
     remote(
         own_out, out_other, core_send.at[lines + 1], core_recv.at[lines + 1], sibling
@@ -1309,10 +1313,10 @@
             pltpu.VMEM((SMALL, 128), F32),
             pltpu.VMEM((lines, planes, rows, 128), BF),
             pltpu.VMEM((lines, planes, rows, 128), BF),
-            pltpu.VMEM((planes, SMALL, 128), F32),
+            pltpu.VMEM((planes, SMALL, 128), BF),
             pltpu.VMEM((lines, rows, 128), BF),
             pltpu.VMEM((lines, rows, 128), BF),
-            pltpu.VMEM((lines, SMALL, 128), F32),
+            pltpu.VMEM((lines, SMALL, 128), BF),
             sem((lines + 3,)),
             sem((lines + 3,)),
             sem((lines * (planes - 1) + planes,)),
@@ -1339,12 +1343,12 @@
 
 
 def update_kernel(head, *refs, tokens_all):
-    out_other, in_other, grad, small = refs[:4]
-    state = refs[6:30]
-    output, input_grad = refs[30:32]
-    results = refs[32:]
+    out_other, in_other, grad, small, scales = refs[:5]
+    state = refs[7:31]
+    output, input_grad = refs[31:33]
+    results = refs[33:]
     step = pl.program_id(0)
-    factor = tokens_all / small[17:18, :]
+    factor = scales[:1, :]
     output[...] = out_other[...]
     input_grad[...] = in_other[...].astype(F32) * factor
 
@@ -1397,7 +1401,7 @@
             )
 
 
-def run_update(tokens_all, head, output, input_grad, out_other, in_other, grad, small, state):
+def run_update(tokens_all, head, output, input_grad, out_other, in_other, grad, small, factor, state):
     half = out_other.shape[0]
     steps = 2
 
@@ -1418,16 +1422,16 @@
         grid_spec=pltpu.PrefetchScalarGridSpec(
             num_scalar_prefetch=1,
             grid=(steps,),
-            in_specs=[other, other, all_of(grad), all_of(small), anywhere, anywhere]
+            in_specs=[other, other, all_of(grad), all_of(small), all_of(factor), anywhere, anywhere]
             + [all_of(a) for a in state],
             out_specs=[final, final] + [all_of(a) for a in state],
         ),
-        input_output_aliases={5: 0, 6: 1},
+        input_output_aliases={6: 0, 7: 1},
         compiler_params=pltpu.CompilerParams(
             dimension_semantics=("arbitrary",), vmem_limit_bytes=LIMIT
         ),
         name="update",
-    )(head, out_other, in_other, grad, small, output, input_grad, *state)
+    )(head, out_other, in_other, grad, small, factor, output, input_grad, *state)
 
 
 def per_device(
@@ -1487,7 +1491,7 @@
         values[0],
         hidden_filter,
     )
-    output, input_grad, input_low, mine, theirs, small_mine, small_theirs = run_block(
+    output, input_grad, input_low, mine, theirs, small_mine, small_theirs, factor = run_block(
         resolution, live_images, head, tokens, cotangent, blocks, filters, norm_params
     )
     grad, small, out_other, input_other = run_reduce(
@@ -1514,7 +1518,16 @@
     tokens_all = devices * tokens.shape[0] * tokens.shape[1] * tokens.shape[2]
     results = list(
         run_update(
-            tokens_all, head, output, input_grad, out_other, input_other, grad, small, state
+            tokens_all,
+            head,
+            output,
+            input_grad,
+            out_other,
+            input_other,
+            grad,
+            small,
+            factor,
+            state,
         )
     )
     for n, turn in zip((1, 3, 4, 6), turns):

time: 148 us -> 147 us (level)
  no operation moved by 1% of the time
where the time goes in v7:
time: 147 us; the launch traced here: 146 us
  Pallas kernels  146 us (99%)
    pallas_call x1, Pallas kernels, run_block(): pl.pallas_call(kernel, out_shape=out_shape, grid_spec=pltpu.PrefetchScala...  103 us
    pallas_call x1, Pallas kernels, run_gather(): pl.pallas_call(kernel, out_shape=[jax.ShapeDtypeStruct((2 * devices, rows...  20.3 us
    pallas_call x1, Pallas kernels, run_reduce(): pl.pallas_call(kernel, out_shape=[jax.ShapeDtypeStruct((rows, 128), F32),...  16.6 us
    pallas_call x1, Pallas kernels, run_update(): pl.pallas_call(kernel, out_shape=[jax.ShapeDtypeStruct(a.shape, a.dtype)...  5.38 us

profile of v7, /device:TPU:0, one launch (start us, length us, event | category | flops | bytes accessed | tf_op | source)
XLA Modules:
  0.0 146.3 jit_solution(13899279380320954469)
XLA Ops:
  0.7 20.3 %gather.1 = (bf16[32,176,128]{2,1,0:T(8,128)(2,1)}, f32[2,16,640]{2,1,0:T(8,128)}) custom-call(s32[16]{0:T(128)} %refs_0_.3, s32[16]{0:T(128)} %refs_1_.3, f32[3,8,64]{2,1,0:T(8,128)} %refs_8_.4, f32[8,64]{1,0:T(8,128)} %bitcast.35, f32[8,512]{1,0:T(8,128)} %refs_14_.1, f32[8,512]{1,0:T(8,128)} %bitcast.29, f32[64,160]{1,0:T(8,128)} %bitcast.25, ...), custom_call_target="tpu_custom_call" | custom-call | tf_op jit(solution)/shard_map/gather/pallas_call | solution.py:1107
  21.0 103.2 %block.1 = (bf16[16,32,32,128]{3,2,1,0:T(8,128)(2,1)}, f32[16,32,32,128]{3,2,1,0:T(8,128)}, bf16[8,32,32,128]{3,2,1,0:T(8,128)(2,1)}, f32[4,4,160,128]{3,2,1,0:T...) custom-call(s32[16]{0:T(128)} %refs_0_.3, s32[16]{0:T(128)} %refs_1_.3, ...), custom_call_target="tpu_custom_call" | custom-call | tf_op jit(solution)/shard_map/block/pallas_call | solution.py:841
  124.2 16.6 %reduce.1 = (f32[160,128]{1,0:T(8,128)}, f32[64,128]{1,0:T(8,128)}, bf16[8,32,32,128]{3,2,1,0:T(8,128)(2,1)}, bf16[8,32,32,128]{3,2,1,0:T(8,128)(2,1)}) custom-call(f32[4,4,160,128]{3,2,1,0:T(8,128)} %get-tuple-element.68.refs_0_, bf16[4,4,160,128]{3,2,1,0:T(8,128)(2,1)} %get-tuple-element.69.refs_1_, f32[64,128]{1,0:T(8,128)} %get-tuple-element.70.refs_2_, ...), custom_call_target="tpu_custom_call" | custom-call | tf_op jit(solution)/shard_map/reduce/pallas_call | solution.py:1300
  140.9 5.4 %update.1 = (bf16[16,32,32,128]{3,2,1,0:T(8,128)(2,1)}, f32[16,32,32,128]{3,2,1,0:T(8,128)}, f32[3,8,64]{2,1,0:T(8,128)}, f32[3,8,64]{2,1,0:T(8,128)}, f32[3,8,6...) custom-call(s32[1]{0:T(128)} %bitcast.refs_2_.refs_0_, ...), custom_call_target="tpu_custom_call", output_to_operand_aliasing={{0}: (6, {}), {1}: (7, {})} | custom-call | tf_op jit(solution)/shard_map/update/pallas_call | solution.py:1419
